TPU v7x, 32 devices: a whole 2x2x4 slice. The times are simulated.
32 devices in a mesh: groups: 2 (over x), shard: 16 (over z, y, core).
Axes of the slice: x: 2, y: 2, z: 4, core: 2. Of those that a mesh axis runs over, the one named last changes fastest.
Arguments:
- embeddings: bfloat16 [8192, 1024], P(('groups', 'shard')), parts along dimension 0
- cluster_ids: int32 [8192], P(('groups', 'shard')), parts along dimension 0, may hold values from 0 to 127, as said below
- priority: int32 [8192], P(('groups', 'shard')), parts along dimension 0, may hold values from 0 to 4095, each once
Outputs:
- best_match: float32 [8192], P(('groups', 'shard')), parts along dimension 0
There are 2 independent parts, one for each index of `groups`. A program takes and returns all parts, laid end to end along the dimension named above; each array names one. Nothing has to cross between parts.
Inputs may be any that keep to these rules, and one draw needn't show every extreme that they name: `cluster_ids`: cluster c belongs to owner device c // 8 of the shard axis. The rows of one device hold at most 32 rows of the clusters of any one owner; in every draw one owner receives exactly 32 rows from every device. `priority`: A permutation of the rows of one group.
All inputs are finite; a program needn't handle non-finite values.
Results may differ from a plain program's by a relative error of at most 0.00046.
Values may be sent and summed in bfloat16 or wider, within the bound.
No kernel may reach another device: no remote copies, remote signals or barrier semaphores. Data moves between devices by JAX's collectives and lax.ppermute only.
A program may use at most 64 MiB of HBM per device.

v0:
```python
import math

import jax
import jax.numpy as jnp
from jax import lax
from jax.sharding import PartitionSpec as P

CL_DEV = 8


def scores(left, right):
    return lax.dot_general(
        left, right, (((1,), (1,)), ((), ())), preferred_element_type=jnp.float32
    )


def slot_maxima(units, clusters, ranks):
    total = units.shape[0]
    block = math.gcd(512, total)

    def one_block(start):
        sims = scores(units, units)
        mask = (
            (clusters[:, None] == clusters[None, :])
            & (ranks[None, :] < ranks[:, None])
            & (clusters[None, :] >= 0)
        )
        return jnp.max(jnp.where(mask, sims, jnp.float32(-1.0)), axis=1)

    starts = jnp.arange(0, total, block, dtype=jnp.int32)
    return lax.map(one_block, starts).reshape(-1)


def shards(embeddings, cluster_ids, priority):
    rows, width = embeddings.shape
    owners = lax.axis_size("shard")
    capacity = max(2, 2 * rows // owners)
    slots = owners * capacity
    wide = embeddings.astype(jnp.float32)
    squares = jnp.sum(wide * wide, axis=1, keepdims=True)
    unit = (wide * lax.rsqrt(squares + 1e-06)).astype(jnp.bfloat16)
    owner = cluster_ids // CL_DEV
    onehot = (owner[:, None] == jnp.arange(owners, dtype=jnp.int32)[None, :]).astype(jnp.int32)
    position = jnp.sum(jnp.cumsum(onehot, axis=0) * onehot, axis=1) - 1
    target = owner * capacity + position
    outgoing = jnp.zeros((slots, width), jnp.bfloat16).at[target].set(unit)
    outgoing_cl = jnp.full((slots,), -1, jnp.int32).at[target].set(cluster_ids)
    outgoing_rk = jnp.zeros((slots,), jnp.int32).at[target].set(priority)
    arrived, arrived_cl, arrived_rk = (
        lax.all_to_all(
            outgoing.reshape(owners, capacity, width),
            "shard",
            split_axis=0,
            concat_axis=0,
            tiled=True,
        ),
        lax.all_to_all(
            outgoing_cl.reshape(owners, capacity), "shard", split_axis=0, concat_axis=0, tiled=True
        ),
        lax.all_to_all(
            outgoing_rk.reshape(owners, capacity), "shard", split_axis=0, concat_axis=0, tiled=True
        ),
    )
    arrived = arrived.reshape(slots, width)
    arrived_cl = arrived_cl.reshape(slots)
    arrived_rk = arrived_rk.reshape(slots)
    maxima = slot_maxima(arrived, arrived_cl, arrived_rk)
    returned = lax.all_to_all(
        maxima.reshape(owners, capacity), "shard", split_axis=0, concat_axis=0, tiled=True
    )
    return returned.reshape(slots)[target]


def solution(mesh):
    placed = (P(("groups", "shard"), None), P(("groups", "shard")), P(("groups", "shard")))
    return jax.shard_map(
        shards, mesh=mesh, in_specs=placed, out_specs=P(("groups", "shard")), check_vma=False
    )
```

profile of v0, /device:TPU:0, one launch (start us, length us, event | category | flops | bytes accessed | tf_op | source)
XLA Modules:
  0.0 72.7 jit_solution(9484472652311144460)
XLA Ops:
  0.0 0.0 copy-start.1
  0.0 0.0 copy-start
  0.0 0.8 %and_select_fusion = s32[256]{0:T(256)S(1)} fusion(s32[256]{0:T(256)} %param.4), kind=kLoop, calls=%fused_computation.23 | loop fusion | flops 3840 | bytes 2048 | tf_op jit(solution)/shard_map/jit(floor_divide)/jit(_where)/select_n | solution.py:42
  0.8 0.0 copy-done.1
  0.8 0.6 reduce-window.6
  1.4 0.2 slice_reduce_fusion
  1.6 0.1 fusion.8
  1.7 1.6 %scatter_custom_fusion.1 = s32[512]{0:T(512)S(1)} fusion(s32[256]{0:T(256)S(1)} %compare_select_fusion, s32[256]{0:T(256)} %param.5, s32[]{:T(128)} %constant.22.clone.1), kind=kCustom, calls=%fused_computation.29 | custom fusion | bytes 2560 | tf_op jit(solution)/shard_map/scatter | solution.py:48
  3.3 0.7 all_to_all.23
  4.0 7.4 %all-to-all-start.1 = ((s32[16,1,32]{2,1,0:T(1,128)}), s32[16,1,32]{2,1,0:T(1,128)S(1)}, u32[]{:S(2)}, u32[]{:S(2)}) async-start(s32[16,1,32]{2,1,0:T(1,128)} %all_to_all.23), calls=%async_computation.1 | async-start | bytes 16384 | tf_op jit(solution)/shard_map/all_to_all | solution.py:60
  11.4 1.2 %fusion.1 = f32[256]{0:T(256)S(1)} fusion(bf16[256,1024]{1,0:T(8,128)(2,1)} %param.3), kind=kLoop, calls=%fused_computation.8 | loop fusion | flops 786176 | bytes 525312 | tf_op jit(solution)/shard_map/reduce_sum | solution.py:40
  12.6 1.4 %scatter_custom_fusion = s32[512]{0:T(512)S(1)} fusion(s32[256]{0:T(256)S(1)} %compare_select_fusion, s32[256]{0:T(256)S(1)} %copy-done.1, s32[]{:T(128)} %constant.20.clone.1), kind=kCustom, calls=%fused_computation.31 | custom fusion | bytes 2052 | tf_op jit(solution)/shard_map/scatter | solution.py:47
  14.0 0.7 all_to_all.21
  14.7 3.1 %all-to-all-done.1 = s32[16,1,32]{2,1,0:T(1,128)S(1)} async-done(((s32[16,1,32]{2,1,0:T(1,128)}), s32[16,1,32]{2,1,0:T(1,128)S(1)}, u32[]{:S(2)}, u32[]{:S(2)}) %all-to-all-start.1) | async-done | bytes 2080 | tf_op jit(solution)/shard_map/all_to_all | solution.py:60
  17.8 3.5 %all-to-all-start = ((s32[16,1,32]{2,1,0:T(1,128)}), s32[16,1,32]{2,1,0:T(1,128)S(1)}, u32[]{:S(2)}, u32[]{:S(2)}) async-start(s32[16,1,32]{2,1,0:T(1,128)} %all_to_all.21), calls=%async_computation | async-start | bytes 16384 | tf_op jit(solution)/shard_map/all_to_all | solution.py:57
  21.3 0.0 copy-done
  21.3 2.7 %scatter_custom_fusion.2 = bf16[512,1024]{1,0:T(8,128)(2,1)} fusion(s32[256]{0:T(256)S(1)} %compare_select_fusion, bf16[256,1024]{1,0:T(8,128)(2,1)S(1)} %copy-done, f32[256]{0:T(256)S(1)} %add_rsqrt_fusion, bf16[]{:T(256)} %constant.45.clone.1), kind=kCustom, calls=%fused_computation.10 | custom fusion | flops 786432 | bytes 1573890 | tf_op jit(solution)/shard_map/scatter | solution.py:46
  24.0 3.6 %all-to-all-done = s32[16,1,32]{2,1,0:T(1,128)S(1)} async-done(((s32[16,1,32]{2,1,0:T(1,128)}), s32[16,1,32]{2,1,0:T(1,128)S(1)}, u32[]{:S(2)}, u32[]{:S(2)}) %all-to-all-start) | async-done | bytes 2080 | tf_op jit(solution)/shard_map/all_to_all | solution.py:57
  27.6 3.7 %all-to-all-start.2 = ((bf16[16,32,1024]{2,1,0:T(8,128)(2,1)}), bf16[16,32,1024]{2,1,0:T(8,128)(2,1)S(1)}, u32[]{:S(2)}, u32[]{:S(2)}) async-start(bf16[16,32,1024]{2,1,0:T(8,128)(2,1)} %bitcast.2), calls=%async_computation.2 | async-start | bytes 2097152 | tf_op jit(solution)/shard_map/all_to_all | solution.py:50
  31.3 0.5 broadcast.67
  31.8 0.7 reduce.11
  32.5 0.1 lt.30
  32.6 0.7 reduce.12
  33.2 0.1 eq.52
  33.3 20.9 %all-to-all-done.2 = bf16[16,32,1024]{2,1,0:T(8,128)(2,1)S(1)} async-done(((bf16[16,32,1024]{2,1,0:T(8,128)(2,1)}), bf16[16,32,1024]{2,1,0:T(8,128)(2,1)S(1)}, u32[]{:S(2)}, u32[]{:S(2)}) %all-to-all-start.2) | async-done | bytes 1048608 | tf_op jit(solution)/shard_map/all_to_all | solution.py:50
  54.2 0.8 %fusion = f32[512]{0:T(512)S(1)} fusion(bf16[512,1024]{1,0:T(8,128)(2,1)S(1)} %bitcast.21, s32[512]{0:T(512)S(1)} %lt.30, s32[512]{0:T(512)S(1)} %eq.52, pred[512]{0:T(512)(128)(4,1)S(1)} %broadcast_compare_fusion), kind=kOutput, calls=%fused_computation.7 | convolution fusion | flops 538443264 | bytes 1055232 | tf_op jit(solution)/shard_map/while/body/eval_jaxpr/dot_general | solution.py:12
  55.0 0.7 all_to_all.26
  55.7 6.8 %all-to-all-start.3 = ((f32[16,1,32]{2,1,0:T(1,128)}), f32[16,1,32]{2,1,0:T(1,128)S(1)}, u32[]{:S(2)}, u32[]{:S(2)}) async-start(f32[16,1,32]{2,1,0:T(1,128)} %all_to_all.26), calls=%async_computation.3 | async-start | bytes 16384 | tf_op jit(solution)/shard_map/all_to_all | solution.py:68
  62.5 6.4 %all-to-all-done.3 = f32[16,1,32]{2,1,0:T(1,128)S(1)} async-done(((f32[16,1,32]{2,1,0:T(1,128)}), f32[16,1,32]{2,1,0:T(1,128)S(1)}, u32[]{:S(2)}, u32[]{:S(2)}) %all-to-all-start.3) | async-done | bytes 2080 | tf_op jit(solution)/shard_map/all_to_all | solution.py:68
  68.9 0.5 broadcast.69
  69.4 0.7 reduce.13
  70.1 0.1 reshape.63
  70.2 2.5 %gather_fusion = f32[256]{0:T(256)} fusion(f32[512]{0:T(512)S(1)} %reshape.63, s32[1024]{0:T(1024)S(1)} %pad_clamp_fusion), kind=kCustom, calls=%fused_computation | custom fusion | bytes 3072 | tf_op jit(solution)/shard_map/gather | solution.py:71
  (8 shorter events, 0.1 us)
Async XLA Ops:
  0.0 0.8 %copy-start.1 = (s32[256]{0:T(256)S(1)}, s32[256]{0:T(256)}, u32[]{:S(2)}) copy-start(s32[256]{0:T(256)} %param.4) | copy-start | bytes 3076
  0.0 21.3 %copy-start = (bf16[256,1024]{1,0:T(8,128)(2,1)S(1)}, bf16[256,1024]{1,0:T(8,128)(2,1)}, u32[]{:S(2)}) copy-start(bf16[256,1024]{1,0:T(8,128)(2,1)} %param.3) | copy-start | bytes 1572868
  4.0 13.8 %all-to-all-start.1 = ((s32[16,1,32]{2,1,0:T(1,128)}), s32[16,1,32]{2,1,0:T(1,128)S(1)}, u32[]{:S(2)}, u32[]{:S(2)}) async-start(s32[16,1,32]{2,1,0:T(1,128)} %all_to_all.23), calls=%async_computation.1 | async-start | bytes 16384 | tf_op jit(solution)/shard_map/all_to_all | solution.py:60
  17.8 9.9 %all-to-all-start = ((s32[16,1,32]{2,1,0:T(1,128)}), s32[16,1,32]{2,1,0:T(1,128)S(1)}, u32[]{:S(2)}, u32[]{:S(2)}) async-start(s32[16,1,32]{2,1,0:T(1,128)} %all_to_all.21), calls=%async_computation | async-start | bytes 16384 | tf_op jit(solution)/shard_map/all_to_all | solution.py:57
  27.6 26.6 %all-to-all-start.2 = ((bf16[16,32,1024]{2,1,0:T(8,128)(2,1)}), bf16[16,32,1024]{2,1,0:T(8,128)(2,1)S(1)}, u32[]{:S(2)}, u32[]{:S(2)}) async-start(bf16[16,32,1024]{2,1,0:T(8,128)(2,1)} %bitcast.2), calls=%async_computation.2 | async-start | bytes 2097152 | tf_op jit(solution)/shard_map/all_to_all | solution.py:50
  55.7 13.2 %all-to-all-start.3 = ((f32[16,1,32]{2,1,0:T(1,128)}), f32[16,1,32]{2,1,0:T(1,128)S(1)}, u32[]{:S(2)}, u32[]{:S(2)}) async-start(f32[16,1,32]{2,1,0:T(1,128)} %all_to_all.26), calls=%async_computation.3 | async-start | bytes 16384 | tf_op jit(solution)/shard_map/all_to_all | solution.py:68
where the time goes:
time: 73.1 us; the launch traced here: 72.7 us
  waiting for transfers between devices  34 us (47%)
  starting transfers between devices  21.3 us (29%)
  local copies, waits for them, and re-layouts  8.95 us (12%)
  other arithmetic  7.49 us (10%)
  matrix products  0.81 us (1%)
    all_to_all x1, waiting for transfers between devices, shards(): lax.all_to_all(outgoing.reshape(owners, capacity, width), 'shard', split_...  20.9 us
    all_to_all x1, starting transfers between devices, shards(): lax.all_to_all(outgoing_rk.reshape(owners, capacity), 'shard', split_axis...  7.39 us
    all_to_all x1, starting transfers between devices, shards(): lax.all_to_all(maxima.reshape(owners, capacity), 'shard', split_axis=0, c...  6.82 us
    all_to_all x1, waiting for transfers between devices, shards(): lax.all_to_all(maxima.reshape(owners, capacity), 'shard', split_axis=0, c...  6.39 us
    all_to_all x1, starting transfers between devices, shards(): lax.all_to_all(outgoing.reshape(owners, capacity, width), 'shard', split_...  3.65 us
    all_to_all x1, waiting for transfers between devices, shards(): lax.all_to_all(outgoing_cl.reshape(owners, capacity), 'shard', split_axis...  3.62 us
    all_to_all x1, starting transfers between devices, shards(): lax.all_to_all(outgoing_cl.reshape(owners, capacity), 'shard', split_axis...  3.49 us
    all_to_all x1, waiting for transfers between devices, shards(): lax.all_to_all(outgoing_rk.reshape(owners, capacity), 'shard', split_axis...  3.1 us
  transfers between devices with their start and end apart: 4, of which 4 were waited for; matrix products, arithmetic and copies ran while one was open for 10% of the time, Pallas kernels for 0%

commit v1 on v0

v1 whole, which is shorter than its diff:
```python
import jax
import jax.numpy as jnp
from jax import lax
from jax.experimental import pallas as pl
from jax.experimental.pallas import tpu as pltpu
from jax.sharding import PartitionSpec as P

CL_DEV = 8
LANES = 128
RADIX = 256
SPAN = 65536


def iota(shape, dim):
    return lax.broadcasted_iota(jnp.int32, shape, dim)


def matmul_nt(left, right):
    return lax.dot_general(
        left, right, (((1,), (1,)), ((), ())), preferred_element_type=jnp.float32
    )


def matmul(left, right):
    return jnp.dot(left, right, preferred_element_type=jnp.float32)


def onehots(mask):
    return jnp.where(mask, 1.0, 0.0).astype(jnp.bfloat16)


def pack_kernel(owners, capacity, emb_ref, cl_ref, rk_ref, out_ref, pos_ref):
    rows, width = emb_ref.shape
    slots = owners * capacity
    cl = cl_ref[...]
    rk = rk_ref[...]
    owner = cl // CL_DEV
    mine = iota((owners, rows), 0) == owner
    earlier = onehots(iota((rows, rows), 0) < iota((rows, rows), 1))
    before = matmul(onehots(mine), earlier)
    pos = jnp.sum(jnp.where(mine, before, 0.0), axis=0, keepdims=True).astype(jnp.int32)
    pos_ref[...] = pos
    place = onehots(iota((slots, rows), 0) == owner * capacity + pos)
    line = iota((LANES, rows), 0)
    meta = jnp.where(
        line == 0,
        cl - owner * CL_DEV + 1,
        jnp.where(line == 1, rk // RADIX, jnp.where(line == 2, rk % RADIX, 0)),
    )
    meta = meta.astype(jnp.float32).astype(jnp.bfloat16)
    out_ref[:, width:] = matmul_nt(place, meta).astype(jnp.bfloat16)
    wide = emb_ref[...].astype(jnp.float32)
    squares = jnp.sum(wide * wide, axis=1, keepdims=True)
    unit = (wide * lax.rsqrt(squares + 1e-06)).astype(jnp.bfloat16)
    out_ref[:, :width] = matmul(place, unit).astype(jnp.bfloat16)


def match_kernel(owners, capacity, in_ref, out_ref):
    slots, full = in_ref.shape
    width = full - LANES
    meta = in_ref[:, width:]
    pick = onehots(iota((8, LANES), 0) == iota((8, LANES), 1))
    across = matmul_nt(pick, meta)
    low = across[0:1] * SPAN
    code = low + across[1:2] * RADIX + across[2:3]
    down = meta.astype(jnp.float32)
    code_down = down[:, 0:1] * SPAN + down[:, 1:2] * RADIX + down[:, 2:3]
    units = in_ref[:, :width]
    best = jnp.full((1, slots), -1.0, jnp.float32)
    step = min(LANES, slots)
    for start in range(0, slots, step):
        sims = matmul_nt(in_ref[start:start + step, :width], units)
        key = code_down[start:start + step]
        seen = jnp.where((key >= low) & (key < code), sims, -1.0)
        best = jnp.maximum(best, jnp.max(seen, axis=0, keepdims=True))
    for source in range(owners):
        base = source * capacity // LANES * LANES
        out_ref[source] = best[:, base:base + LANES]


def unpack_kernel(owners, capacity, got_ref, cl_ref, pos_ref, out_ref):
    rows = cl_ref.shape[1]
    me = lax.axis_index("shard")
    got = got_ref[:, 0, :]
    high = got.astype(jnp.bfloat16)
    rest = got - high.astype(jnp.float32)
    middle = rest.astype(jnp.bfloat16)
    last = (rest - middle.astype(jnp.float32)).astype(jnp.bfloat16)
    lane = pos_ref[...] + lax.rem(me * capacity, LANES)
    pick = onehots(iota((LANES, rows), 0) == lane)
    found = matmul(high, pick) + matmul(middle, pick) + matmul(last, pick)
    mine = iota((owners, rows), 0) == cl_ref[...] // CL_DEV
    out_ref[...] = jnp.sum(jnp.where(mine, found, 0.0), axis=0, keepdims=True)


def call(kernel, shapes, *args):
    return pl.pallas_call(
        kernel,
        out_shape=shapes,
        compiler_params=pltpu.CompilerParams(vmem_limit_bytes=32 * 2**20),
    )(*args)


def shards(embeddings, cluster_ids, priority):
    rows, width = embeddings.shape
    owners = lax.axis_size("shard")
    capacity = max(2, 2 * rows // owners)
    slots = owners * capacity
    cl = cluster_ids.reshape(1, rows)
    rk = priority.reshape(1, rows)
    full = width + LANES

    def pack(*refs):
        pack_kernel(owners, capacity, *refs)

    def match(*refs):
        match_kernel(owners, capacity, *refs)

    def unpack(*refs):
        unpack_kernel(owners, capacity, *refs)

    outgoing, pos = call(
        pack,
        (
            jax.ShapeDtypeStruct((slots, full), jnp.bfloat16),
            jax.ShapeDtypeStruct((1, rows), jnp.int32),
        ),
        embeddings, cl, rk,
    )
    arrived = lax.all_to_all(
        outgoing.reshape(owners, capacity, full), "shard", split_axis=0, concat_axis=0, tiled=True
    ).reshape(slots, full)
    maxima = call(match, jax.ShapeDtypeStruct((owners, 1, LANES), jnp.float32), arrived)
    returned = lax.all_to_all(maxima, "shard", split_axis=0, concat_axis=0, tiled=True)
    out = call(unpack, jax.ShapeDtypeStruct((1, rows), jnp.float32), returned, cl, pos)
    return out.reshape(rows)


def solution(mesh):
    placed = (P(("groups", "shard"), None), P(("groups", "shard")), P(("groups", "shard")))
    return jax.shard_map(
        shards, mesh=mesh, in_specs=placed, out_specs=P(("groups", "shard")), check_vma=False
    )
```

time: 73.1 us -> 51.8 us (0.71)
  blocking collectives: 0 us -> 46.2 us
  waiting for transfers between devices: 34 us -> 0 us
  starting transfers between devices: 21.3 us -> 0 us
  other arithmetic: 7.49 us -> 0 us
  local copies, waits for them, and re-layouts: 8.95 us -> 2.4 us
  Pallas kernels: 0 us -> 2.99 us
  matrix products: 0.81 us -> 0 us
    all_to_all x0 -> x2, blocking collectives: none -> 46.2 us  [the longest x1 36.7 us: shards(): lax.all_to_all(outgoing.reshape(owners, capacity, full), 'shard', split_a...]
    all_to_all x4 -> x0, waiting for transfers between devices: 34 us -> none  [the longest x1 20.9 us: shards(): lax.all_to_all(outgoing.reshape(owners, capacity, width), 'shard', split_...]
    all_to_all x4 -> x0, starting transfers between devices: 21.3 us -> none  [the longest x1 7.39 us: shards(): lax.all_to_all(outgoing_rk.reshape(owners, capacity), 'shard', split_axis...]
    all_to_all x5 -> x0, local copies, waits for them, and re-layouts: 3.07 us -> none  [the longest x2 1.2 us: shards(): lax.all_to_all(maxima.reshape(owners, capacity), 'shard', split_axis=0, c...]
    pallas_call x0 -> x3, Pallas kernels: none -> 2.99 us  [call(): pl.pallas_call(kernel, out_shape=shapes, compiler_params=pltpu.CompilerPa...]
    scatter x2 -> x0, local copies, waits for them, and re-layouts: 2.95 us -> none  [the longest x1 1.55 us: shards(): outgoing_rk = jnp.zeros((slots,), jnp.int32).at[target].set(priority)]
    scatter x1 -> x0, other arithmetic: 2.73 us -> none  [shards(): outgoing = jnp.zeros((slots, width), jnp.bfloat16).at[target].set(unit)]
    gather x1 -> x0, local copies, waits for them, and re-layouts: 2.5 us -> none  [shards(): return returned.reshape(slots)[target]]
  transfers between devices with their start and end apart: 4 -> 0, of which waited for: 4 -> 0; matrix products, arithmetic and copies ran while one was open for 10% -> 0% of each run, Pallas kernels for 0% -> 0%
where the time goes in v1:
time: 51.8 us; the launch traced here: 51.6 us
  blocking collectives  46.2 us (89%)
  Pallas kernels  2.99 us (6%)
  local copies, waits for them, and re-layouts  2.4 us (5%)
    all_to_all x1, blocking collectives, shards(): lax.all_to_all(outgoing.reshape(owners, capacity, full), 'shard', split_a...  36.7 us
    all_to_all x1, blocking collectives, shards(): lax.all_to_all(maxima, 'shard', split_axis=0, concat_axis=0, tiled=True)  9.5 us
    pallas_call x3, Pallas kernels, call(): pl.pallas_call(kernel, out_shape=shapes, compiler_params=pltpu.CompilerPa...  2.99 us
    unnamed x8, local copies, waits for them, and re-layouts  2.4 us

profile of v1, /device:TPU:0, one launch (start us, length us, event | category | flops | bytes accessed | tf_op | source)
XLA Modules:
  0.0 51.6 jit_solution(2144908111153139065)
XLA Ops:
  0.0 0.0 copy-start
  0.0 1.0 %copy-done = bf16[256,1024]{1,0:T(8,128)(2,1)S(1)} copy-done((bf16[256,1024]{1,0:T(8,128)(2,1)S(1)}, bf16[256,1024]{1,0:T(8,128)(2,1)}, u32[]{:S(2)}) %copy-start) | copy-done | bytes 524312
  1.0 0.0 copy-start.1
  1.0 0.7 %copy-done.1 = s32[256]{0:T(256)S(1)} copy-done((s32[256]{0:T(256)S(1)}, s32[256]{0:T(256)}, u32[]{:S(2)}) %copy-start.1) | copy-done | bytes 1048
  1.7 0.0 copy-start.3
  1.7 0.7 %copy-done.3 = s32[256]{0:T(256)S(1)} copy-done((s32[256]{0:T(256)S(1)}, s32[256]{0:T(256)}, u32[]{:S(2)}) %copy-start.3) | copy-done | bytes 1048
  2.4 0.7 %shard_map.37 = (bf16[512,1152]{1,0:T(8,128)(2,1)S(1)}, s32[1,256]{1,0:T(1,128)S(1)}) custom-call(bf16[256,1024]{1,0:T(8,128)(2,1)S(1)} %copy-done, s32[1,256]{1,0:T(1,128)S(1)} %bitcast.7, s32[1,256]{1,0:T(1,128)S(1)} %bitcast.9), custom_call_target="tpu_custom_call" | custom-call | tf_op jit(solution)/shard_map/pallas_call | solution.py:97
  3.1 36.7 %all_to_all.10 = bf16[16,32,1152]{2,1,0:T(8,128)(2,1)S(1)} all-to-all(bf16[16,32,1152]{2,1,0:T(8,128)(2,1)S(1)} %bitcast.6), channel_id=1, replica_groups=mesh['groups'=2,'shard'=16] {'shard'}, dimensions={0} | all-to-all | bytes 2359296 | tf_op jit(solution)/shard_map/all_to_all | solution.py:130
  39.8 0.0 copy-start.2
  39.8 1.5 %shard_map.38 = f32[16,1,128]{2,1,0:T(1,128)S(1)} custom-call(bf16[512,1152]{1,0:T(8,128)(2,1)S(1)} %bitcast.5), custom_call_target="tpu_custom_call" | custom-call | tf_op jit(solution)/shard_map/pallas_call | solution.py:97
  41.3 9.5 %all_to_all.11.refs_0_ = f32[16,1,128]{2,1,0:T(1,128)S(1)} all-to-all(f32[16,1,128]{2,1,0:T(1,128)S(1)} %shard_map.38), channel_id=1, replica_groups=mesh['groups'=2,'shard'=16] {'shard'}, dimensions={0} | all-to-all | bytes 16384 | tf_op jit(solution)/shard_map/all_to_all | solution.py:134
  50.8 0.0 copy-done.2
  50.8 0.7 %shard_map.39 = f32[1,256]{1,0:T(1,128)} custom-call(f32[16,1,128]{2,1,0:T(1,128)S(1)} %all_to_all.11.refs_0_, s32[1,256]{1,0:T(1,128)S(1)} %bitcast.8, s32[1,256]{1,0:T(1,128)S(1)} %get-tuple-element.8.refs_2_), custom_call_target="tpu_custom_call" | custom-call | tf_op jit(solution)/shard_map/pallas_call | solution.py:97
Async XLA Ops:
  0.0 1.0 %copy-start = (bf16[256,1024]{1,0:T(8,128)(2,1)S(1)}, bf16[256,1024]{1,0:T(8,128)(2,1)}, u32[]{:S(2)}) copy-start(bf16[256,1024]{1,0:T(8,128)(2,1)} %refs_0_.1) | copy-start | bytes 1572868
  1.0 0.7 %copy-start.1 = (s32[256]{0:T(256)S(1)}, s32[256]{0:T(256)}, u32[]{:S(2)}) copy-start(s32[256]{0:T(256)} %param.4) | copy-start | bytes 3076
  1.7 0.7 %copy-start.3 = (s32[256]{0:T(256)S(1)}, s32[256]{0:T(256)}, u32[]{:S(2)}) copy-start(s32[256]{0:T(256)} %param.5) | copy-start | bytes 3076
  39.8 11.1 %copy-start.2 = (s32[256]{0:T(256)S(1)}, s32[256]{0:T(256)}, u32[]{:S(2)}) copy-start(s32[256]{0:T(256)} %param.4) | copy-start | bytes 3076

commit v2 on v1

v2 whole, which is shorter than its diff:
```python
import jax
import jax.numpy as jnp
from jax import lax
from jax.experimental import pallas as pl
from jax.experimental.pallas import tpu as pltpu
from jax.sharding import PartitionSpec as P

CL_DEV = 8
LANES = 128
RADIX = 256
SPAN = 65536


def iota(shape, dim):
    return lax.broadcasted_iota(jnp.int32, shape, dim)


def matmul_nt(left, right):
    return lax.dot_general(
        left, right, (((1,), (1,)), ((), ())), preferred_element_type=jnp.float32
    )


def matmul(left, right):
    return jnp.dot(left, right, preferred_element_type=jnp.float32)


def onehots(mask):
    return jnp.where(mask, 1.0, 0.0).astype(jnp.bfloat16)


def pack_kernel(owners, capacity, paired, emb_any, cl_any, rk_any, *rest):
    *out_refs, pos_ref, emb_ref, cl_ref, rk_ref, sems = rest
    copies = [
        pltpu.make_async_copy(source, target, sems.at[number])
        for number, (source, target) in enumerate(
            ((cl_any, cl_ref), (rk_any, rk_ref), (emb_any, emb_ref))
        )
    ]
    for copy in copies:
        copy.start()
    rows, width = emb_ref.shape
    slots = owners * capacity
    copies[0].wait()
    cl = cl_ref[...]
    owner = cl // CL_DEV
    block = owner ^ lax.axis_index("shard") if paired else owner
    mine = iota((owners, rows), 0) == block
    earlier = onehots(iota((rows, rows), 0) < iota((rows, rows), 1))
    before = matmul(onehots(mine), earlier)
    pos = jnp.sum(jnp.where(mine, before, 0.0), axis=0, keepdims=True).astype(jnp.int32)
    place = block * capacity + pos
    pos_ref[...] = place
    place = onehots(iota((slots, rows), 0) == place)
    copies[1].wait()
    rk = rk_ref[...]
    line = iota((LANES, rows), 0)
    meta = jnp.where(
        line == 0,
        cl - owner * CL_DEV + 1,
        jnp.where(line == 1, rk // RADIX, jnp.where(line == 2, rk % RADIX, 0)),
    )
    meta = matmul_nt(place, meta.astype(jnp.float32).astype(jnp.bfloat16)).astype(jnp.bfloat16)
    copies[2].wait()
    wide = emb_ref[...].astype(jnp.float32)
    squares = jnp.sum(wide * wide, axis=1, keepdims=True)
    unit = (wide * lax.rsqrt(squares + 1e-06)).astype(jnp.bfloat16)
    unit = matmul(place, unit).astype(jnp.bfloat16)
    size = slots // len(out_refs)
    for number, out_ref in enumerate(out_refs):
        out_ref[:, :width] = unit[number * size:(number + 1) * size]
        out_ref[:, width:] = meta[number * size:(number + 1) * size]


def match_kernel(owners, capacity, inputs, *rest):
    in_refs, out_refs = rest[:inputs], rest[inputs:]
    width = in_refs[0].shape[1] - LANES
    slots = owners * capacity
    arrived = jnp.concatenate([ref[...] for ref in in_refs], axis=0)
    meta = arrived[:, width:]
    units = arrived[:, :width]
    pick = onehots(iota((8, LANES), 0) == iota((8, LANES), 1))
    across = matmul_nt(pick, meta)
    low = across[0:1] * SPAN
    code = low + across[1:2] * RADIX + across[2:3]
    down = meta.astype(jnp.float32)
    code_down = down[:, 0:1] * SPAN + down[:, 1:2] * RADIX + down[:, 2:3]
    best = jnp.full((1, slots), -1.0, jnp.float32)
    step = min(LANES, slots)
    for start in range(0, slots, step):
        sims = matmul_nt(units[start:start + step], units)
        key = code_down[start:start + step]
        seen = jnp.where((key >= low) & (key < code), sims, -1.0)
        best = jnp.maximum(best, jnp.max(seen, axis=0, keepdims=True))
    for source in range(owners):
        base = source * capacity // LANES * LANES
        line = best[:, base:base + LANES]
        if len(out_refs) == 1:
            out_refs[0][source] = line
        else:
            out_refs[source][...] = line


def unpack_kernel(owners, capacity, paired, *refs):
    *got_refs, place_ref, out_ref = refs
    rows = place_ref.shape[1]
    place = place_ref[...]
    block = place // capacity
    if paired:
        got = jnp.concatenate([ref[...] for ref in got_refs], axis=0)
        lane = lax.rem(place, LANES)
    else:
        got = got_refs[0][:, 0, :]
        lane = lax.rem(place, capacity) + lax.rem(lax.axis_index("shard") * capacity, LANES)
    high = got.astype(jnp.bfloat16)
    rest = got - high.astype(jnp.float32)
    middle = rest.astype(jnp.bfloat16)
    last = (rest - middle.astype(jnp.float32)).astype(jnp.bfloat16)
    pick = onehots(iota((LANES, rows), 0) == lane)
    found = matmul(high, pick) + matmul(middle, pick) + matmul(last, pick)
    mine = iota((owners, rows), 0) == block
    out_ref[...] = jnp.sum(jnp.where(mine, found, 0.0), axis=0, keepdims=True)


def call(kernel, shapes, args, **kwargs):
    return pl.pallas_call(
        kernel,
        out_shape=shapes,
        compiler_params=pltpu.CompilerParams(vmem_limit_bytes=32 * 2**20),
        **kwargs,
    )(*args)


def exchange(blocks):
    owners = len(blocks)
    return [blocks[0]] + [
        lax.ppermute(blocks[k], "shard", [(d, d ^ k) for d in range(owners)])
        for k in range(1, owners)
    ]


def shards(embeddings, cluster_ids, priority):
    rows, width = embeddings.shape
    owners = lax.axis_size("shard")
    capacity = max(2, 2 * rows // owners)
    slots = owners * capacity
    full = width + LANES
    paired = owners <= 16 and capacity % 16 == 0 and LANES % capacity == 0
    pieces = owners if paired else 1

    def pack(*refs):
        pack_kernel(owners, capacity, paired, *refs)

    def match(*refs):
        match_kernel(owners, capacity, pieces, *refs)

    def unpack(*refs):
        unpack_kernel(owners, capacity, paired, *refs)

    *outgoing, place = call(
        pack,
        [jax.ShapeDtypeStruct((slots // pieces, full), jnp.bfloat16)] * pieces
        + [jax.ShapeDtypeStruct((1, rows), jnp.int32)],
        (embeddings, cluster_ids.reshape(1, rows), priority.reshape(1, rows)),
        in_specs=[pl.BlockSpec(memory_space=pl.ANY)] * 3,
        scratch_shapes=[
            pltpu.VMEM((rows, width), jnp.bfloat16),
            pltpu.VMEM((1, rows), jnp.int32),
            pltpu.VMEM((1, rows), jnp.int32),
            pltpu.SemaphoreType.DMA((3,)),
        ],
    )
    if paired:
        maxima = call(
            match, [jax.ShapeDtypeStruct((1, LANES), jnp.float32)] * owners, exchange(outgoing)
        )
        returned = exchange(maxima)
    else:
        arrived = lax.all_to_all(
            outgoing[0].reshape(owners, capacity, full), "shard", 0, 0, tiled=True
        ).reshape(slots, full)
        maxima = call(match, [jax.ShapeDtypeStruct((owners, 1, LANES), jnp.float32)], [arrived])
        returned = [lax.all_to_all(maxima[0], "shard", 0, 0, tiled=True)]
    out = call(unpack, jax.ShapeDtypeStruct((1, rows), jnp.float32), [*returned, place])
    return out.reshape(rows)


def solution(mesh):
    placed = (P(("groups", "shard"), None), P(("groups", "shard")), P(("groups", "shard")))
    return jax.shard_map(
        shards, mesh=mesh, in_specs=placed, out_specs=P(("groups", "shard")), check_vma=False
    )
```

time: 51.8 us -> 67.1 us (1.30)
  starting transfers between devices: 0 us -> 52.3 us
  blocking collectives: 46.2 us -> 0 us
  waiting for transfers between devices: 0 us -> 9.49 us
    ppermute x0 -> x30, starting transfers between devices: none -> 52.3 us  [exchange(): lax.ppermute(blocks[k], 'shard', [(d, d ^ k) for d in range(owners)])]
    all_to_all x2 -> x0, blocking collectives: 46.2 us -> none  [the longest x1 36.7 us: shards(): lax.all_to_all(outgoing.reshape(owners, capacity, full), 'shard', split_a...]
    ppermute x0 -> x30, waiting for transfers between devices: none -> 9.49 us  [exchange(): lax.ppermute(blocks[k], 'shard', [(d, d ^ k) for d in range(owners)])]
    unnamed x8 -> x6, local copies, waits for them, and re-layouts: 2.4 us -> 1.73 us
  transfers between devices with their start and end apart: 0 -> 30, of which waited for: 0 -> 6; matrix products, arithmetic and copies ran while one was open for 0% -> 0% of each run, Pallas kernels for 0% -> 0%
where the time goes in v2:
time: 67.1 us; the launch traced here: 66.9 us
  starting transfers between devices  52.3 us (78%)
  waiting for transfers between devices  9.49 us (14%)
  Pallas kernels  3.41 us (5%)
  local copies, waits for them, and re-layouts  1.73 us (3%)
    ppermute x30, starting transfers between devices, exchange(): lax.ppermute(blocks[k], 'shard', [(d, d ^ k) for d in range(owners)])  52.3 us
    ppermute x30, waiting for transfers between devices, exchange(): lax.ppermute(blocks[k], 'shard', [(d, d ^ k) for d in range(owners)])  9.49 us
    pallas_call x3, Pallas kernels, call(): pl.pallas_call(kernel, out_shape=shapes, compiler_params=pltpu.CompilerPa...  3.41 us
    unnamed x6, local copies, waits for them, and re-layouts  1.73 us
  transfers between devices with their start and end apart: 30, of which 6 were waited for; matrix products, arithmetic and copies ran while one was open for 0% of the time, Pallas kernels for 0%

profile of v2, /device:TPU:0, one launch (start us, length us, event | category | flops | bytes accessed | tf_op | source)
XLA Modules:
  0.0 66.9 jit_solution(18204660502526476522)
XLA Ops:
  0.0 0.7 %copy-done.2 = s32[256]{0:T(256)S(1)} copy-done((s32[256]{0:T(256)S(1)}, s32[256]{0:T(256)}, u32[]{:S(2)}) %copy-start.2) | copy-done | bytes 1048
  0.7 0.0 copy-done.1
  0.7 1.0 %copy-done = bf16[256,1024]{1,0:T(8,128)(2,1)S(1)} copy-done((bf16[256,1024]{1,0:T(8,128)(2,1)S(1)}, bf16[256,1024]{1,0:T(8,128)(2,1)}, u32[]{:S(2)}) %copy-start) | copy-done | bytes 524312
  1.7 1.1 %shard_map.37 = (bf16[32,1152]{1,0:T(8,128)(2,1)S(1)}, bf16[32,1152]{1,0:T(8,128)(2,1)S(1)}, bf16[32,1152]{1,0:T(8,128)(2,1)S(1)}, bf16[32,1152]{1,0:T(8,128)(2,...) custom-call(bf16[256,1024]{1,0:T(8,128)(2,1)S(1)} %copy-done, ...), custom_call_target="tpu_custom_call" | custom-call | tf_op jit(solution)/shard_map/pallas_call | solution.py:126
  2.9 0.5 collective-permute-start
  3.4 2.6 %collective-permute-start.1 = (bf16[32,1152]{1,0:T(8,128)(2,1)S(1)}, bf16[32,1152]{1,0:T(8,128)(2,1)S(1)}, u32[]{:S(2)}, u32[]{:S(2)}) collective-permute-start(bf16[32,1152]{1,0:T(8,128)(2,1)S(1)} %get-tuple-element.40), channel_id=1, source_target_pairs={{0,2},{1,3},{2,0},{3,1},{4,6},{5,7},{6,4},{7,5},{8,10},{9,11},{10,... | collective-permute-start | bytes 221192 | tf_op jit(solution)/shard_map/ppermute | solution.py:137
  6.0 0.1 collective-permute-start.2
  6.1 1.8 %collective-permute-start.3 = (bf16[32,1152]{1,0:T(8,128)(2,1)S(1)}, bf16[32,1152]{1,0:T(8,128)(2,1)S(1)}, u32[]{:S(2)}, u32[]{:S(2)}) collective-permute-start(bf16[32,1152]{1,0:T(8,128)(2,1)S(1)} %get-tuple-element.42), channel_id=1, source_target_pairs={{0,4},{1,5},{2,6},{3,7},{4,0},{5,1},{6,2},{7,3},{8,12},{9,13},{10,... | collective-permute-start | bytes 221192 | tf_op jit(solution)/shard_map/ppermute | solution.py:137
  7.9 0.0 collective-permute-start.4
  7.9 0.0 collective-permute-done.refs_1_
  7.9 2.6 %collective-permute-start.5 = (bf16[32,1152]{1,0:T(8,128)(2,1)S(1)}, bf16[32,1152]{1,0:T(8,128)(2,1)S(1)}, u32[]{:S(2)}, u32[]{:S(2)}) collective-permute-start(bf16[32,1152]{1,0:T(8,128)(2,1)S(1)} %get-tuple-element.44), channel_id=1, source_target_pairs={{0,6},{1,7},{2,4},{3,5},{4,2},{5,3},{6,0},{7,1},{8,14},{9,15},{10,... | collective-permute-start | bytes 221192 | tf_op jit(solution)/shard_map/ppermute | solution.py:137
  10.5 0.0 collective-permute-done.1.refs_2_
  10.5 0.4 collective-permute-start.6
  10.9 0.0 collective-permute-done.2.refs_3_
  10.9 2.6 %collective-permute-start.7 = (bf16[32,1152]{1,0:T(8,128)(2,1)S(1)}, bf16[32,1152]{1,0:T(8,128)(2,1)S(1)}, u32[]{:S(2)}, u32[]{:S(2)}) collective-permute-start(bf16[32,1152]{1,0:T(8,128)(2,1)S(1)} %get-tuple-element.46), channel_id=1, source_target_pairs={{0,8},{1,9},{2,10},{3,11},{4,12},{5,13},{6,14},{7,15},{8,0},{9,1},... | collective-permute-start | bytes 221192 | tf_op jit(solution)/shard_map/ppermute | solution.py:137
  13.5 0.0 collective-permute-done.3.refs_4_
  13.5 1.0 %collective-permute-start.8 = (bf16[32,1152]{1,0:T(8,128)(2,1)S(1)}, bf16[32,1152]{1,0:T(8,128)(2,1)S(1)}, u32[]{:S(2)}, u32[]{:S(2)}) collective-permute-start(bf16[32,1152]{1,0:T(8,128)(2,1)S(1)} %get-tuple-element.47), channel_id=1, source_target_pairs={{0,9},{1,8},{2,11},{3,10},{4,13},{5,12},{6,15},{7,14},{8,1},{9,0},... | collective-permute-start | bytes 221192 | tf_op jit(solution)/shard_map/ppermute | solution.py:137
  14.5 0.0 collective-permute-done.4.refs_5_
  14.5 2.4 %collective-permute-start.9 = (bf16[32,1152]{1,0:T(8,128)(2,1)S(1)}, bf16[32,1152]{1,0:T(8,128)(2,1)S(1)}, u32[]{:S(2)}, u32[]{:S(2)}) collective-permute-start(bf16[32,1152]{1,0:T(8,128)(2,1)S(1)} %get-tuple-element.48), channel_id=1, source_target_pairs={{0,10},{1,11},{2,8},{3,9},{4,14},{5,15},{6,12},{7,13},{8,2},{9,3},... | collective-permute-start | bytes 221192 | tf_op jit(solution)/shard_map/ppermute | solution.py:137
  16.8 0.0 collective-permute-done.5.refs_6_
  16.8 0.9 %collective-permute-start.10 = (bf16[32,1152]{1,0:T(8,128)(2,1)S(1)}, bf16[32,1152]{1,0:T(8,128)(2,1)S(1)}, u32[]{:S(2)}, u32[]{:S(2)}) collective-permute-start(bf16[32,1152]{1,0:T(8,128)(2,1)S(1)} %get-tuple-element.49), channel_id=1, source_target_pairs={{0,11},{1,10},{2,9},{3,8},{4,15},{5,14},{6,13},{7,12},{8,3},{9,2},... | collective-permute-start | bytes 221192 | tf_op jit(solution)/shard_map/ppermute | solution.py:137
  17.7 0.1 collective-permute-done.6.refs_7_
  17.9 2.7 %collective-permute-start.11 = (bf16[32,1152]{1,0:T(8,128)(2,1)S(1)}, bf16[32,1152]{1,0:T(8,128)(2,1)S(1)}, u32[]{:S(2)}, u32[]{:S(2)}) collective-permute-start(bf16[32,1152]{1,0:T(8,128)(2,1)S(1)} %get-tuple-element.50), channel_id=1, source_target_pairs={{0,12},{1,13},{2,14},{3,15},{4,8},{5,9},{6,10},{7,11},{8,4},{9,5},... | collective-permute-start | bytes 221192 | tf_op jit(solution)/shard_map/ppermute | solution.py:137
  20.5 0.0 collective-permute-done.7.refs_8_
  20.5 6.3 %collective-permute-start.12 = (bf16[32,1152]{1,0:T(8,128)(2,1)S(1)}, bf16[32,1152]{1,0:T(8,128)(2,1)S(1)}, u32[]{:S(2)}, u32[]{:S(2)}) collective-permute-start(bf16[32,1152]{1,0:T(8,128)(2,1)S(1)} %get-tuple-element.51), channel_id=1, source_target_pairs={{0,13},{1,12},{2,15},{3,14},{4,9},{5,8},{6,11},{7,10},{8,5},{9,4},... | collective-permute-start | bytes 221192 | tf_op jit(solution)/shard_map/ppermute | solution.py:137
  26.8 0.0 collective-permute-done.8.refs_9_
  26.8 3.0 %collective-permute-start.13 = (bf16[32,1152]{1,0:T(8,128)(2,1)S(1)}, bf16[32,1152]{1,0:T(8,128)(2,1)S(1)}, u32[]{:S(2)}, u32[]{:S(2)}) collective-permute-start(bf16[32,1152]{1,0:T(8,128)(2,1)S(1)} %get-tuple-element.52), channel_id=1, source_target_pairs={{0,14},{1,15},{2,12},{3,13},{4,10},{5,11},{6,8},{7,9},{8,6},{9,7},... | collective-permute-start | bytes 221192 | tf_op jit(solution)/shard_map/ppermute | solution.py:137
  29.8 0.4 collective-permute-done.9.refs_10_
  30.2 2.2 %collective-permute-start.14 = (bf16[32,1152]{1,0:T(8,128)(2,1)S(1)}, bf16[32,1152]{1,0:T(8,128)(2,1)S(1)}, u32[]{:S(2)}, u32[]{:S(2)}) collective-permute-start(bf16[32,1152]{1,0:T(8,128)(2,1)S(1)} %get-tuple-element.53), channel_id=1, source_target_pairs={{0,15},{1,14},{2,13},{3,12},{4,11},{5,10},{6,9},{7,8},{8,7},{9,6},... | collective-permute-start | bytes 221192 | tf_op jit(solution)/shard_map/ppermute | solution.py:137
  32.4 0.0 collective-permute-done.10.refs_11_
  32.4 0.0 collective-permute-done.11.refs_12_
  32.4 0.0 collective-permute-done.12.refs_13_
  32.4 1.9 %collective-permute-done.13.refs_14_ = bf16[32,1152]{1,0:T(8,128)(2,1)S(1)} collective-permute-done((bf16[32,1152]{1,0:T(8,128)(2,1)S(1)}, bf16[32,1152]{1,0:T(8,128)(2,1)S(1)}, u32[]{:S(2)}, u32[]{:S(2)}) %collective-permute-start.13) | collective-permute-done | bytes 73760 | tf_op jit(solution)/shard_map/ppermute | solution.py:137
  34.3 3.2 %collective-permute-done.14.refs_15_ = bf16[32,1152]{1,0:T(8,128)(2,1)S(1)} collective-permute-done((bf16[32,1152]{1,0:T(8,128)(2,1)S(1)}, bf16[32,1152]{1,0:T(8,128)(2,1)S(1)}, u32[]{:S(2)}, u32[]{:S(2)}) %collective-permute-start.14) | collective-permute-done | bytes 73760 | tf_op jit(solution)/shard_map/ppermute | solution.py:137
  37.5 1.6 %shard_map.38 = (f32[1,128]{1,0:T(1,128)S(1)}, f32[1,128]{1,0:T(1,128)S(1)}, f32[1,128]{1,0:T(1,128)S(1)}, f32[1,128]{1,0:T(1,128)S(1)}, f32[1,128]{1,0:T(1,128)...) custom-call(bf16[32,1152]{1,0:T(8,128)(2,1)S(1)} %get-tuple-element., ...), custom_call_target="tpu_custom_call" | custom-call | tf_op jit(solution)/shard_map/pallas_call | solution.py:126
  39.1 0.1 collective-permute-start.15
  39.2 0.8 %collective-permute-start.16 = (f32[1,128]{1,0:T(1,128)S(1)}, f32[1,128]{1,0:T(1,128)S(1)}, u32[]{:S(2)}, u32[]{:S(2)}) collective-permute-start(f32[1,128]{1,0:T(1,128)S(1)} %get-tuple-element.56), channel_id=1, source_target_pairs={{0,2},{1,3},{2,0},{3,1},{4,6},{5,7},{6,4},{7,5},{8,10},{9,11},{10,... | collective-permute-start | bytes 1544 | tf_op jit(solution)/shard_map/ppermute | solution.py:137
  40.0 1.0 %collective-permute-start.17 = (f32[1,128]{1,0:T(1,128)S(1)}, f32[1,128]{1,0:T(1,128)S(1)}, u32[]{:S(2)}, u32[]{:S(2)}) collective-permute-start(f32[1,128]{1,0:T(1,128)S(1)} %get-tuple-element.57), channel_id=1, source_target_pairs={{0,3},{1,2},{2,1},{3,0},{4,7},{5,6},{6,5},{7,4},{8,11},{9,10},{10,... | collective-permute-start | bytes 1544 | tf_op jit(solution)/shard_map/ppermute | solution.py:137
  41.0 4.7 %collective-permute-start.18 = (f32[1,128]{1,0:T(1,128)S(1)}, f32[1,128]{1,0:T(1,128)S(1)}, u32[]{:S(2)}, u32[]{:S(2)}) collective-permute-start(f32[1,128]{1,0:T(1,128)S(1)} %get-tuple-element.58), channel_id=1, source_target_pairs={{0,4},{1,5},{2,6},{3,7},{4,0},{5,1},{6,2},{7,3},{8,12},{9,13},{10,... | collective-permute-start | bytes 1544 | tf_op jit(solution)/shard_map/ppermute | solution.py:137
  45.7 0.0 collective-permute-start.19
  45.7 0.0 collective-permute-done.15.refs_1_
  45.7 1.8 %collective-permute-start.20 = (f32[1,128]{1,0:T(1,128)S(1)}, f32[1,128]{1,0:T(1,128)S(1)}, u32[]{:S(2)}, u32[]{:S(2)}) collective-permute-start(f32[1,128]{1,0:T(1,128)S(1)} %get-tuple-element.60), channel_id=1, source_target_pairs={{0,6},{1,7},{2,4},{3,5},{4,2},{5,3},{6,0},{7,1},{8,14},{9,15},{10,... | collective-permute-start | bytes 1544 | tf_op jit(solution)/shard_map/ppermute | solution.py:137
  47.5 0.0 collective-permute-done.16.refs_2_
  47.5 0.6 collective-permute-start.21
  48.1 0.0 collective-permute-done.17.refs_3_
  48.1 2.9 %collective-permute-start.22 = (f32[1,128]{1,0:T(1,128)S(1)}, f32[1,128]{1,0:T(1,128)S(1)}, u32[]{:S(2)}, u32[]{:S(2)}) collective-permute-start(f32[1,128]{1,0:T(1,128)S(1)} %get-tuple-element.62), channel_id=1, source_target_pairs={{0,8},{1,9},{2,10},{3,11},{4,12},{5,13},{6,14},{7,15},{8,0},{9,1},... | collective-permute-start | bytes 1544 | tf_op jit(solution)/shard_map/ppermute | solution.py:137
  51.0 0.0 collective-permute-done.18.refs_4_
  51.0 0.2 collective-permute-start.23
  51.1 0.0 collective-permute-done.19.refs_5_
  51.1 2.5 %collective-permute-start.24 = (f32[1,128]{1,0:T(1,128)S(1)}, f32[1,128]{1,0:T(1,128)S(1)}, u32[]{:S(2)}, u32[]{:S(2)}) collective-permute-start(f32[1,128]{1,0:T(1,128)S(1)} %get-tuple-element.64), channel_id=1, source_target_pairs={{0,10},{1,11},{2,8},{3,9},{4,14},{5,15},{6,12},{7,13},{8,2},{9,3},... | collective-permute-start | bytes 1544 | tf_op jit(solution)/shard_map/ppermute | solution.py:137
  53.7 0.0 collective-permute-done.20.refs_6_
  53.7 0.7 %collective-permute-start.25 = (f32[1,128]{1,0:T(1,128)S(1)}, f32[1,128]{1,0:T(1,128)S(1)}, u32[]{:S(2)}, u32[]{:S(2)}) collective-permute-start(f32[1,128]{1,0:T(1,128)S(1)} %get-tuple-element.65), channel_id=1, source_target_pairs={{0,11},{1,10},{2,9},{3,8},{4,15},{5,14},{6,13},{7,12},{8,3},{9,2},... | collective-permute-start | bytes 1544 | tf_op jit(solution)/shard_map/ppermute | solution.py:137
  54.4 0.0 collective-permute-done.21.refs_7_
  54.4 2.2 %collective-permute-start.26 = (f32[1,128]{1,0:T(1,128)S(1)}, f32[1,128]{1,0:T(1,128)S(1)}, u32[]{:S(2)}, u32[]{:S(2)}) collective-permute-start(f32[1,128]{1,0:T(1,128)S(1)} %get-tuple-element.66), channel_id=1, source_target_pairs={{0,12},{1,13},{2,14},{3,15},{4,8},{5,9},{6,10},{7,11},{8,4},{9,5},... | collective-permute-start | bytes 1544 | tf_op jit(solution)/shard_map/ppermute | solution.py:137
  56.7 0.0 collective-permute-done.22.refs_8_
  56.7 1.6 %collective-permute-start.27 = (f32[1,128]{1,0:T(1,128)S(1)}, f32[1,128]{1,0:T(1,128)S(1)}, u32[]{:S(2)}, u32[]{:S(2)}) collective-permute-start(f32[1,128]{1,0:T(1,128)S(1)} %get-tuple-element.67), channel_id=1, source_target_pairs={{0,13},{1,12},{2,15},{3,14},{4,9},{5,8},{6,11},{7,10},{8,5},{9,4},... | collective-permute-start | bytes 1544 | tf_op jit(solution)/shard_map/ppermute | solution.py:137
  58.2 0.0 collective-permute-done.23.refs_9_
  58.3 2.3 %collective-permute-start.28 = (f32[1,128]{1,0:T(1,128)S(1)}, f32[1,128]{1,0:T(1,128)S(1)}, u32[]{:S(2)}, u32[]{:S(2)}) collective-permute-start(f32[1,128]{1,0:T(1,128)S(1)} %get-tuple-element.68), channel_id=1, source_target_pairs={{0,14},{1,15},{2,12},{3,13},{4,10},{5,11},{6,8},{7,9},{8,6},{9,7},... | collective-permute-start | bytes 1544 | tf_op jit(solution)/shard_map/ppermute | solution.py:137
  60.5 0.0 collective-permute-done.24.refs_10_
  60.5 1.9 %collective-permute-start.29 = (f32[1,128]{1,0:T(1,128)S(1)}, f32[1,128]{1,0:T(1,128)S(1)}, u32[]{:S(2)}, u32[]{:S(2)}) collective-permute-start(f32[1,128]{1,0:T(1,128)S(1)} %get-tuple-element.69), channel_id=1, source_target_pairs={{0,15},{1,14},{2,13},{3,12},{4,11},{5,10},{6,9},{7,8},{8,7},{9,6},... | collective-permute-start | bytes 1544 | tf_op jit(solution)/shard_map/ppermute | solution.py:137
  62.5 0.0 collective-permute-done.25.refs_11_
  62.5 2.0 %collective-permute-done.28.refs_14_ = f32[1,128]{1,0:T(1,128)S(1)} collective-permute-done((f32[1,128]{1,0:T(1,128)S(1)}, f32[1,128]{1,0:T(1,128)S(1)}, u32[]{:S(2)}, u32[]{:S(2)}) %collective-permute-start.28) | collective-permute-done | bytes 544 | tf_op jit(solution)/shard_map/ppermute | solution.py:137
  64.5 1.7 %collective-permute-done.29.refs_15_ = f32[1,128]{1,0:T(1,128)S(1)} collective-permute-done((f32[1,128]{1,0:T(1,128)S(1)}, f32[1,128]{1,0:T(1,128)S(1)}, u32[]{:S(2)}, u32[]{:S(2)}) %collective-permute-start.29) | collective-permute-done | bytes 544 | tf_op jit(solution)/shard_map/ppermute | solution.py:137
  66.2 0.7 %shard_map.39 = f32[1,256]{1,0:T(1,128)} custom-call(f32[1,128]{1,0:T(1,128)S(1)} %get-tuple-element.54.refs_0_, f32[1,128]{1,0:T(1,128)S(1)} %collective-permute-done.15.refs_1_, f32[1,128]{1,0:T(1,128)S(1)} %collective-permute-done.16.refs_2_, f32[1,128]{1,0:T(1,128)S(1)} %collective-permute-done.17.refs_3_, f32[1,128]{1,0:T(1,128)S(1)} %collective-permute-done.18.refs_4_, ...), custom_call_target="tpu_custom_call" | custom-call | tf_op jit(solution)/shard_map/pallas_call | solution.py:126
  (5 shorter events, 0.0 us)
Async XLA Ops:
  0.0 0.7 %copy-start.2 = (s32[256]{0:T(256)S(1)}, s32[256]{0:T(256)}, u32[]{:S(2)}) copy-start(s32[256]{0:T(256)} %param.5) | copy-start | bytes 3076
  0.0 0.7 %copy-start.1 = (s32[256]{0:T(256)S(1)}, s32[256]{0:T(256)}, u32[]{:S(2)}) copy-start(s32[256]{0:T(256)} %param.4) | copy-start | bytes 3076
  0.7 1.0 %copy-start = (bf16[256,1024]{1,0:T(8,128)(2,1)S(1)}, bf16[256,1024]{1,0:T(8,128)(2,1)}, u32[]{:S(2)}) copy-start(bf16[256,1024]{1,0:T(8,128)(2,1)} %refs_0_.1) | copy-start | bytes 1572868
  2.9 5.0 %collective-permute-start = (bf16[32,1152]{1,0:T(8,128)(2,1)S(1)}, bf16[32,1152]{1,0:T(8,128)(2,1)S(1)}, u32[]{:S(2)}, u32[]{:S(2)}) collective-permute-start(bf16[32,1152]{1,0:T(8,128)(2,1)S(1)} %get-tuple-element.39), channel_id=1, source_target_pairs={{0,1},{1,0},{2,3},{3,2},{4,5},{5,4},{6,7},{7,6},{8,9},{9,8},{10,11... | collective-permute-start | bytes 221192 | tf_op jit(solution)/shard_map/ppermute | solution.py:137
  3.4 7.1 %collective-permute-start.1 = (bf16[32,1152]{1,0:T(8,128)(2,1)S(1)}, bf16[32,1152]{1,0:T(8,128)(2,1)S(1)}, u32[]{:S(2)}, u32[]{:S(2)}) collective-permute-start(bf16[32,1152]{1,0:T(8,128)(2,1)S(1)} %get-tuple-element.40), channel_id=1, source_target_pairs={{0,2},{1,3},{2,0},{3,1},{4,6},{5,7},{6,4},{7,5},{8,10},{9,11},{10,... | collective-permute-start | bytes 221192 | tf_op jit(solution)/shard_map/ppermute | solution.py:137
  6.0 4.9 %collective-permute-start.2 = (bf16[32,1152]{1,0:T(8,128)(2,1)S(1)}, bf16[32,1152]{1,0:T(8,128)(2,1)S(1)}, u32[]{:S(2)}, u32[]{:S(2)}) collective-permute-start(bf16[32,1152]{1,0:T(8,128)(2,1)S(1)} %get-tuple-element.41), channel_id=1, source_target_pairs={{0,3},{1,2},{2,1},{3,0},{4,7},{5,6},{6,5},{7,4},{8,11},{9,10},{10,... | collective-permute-start | bytes 221192 | tf_op jit(solution)/shard_map/ppermute | solution.py:137
  6.1 7.4 %collective-permute-start.3 = (bf16[32,1152]{1,0:T(8,128)(2,1)S(1)}, bf16[32,1152]{1,0:T(8,128)(2,1)S(1)}, u32[]{:S(2)}, u32[]{:S(2)}) collective-permute-start(bf16[32,1152]{1,0:T(8,128)(2,1)S(1)} %get-tuple-element.42), channel_id=1, source_target_pairs={{0,4},{1,5},{2,6},{3,7},{4,0},{5,1},{6,2},{7,3},{8,12},{9,13},{10,... | collective-permute-start | bytes 221192 | tf_op jit(solution)/shard_map/ppermute | solution.py:137
  7.9 6.6 %collective-permute-start.4 = (bf16[32,1152]{1,0:T(8,128)(2,1)S(1)}, bf16[32,1152]{1,0:T(8,128)(2,1)S(1)}, u32[]{:S(2)}, u32[]{:S(2)}) collective-permute-start(bf16[32,1152]{1,0:T(8,128)(2,1)S(1)} %get-tuple-element.43), channel_id=1, source_target_pairs={{0,5},{1,4},{2,7},{3,6},{4,1},{5,0},{6,3},{7,2},{8,13},{9,12},{10,... | collective-permute-start | bytes 221192 | tf_op jit(solution)/shard_map/ppermute | solution.py:137
  7.9 9.0 %collective-permute-start.5 = (bf16[32,1152]{1,0:T(8,128)(2,1)S(1)}, bf16[32,1152]{1,0:T(8,128)(2,1)S(1)}, u32[]{:S(2)}, u32[]{:S(2)}) collective-permute-start(bf16[32,1152]{1,0:T(8,128)(2,1)S(1)} %get-tuple-element.44), channel_id=1, source_target_pairs={{0,6},{1,7},{2,4},{3,5},{4,2},{5,3},{6,0},{7,1},{8,14},{9,15},{10,... | collective-permute-start | bytes 221192 | tf_op jit(solution)/shard_map/ppermute | solution.py:137
  10.5 7.4 %collective-permute-start.6 = (bf16[32,1152]{1,0:T(8,128)(2,1)S(1)}, bf16[32,1152]{1,0:T(8,128)(2,1)S(1)}, u32[]{:S(2)}, u32[]{:S(2)}) collective-permute-start(bf16[32,1152]{1,0:T(8,128)(2,1)S(1)} %get-tuple-element.45), channel_id=1, source_target_pairs={{0,7},{1,6},{2,5},{3,4},{4,3},{5,2},{6,1},{7,0},{8,15},{9,14},{10,... | collective-permute-start | bytes 221192 | tf_op jit(solution)/shard_map/ppermute | solution.py:137
  10.9 9.6 %collective-permute-start.7 = (bf16[32,1152]{1,0:T(8,128)(2,1)S(1)}, bf16[32,1152]{1,0:T(8,128)(2,1)S(1)}, u32[]{:S(2)}, u32[]{:S(2)}) collective-permute-start(bf16[32,1152]{1,0:T(8,128)(2,1)S(1)} %get-tuple-element.46), channel_id=1, source_target_pairs={{0,8},{1,9},{2,10},{3,11},{4,12},{5,13},{6,14},{7,15},{8,0},{9,1},... | collective-permute-start | bytes 221192 | tf_op jit(solution)/shard_map/ppermute | solution.py:137
  13.5 13.3 %collective-permute-start.8 = (bf16[32,1152]{1,0:T(8,128)(2,1)S(1)}, bf16[32,1152]{1,0:T(8,128)(2,1)S(1)}, u32[]{:S(2)}, u32[]{:S(2)}) collective-permute-start(bf16[32,1152]{1,0:T(8,128)(2,1)S(1)} %get-tuple-element.47), channel_id=1, source_target_pairs={{0,9},{1,8},{2,11},{3,10},{4,13},{5,12},{6,15},{7,14},{8,1},{9,0},... | collective-permute-start | bytes 221192 | tf_op jit(solution)/shard_map/ppermute | solution.py:137
  14.5 15.7 %collective-permute-start.9 = (bf16[32,1152]{1,0:T(8,128)(2,1)S(1)}, bf16[32,1152]{1,0:T(8,128)(2,1)S(1)}, u32[]{:S(2)}, u32[]{:S(2)}) collective-permute-start(bf16[32,1152]{1,0:T(8,128)(2,1)S(1)} %get-tuple-element.48), channel_id=1, source_target_pairs={{0,10},{1,11},{2,8},{3,9},{4,14},{5,15},{6,12},{7,13},{8,2},{9,3},... | collective-permute-start | bytes 221192 | tf_op jit(solution)/shard_map/ppermute | solution.py:137
  16.8 15.5 %collective-permute-start.10 = (bf16[32,1152]{1,0:T(8,128)(2,1)S(1)}, bf16[32,1152]{1,0:T(8,128)(2,1)S(1)}, u32[]{:S(2)}, u32[]{:S(2)}) collective-permute-start(bf16[32,1152]{1,0:T(8,128)(2,1)S(1)} %get-tuple-element.49), channel_id=1, source_target_pairs={{0,11},{1,10},{2,9},{3,8},{4,15},{5,14},{6,13},{7,12},{8,3},{9,2},... | collective-permute-start | bytes 221192 | tf_op jit(solution)/shard_map/ppermute | solution.py:137
  17.9 14.5 %collective-permute-start.11 = (bf16[32,1152]{1,0:T(8,128)(2,1)S(1)}, bf16[32,1152]{1,0:T(8,128)(2,1)S(1)}, u32[]{:S(2)}, u32[]{:S(2)}) collective-permute-start(bf16[32,1152]{1,0:T(8,128)(2,1)S(1)} %get-tuple-element.50), channel_id=1, source_target_pairs={{0,12},{1,13},{2,14},{3,15},{4,8},{5,9},{6,10},{7,11},{8,4},{9,5},... | collective-permute-start | bytes 221192 | tf_op jit(solution)/shard_map/ppermute | solution.py:137
  20.5 11.8 %collective-permute-start.12 = (bf16[32,1152]{1,0:T(8,128)(2,1)S(1)}, bf16[32,1152]{1,0:T(8,128)(2,1)S(1)}, u32[]{:S(2)}, u32[]{:S(2)}) collective-permute-start(bf16[32,1152]{1,0:T(8,128)(2,1)S(1)} %get-tuple-element.51), channel_id=1, source_target_pairs={{0,13},{1,12},{2,15},{3,14},{4,9},{5,8},{6,11},{7,10},{8,5},{9,4},... | collective-permute-start | bytes 221192 | tf_op jit(solution)/shard_map/ppermute | solution.py:137
  26.8 7.5 %collective-permute-start.13 = (bf16[32,1152]{1,0:T(8,128)(2,1)S(1)}, bf16[32,1152]{1,0:T(8,128)(2,1)S(1)}, u32[]{:S(2)}, u32[]{:S(2)}) collective-permute-start(bf16[32,1152]{1,0:T(8,128)(2,1)S(1)} %get-tuple-element.52), channel_id=1, source_target_pairs={{0,14},{1,15},{2,12},{3,13},{4,10},{5,11},{6,8},{7,9},{8,6},{9,7},... | collective-permute-start | bytes 221192 | tf_op jit(solution)/shard_map/ppermute | solution.py:137
  30.2 7.3 %collective-permute-start.14 = (bf16[32,1152]{1,0:T(8,128)(2,1)S(1)}, bf16[32,1152]{1,0:T(8,128)(2,1)S(1)}, u32[]{:S(2)}, u32[]{:S(2)}) collective-permute-start(bf16[32,1152]{1,0:T(8,128)(2,1)S(1)} %get-tuple-element.53), channel_id=1, source_target_pairs={{0,15},{1,14},{2,13},{3,12},{4,11},{5,10},{6,9},{7,8},{8,7},{9,6},... | collective-permute-start | bytes 221192 | tf_op jit(solution)/shard_map/ppermute | solution.py:137
  39.1 6.6 %collective-permute-start.15 = (f32[1,128]{1,0:T(1,128)S(1)}, f32[1,128]{1,0:T(1,128)S(1)}, u32[]{:S(2)}, u32[]{:S(2)}) collective-permute-start(f32[1,128]{1,0:T(1,128)S(1)} %get-tuple-element.55), channel_id=1, source_target_pairs={{0,1},{1,0},{2,3},{3,2},{4,5},{5,4},{6,7},{7,6},{8,9},{9,8},{10,11... | collective-permute-start | bytes 1544 | tf_op jit(solution)/shard_map/ppermute | solution.py:137
  39.2 8.3 %collective-permute-start.16 = (f32[1,128]{1,0:T(1,128)S(1)}, f32[1,128]{1,0:T(1,128)S(1)}, u32[]{:S(2)}, u32[]{:S(2)}) collective-permute-start(f32[1,128]{1,0:T(1,128)S(1)} %get-tuple-element.56), channel_id=1, source_target_pairs={{0,2},{1,3},{2,0},{3,1},{4,6},{5,7},{6,4},{7,5},{8,10},{9,11},{10,... | collective-permute-start | bytes 1544 | tf_op jit(solution)/shard_map/ppermute | solution.py:137
  40.0 8.1 %collective-permute-start.17 = (f32[1,128]{1,0:T(1,128)S(1)}, f32[1,128]{1,0:T(1,128)S(1)}, u32[]{:S(2)}, u32[]{:S(2)}) collective-permute-start(f32[1,128]{1,0:T(1,128)S(1)} %get-tuple-element.57), channel_id=1, source_target_pairs={{0,3},{1,2},{2,1},{3,0},{4,7},{5,6},{6,5},{7,4},{8,11},{9,10},{10,... | collective-permute-start | bytes 1544 | tf_op jit(solution)/shard_map/ppermute | solution.py:137
  41.0 10.0 %collective-permute-start.18 = (f32[1,128]{1,0:T(1,128)S(1)}, f32[1,128]{1,0:T(1,128)S(1)}, u32[]{:S(2)}, u32[]{:S(2)}) collective-permute-start(f32[1,128]{1,0:T(1,128)S(1)} %get-tuple-element.58), channel_id=1, source_target_pairs={{0,4},{1,5},{2,6},{3,7},{4,0},{5,1},{6,2},{7,3},{8,12},{9,13},{10,... | collective-permute-start | bytes 1544 | tf_op jit(solution)/shard_map/ppermute | solution.py:137
  45.7 5.5 %collective-permute-start.19 = (f32[1,128]{1,0:T(1,128)S(1)}, f32[1,128]{1,0:T(1,128)S(1)}, u32[]{:S(2)}, u32[]{:S(2)}) collective-permute-start(f32[1,128]{1,0:T(1,128)S(1)} %get-tuple-element.59), channel_id=1, source_target_pairs={{0,5},{1,4},{2,7},{3,6},{4,1},{5,0},{6,3},{7,2},{8,13},{9,12},{10,... | collective-permute-start | bytes 1544 | tf_op jit(solution)/shard_map/ppermute | solution.py:137
  45.7 8.0 %collective-permute-start.20 = (f32[1,128]{1,0:T(1,128)S(1)}, f32[1,128]{1,0:T(1,128)S(1)}, u32[]{:S(2)}, u32[]{:S(2)}) collective-permute-start(f32[1,128]{1,0:T(1,128)S(1)} %get-tuple-element.60), channel_id=1, source_target_pairs={{0,6},{1,7},{2,4},{3,5},{4,2},{5,3},{6,0},{7,1},{8,14},{9,15},{10,... | collective-permute-start | bytes 1544 | tf_op jit(solution)/shard_map/ppermute | solution.py:137
  47.5 6.9 %collective-permute-start.21 = (f32[1,128]{1,0:T(1,128)S(1)}, f32[1,128]{1,0:T(1,128)S(1)}, u32[]{:S(2)}, u32[]{:S(2)}) collective-permute-start(f32[1,128]{1,0:T(1,128)S(1)} %get-tuple-element.61), channel_id=1, source_target_pairs={{0,7},{1,6},{2,5},{3,4},{4,3},{5,2},{6,1},{7,0},{8,15},{9,14},{10,... | collective-permute-start | bytes 1544 | tf_op jit(solution)/shard_map/ppermute | solution.py:137
  48.1 8.6 %collective-permute-start.22 = (f32[1,128]{1,0:T(1,128)S(1)}, f32[1,128]{1,0:T(1,128)S(1)}, u32[]{:S(2)}, u32[]{:S(2)}) collective-permute-start(f32[1,128]{1,0:T(1,128)S(1)} %get-tuple-element.62), channel_id=1, source_target_pairs={{0,8},{1,9},{2,10},{3,11},{4,12},{5,13},{6,14},{7,15},{8,0},{9,1},... | collective-permute-start | bytes 1544 | tf_op jit(solution)/shard_map/ppermute | solution.py:137
  51.0 7.3 %collective-permute-start.23 = (f32[1,128]{1,0:T(1,128)S(1)}, f32[1,128]{1,0:T(1,128)S(1)}, u32[]{:S(2)}, u32[]{:S(2)}) collective-permute-start(f32[1,128]{1,0:T(1,128)S(1)} %get-tuple-element.63), channel_id=1, source_target_pairs={{0,9},{1,8},{2,11},{3,10},{4,13},{5,12},{6,15},{7,14},{8,1},{9,0},... | collective-permute-start | bytes 1544 | tf_op jit(solution)/shard_map/ppermute | solution.py:137
  51.1 9.4 %collective-permute-start.24 = (f32[1,128]{1,0:T(1,128)S(1)}, f32[1,128]{1,0:T(1,128)S(1)}, u32[]{:S(2)}, u32[]{:S(2)}) collective-permute-start(f32[1,128]{1,0:T(1,128)S(1)} %get-tuple-element.64), channel_id=1, source_target_pairs={{0,10},{1,11},{2,8},{3,9},{4,14},{5,15},{6,12},{7,13},{8,2},{9,3},... | collective-permute-start | bytes 1544 | tf_op jit(solution)/shard_map/ppermute | solution.py:137
  53.7 8.8 %collective-permute-start.25 = (f32[1,128]{1,0:T(1,128)S(1)}, f32[1,128]{1,0:T(1,128)S(1)}, u32[]{:S(2)}, u32[]{:S(2)}) collective-permute-start(f32[1,128]{1,0:T(1,128)S(1)} %get-tuple-element.65), channel_id=1, source_target_pairs={{0,11},{1,10},{2,9},{3,8},{4,15},{5,14},{6,13},{7,12},{8,3},{9,2},... | collective-permute-start | bytes 1544 | tf_op jit(solution)/shard_map/ppermute | solution.py:137
  54.4 8.0 %collective-permute-start.26 = (f32[1,128]{1,0:T(1,128)S(1)}, f32[1,128]{1,0:T(1,128)S(1)}, u32[]{:S(2)}, u32[]{:S(2)}) collective-permute-start(f32[1,128]{1,0:T(1,128)S(1)} %get-tuple-element.66), channel_id=1, source_target_pairs={{0,12},{1,13},{2,14},{3,15},{4,8},{5,9},{6,10},{7,11},{8,4},{9,5},... | collective-permute-start | bytes 1544 | tf_op jit(solution)/shard_map/ppermute | solution.py:137
  56.7 5.8 %collective-permute-start.27 = (f32[1,128]{1,0:T(1,128)S(1)}, f32[1,128]{1,0:T(1,128)S(1)}, u32[]{:S(2)}, u32[]{:S(2)}) collective-permute-start(f32[1,128]{1,0:T(1,128)S(1)} %get-tuple-element.67), channel_id=1, source_target_pairs={{0,13},{1,12},{2,15},{3,14},{4,9},{5,8},{6,11},{7,10},{8,5},{9,4},... | collective-permute-start | bytes 1544 | tf_op jit(solution)/shard_map/ppermute | solution.py:137
  58.3 6.2 %collective-permute-start.28 = (f32[1,128]{1,0:T(1,128)S(1)}, f32[1,128]{1,0:T(1,128)S(1)}, u32[]{:S(2)}, u32[]{:S(2)}) collective-permute-start(f32[1,128]{1,0:T(1,128)S(1)} %get-tuple-element.68), channel_id=1, source_target_pairs={{0,14},{1,15},{2,12},{3,13},{4,10},{5,11},{6,8},{7,9},{8,6},{9,7},... | collective-permute-start | bytes 1544 | tf_op jit(solution)/shard_map/ppermute | solution.py:137
  60.5 5.7 %collective-permute-start.29 = (f32[1,128]{1,0:T(1,128)S(1)}, f32[1,128]{1,0:T(1,128)S(1)}, u32[]{:S(2)}, u32[]{:S(2)}) collective-permute-start(f32[1,128]{1,0:T(1,128)S(1)} %get-tuple-element.69), channel_id=1, source_target_pairs={{0,15},{1,14},{2,13},{3,12},{4,11},{5,10},{6,9},{7,8},{8,7},{9,6},... | collective-permute-start | bytes 1544 | tf_op jit(solution)/shard_map/ppermute | solution.py:137

commit v3 on v1

v3 whole, which is shorter than its diff:
```python
import jax
import jax.numpy as jnp
from jax import lax
from jax.experimental import pallas as pl
from jax.experimental.pallas import tpu as pltpu
from jax.sharding import PartitionSpec as P

CL_DEV = 8
LANES = 128
RADIX = 256
SPAN = 65536


def iota(shape, dim):
    return lax.broadcasted_iota(jnp.int32, shape, dim)


def matmul_nt(left, right):
    return lax.dot_general(
        left, right, (((1,), (1,)), ((), ())), preferred_element_type=jnp.float32
    )


def matmul(left, right):
    return jnp.dot(left, right, preferred_element_type=jnp.float32)


def onehots(mask):
    return jnp.where(mask, 1.0, 0.0).astype(jnp.bfloat16)


def pack_kernel(owners, capacity, emb_any, cl_any, rk_any, *rest):
    out_ref, place_ref, emb_ref, cl_ref, rk_ref, sems = rest
    copies = [
        pltpu.make_async_copy(source, target, sems.at[number])
        for number, (source, target) in enumerate(
            ((cl_any, cl_ref), (rk_any, rk_ref), (emb_any, emb_ref))
        )
    ]
    for copy in copies:
        copy.start()
    rows, width = emb_ref.shape
    slots = owners * capacity
    copies[0].wait()
    cl = cl_ref[...]
    owner = cl // CL_DEV
    mine = iota((owners, rows), 0) == owner
    earlier = onehots(iota((rows, rows), 0) < iota((rows, rows), 1))
    before = matmul(onehots(mine), earlier)
    pos = jnp.sum(jnp.where(mine, before, 0.0), axis=0, keepdims=True).astype(jnp.int32)
    place = owner * capacity + pos
    place_ref[...] = place
    place = onehots(iota((slots, rows), 0) == place)
    copies[1].wait()
    rk = rk_ref[...]
    line = iota((LANES, rows), 0)
    meta = jnp.where(
        line == 0,
        cl - owner * CL_DEV + 1,
        jnp.where(line == 1, rk // RADIX, jnp.where(line == 2, rk % RADIX, 0)),
    )
    meta = meta.astype(jnp.float32).astype(jnp.bfloat16)
    out_ref[:, width:] = matmul_nt(place, meta).astype(jnp.bfloat16)
    copies[2].wait()
    wide = emb_ref[...].astype(jnp.float32)
    squares = jnp.sum(wide * wide, axis=1, keepdims=True)
    unit = (wide * lax.rsqrt(squares + 1e-06)).astype(jnp.bfloat16)
    out_ref[:, :width] = matmul(place, unit).astype(jnp.bfloat16)


def match_kernel(in_ref, out_ref):
    slots, full = in_ref.shape
    width = full - LANES
    meta = in_ref[:, width:]
    units = in_ref[:, :width]
    pick = onehots(iota((8, LANES), 0) == iota((8, LANES), 1))
    across = matmul_nt(pick, meta)
    low = across[0:1] * SPAN
    code = low + across[1:2] * RADIX + across[2:3]
    down = meta.astype(jnp.float32)
    code_down = down[:, 0:1] * SPAN + down[:, 1:2] * RADIX + down[:, 2:3]
    best = jnp.full((1, slots), -1.0, jnp.float32)
    step = min(LANES, slots)
    for start in range(0, slots, step):
        sims = matmul_nt(units[start:start + step], units)
        key = code_down[start:start + step]
        seen = jnp.where((key >= low) & (key < code), sims, -1.0)
        best = jnp.maximum(best, jnp.max(seen, axis=0, keepdims=True))
    out_ref[0] = best


def unpack_kernel(capacity, got_ref, place_ref, out_ref):
    owners, _, slots = got_ref.shape
    rows = place_ref.shape[1]
    place = place_ref[...]
    got = got_ref[:, 0, :]
    high = got.astype(jnp.bfloat16)
    rest = got - high.astype(jnp.float32)
    middle = rest.astype(jnp.bfloat16)
    last = (rest - middle.astype(jnp.float32)).astype(jnp.bfloat16)
    slot = lax.axis_index("shard") * capacity + lax.rem(place, capacity)
    pick = onehots(iota((slots, rows), 0) == slot)
    found = matmul(high, pick) + matmul(middle, pick) + matmul(last, pick)
    mine = iota((owners, rows), 0) == lax.div(place, capacity)
    out_ref[...] = jnp.sum(jnp.where(mine, found, 0.0), axis=0, keepdims=True)


def call(kernel, shapes, *args, **kwargs):
    return pl.pallas_call(
        kernel,
        out_shape=shapes,
        compiler_params=pltpu.CompilerParams(vmem_limit_bytes=60 * 2**20),
        **kwargs,
    )(*args)


def shards(embeddings, cluster_ids, priority):
    rows, width = embeddings.shape
    owners = lax.axis_size("shard")
    capacity = max(2, 2 * rows // owners)
    slots = owners * capacity
    full = width + LANES

    def pack(*refs):
        pack_kernel(owners, capacity, *refs)

    def unpack(*refs):
        unpack_kernel(capacity, *refs)

    outgoing, place = call(
        pack,
        (
            jax.ShapeDtypeStruct((slots, full), jnp.bfloat16),
            jax.ShapeDtypeStruct((1, rows), jnp.int32),
        ),
        embeddings, cluster_ids.reshape(1, rows), priority.reshape(1, rows),
        in_specs=[pl.BlockSpec(memory_space=pl.ANY)] * 3,
        scratch_shapes=[
            pltpu.VMEM((rows, width), jnp.bfloat16),
            pltpu.VMEM((1, rows), jnp.int32),
            pltpu.VMEM((1, rows), jnp.int32),
            pltpu.SemaphoreType.DMA((3,)),
        ],
    )
    arrived = lax.all_to_all(
        outgoing.reshape(owners, capacity, full), "shard", 0, 0, tiled=True
    ).reshape(slots, full)
    maxima = call(match_kernel, jax.ShapeDtypeStruct((1, 1, slots), jnp.float32), arrived)
    returned = lax.all_gather(maxima, "shard", axis=0, tiled=True)
    out = call(unpack, jax.ShapeDtypeStruct((1, rows), jnp.float32), returned, place)
    return out.reshape(rows)


def solution(mesh):
    placed = (P(("groups", "shard"), None), P(("groups", "shard")), P(("groups", "shard")))
    return jax.shard_map(
        shards, mesh=mesh, in_specs=placed, out_specs=P(("groups", "shard")), check_vma=False
    )
```

time: 51.8 us -> 65.9 us (1.27)
  blocking collectives: 46.2 us -> 57.7 us
  Pallas kernels: 2.99 us -> 7.86 us
  local copies, waits for them, and re-layouts: 2.4 us -> 0 us
    all_gather x0 -> x1, blocking collectives: none -> 20.7 us  [shards(): returned = lax.all_gather(maxima, 'shard', axis=0, tiled=True)]
    all_to_all x2 -> x1, blocking collectives: 46.2 us -> 37 us  [shards(): lax.all_to_all(outgoing.reshape(owners, capacity, full), 'shard', 0, 0, t...]
    pallas_call x3, Pallas kernels: 2.99 us -> 7.86 us  [call(): pl.pallas_call(kernel, out_shape=shapes, compiler_params=pltpu.CompilerPa...]
    unnamed x8 -> x0, local copies, waits for them, and re-layouts: 2.4 us -> none
where the time goes in v3:
time: 65.9 us; the launch traced here: 65.6 us
  blocking collectives  57.7 us (88%)
  Pallas kernels  7.86 us (12%)
    all_to_all x1, blocking collectives, shards(): lax.all_to_all(outgoing.reshape(owners, capacity, full), 'shard', 0, 0, t...  37 us
    all_gather x1, blocking collectives, shards(): returned = lax.all_gather(maxima, 'shard', axis=0, tiled=True)  20.7 us
    pallas_call x3, Pallas kernels, call(): pl.pallas_call(kernel, out_shape=shapes, compiler_params=pltpu.CompilerPa...  7.86 us

profile of v3, /device:TPU:0, one launch (start us, length us, event | category | flops | bytes accessed | tf_op | source)
XLA Modules:
  0.0 65.6 jit_solution(15277582889556445123)
XLA Ops:
  0.0 2.8 %shard_map.37 = (bf16[512,1152]{1,0:T(8,128)(2,1)}, s32[1,256]{1,0:T(1,128)}) custom-call(bf16[256,1024]{1,0:T(8,128)(2,1)} %refs_0_.1, s32[1,256]{1,0:T(1,128)} %bitcast.7, s32[1,256]{1,0:T(1,128)} %bitcast.8), custom_call_target="tpu_custom_call" | custom-call | tf_op jit(solution)/shard_map/pallas_call | solution.py:109
  2.8 37.0 %all_to_all.5 = bf16[16,32,1152]{2,1,0:T(8,128)(2,1)} all-to-all(bf16[16,32,1152]{2,1,0:T(8,128)(2,1)} %bitcast.6), channel_id=1, replica_groups=mesh['groups'=2,'shard'=16] {'shard'}, dimensions={0} | all-to-all | bytes 2359296 | tf_op jit(solution)/shard_map/all_to_all | solution.py:145
  39.8 3.4 %shard_map.38 = f32[1,1,512]{2,1,0:T(1,128)} custom-call(bf16[512,1152]{1,0:T(8,128)(2,1)} %bitcast.5), custom_call_target="tpu_custom_call" | custom-call | tf_op jit(solution)/shard_map/pallas_call | solution.py:109
  43.2 20.7 %all_gather.3.refs_0_ = f32[16,1,512]{2,1,0:T(1,128)} all-gather(f32[1,1,512]{2,1,0:T(1,128)} %shard_map.38), channel_id=1, replica_groups=mesh['groups'=2,'shard'=16] {'shard'}, dimensions={0}, use_global_device_ids=true | all-gather | bytes 34816 | tf_op jit(solution)/shard_map/all_gather | solution.py:149
  63.9 1.7 %shard_map.39 = f32[1,256]{1,0:T(1,128)} custom-call(f32[16,1,512]{2,1,0:T(1,128)} %all_gather.3.refs_0_, s32[1,256]{1,0:T(1,128)} %get-tuple-element.8.refs_1_), custom_call_target="tpu_custom_call" | custom-call | tf_op jit(solution)/shard_map/pallas_call | solution.py:109

commit v4 on v1

v4 whole, which is shorter than its diff:
```python
import jax
import jax.numpy as jnp
from jax import lax
from jax.experimental import pallas as pl
from jax.experimental.pallas import tpu as pltpu
from jax.sharding import PartitionSpec as P

CL_DEV = 8
LANES = 128
RADIX = 256
SPAN = 65536
META = 16


def iota(shape, dim):
    return lax.broadcasted_iota(jnp.int32, shape, dim)


def matmul_nt(left, right):
    return lax.dot_general(
        left, right, (((1,), (1,)), ((), ())), preferred_element_type=jnp.float32
    )


def matmul(left, right):
    return jnp.dot(left, right, preferred_element_type=jnp.float32)


def onehots(mask):
    return jnp.where(mask, 1.0, 0.0).astype(jnp.bfloat16)


def pack_kernel(owners, capacity, tall, emb_ref, code_ref, out_ref, place_ref):
    rows, width = emb_ref.shape
    slots = owners * capacity
    earlier = onehots(iota((rows, rows), 0) < iota((rows, rows), 1))
    code = code_ref[...]
    cl = lax.div(code, SPAN)
    rk = lax.rem(code, SPAN)
    owner = lax.div(cl, CL_DEV)
    mine = iota((owners, rows), 0) == owner
    before = matmul(onehots(mine), earlier)
    pos = jnp.sum(jnp.where(mine, before, 0.0), axis=0, keepdims=True).astype(jnp.int32)
    place = owner * capacity + pos
    place_ref[...] = place
    place = onehots(iota((slots, rows), 0) == place)
    line = iota((META if tall else LANES, rows), 0)
    meta = jnp.where(
        line == 0,
        cl - owner * CL_DEV + 1,
        jnp.where(line == 1, lax.div(rk, RADIX), jnp.where(line == 2, lax.rem(rk, RADIX), 0)),
    )
    meta = meta.astype(jnp.float32).astype(jnp.bfloat16)
    wide = emb_ref[...].astype(jnp.float32)
    squares = jnp.sum(wide * wide, axis=1, keepdims=True)
    unit = (wide * lax.rsqrt(squares + 1e-06)).astype(jnp.bfloat16)
    unit = matmul(place, unit).astype(jnp.bfloat16)
    if not tall:
        out_ref[:, :width] = unit
        out_ref[:, width:] = matmul_nt(place, meta).astype(jnp.bfloat16)
        return
    meta = matmul_nt(meta, place).astype(jnp.bfloat16)
    pieces = width // LANES
    for target in range(owners):
        top = target * capacity
        for piece in range(pieces):
            out_ref[target, piece * capacity:(piece + 1) * capacity] = unit[
                top:top + capacity, piece * LANES:(piece + 1) * LANES
            ]
        left = top // LANES * LANES
        out_ref[target, pieces * capacity:] = meta[:, left:left + LANES]


def match_kernel(owners, capacity, tall, in_ref, out_ref, *scratch):
    slots = owners * capacity
    if tall:
        units = scratch[0]
        pieces = units.shape[1] // LANES
        for piece in range(pieces):
            units[:, piece * LANES:(piece + 1) * LANES] = in_ref[
                :, piece * capacity:(piece + 1) * capacity
            ].reshape(slots, LANES)
        meta = in_ref[:, pieces * capacity:].reshape(owners * META, LANES)
        left = lax.rem(lax.axis_index("shard") * capacity, LANES)
        shape = (LANES, slots)
        spread = onehots(iota(shape, 0) == left + lax.rem(iota(shape, 1), capacity))
        lines = matmul(meta, spread)
        shape = (owners * META, slots)
        kind = lax.rem(iota(shape, 0), META)
        weight = jnp.where(kind == 0, SPAN, jnp.where(kind == 1, RADIX, jnp.where(kind == 2, 1, 0)))
        own = lax.div(iota(shape, 0), META) == lax.div(iota(shape, 1), capacity)
        code = jnp.where(own, lines * weight.astype(jnp.float32), 0.0)
        code = jnp.sum(code, axis=0, keepdims=True)
        low = code - lax.rem(code.astype(jnp.int32), SPAN).astype(jnp.float32)
        code_down = jnp.broadcast_to(code, (8, slots)).T[:, 0:1]
    else:
        width = in_ref.shape[1] - LANES
        units = in_ref
        meta = in_ref[:, width:]
        pick = onehots(iota((8, LANES), 0) == iota((8, LANES), 1))
        across = matmul_nt(pick, meta)
        low = across[0:1] * SPAN
        code = low + across[1:2] * RADIX + across[2:3]
        down = meta.astype(jnp.float32)
        code_down = down[:, 0:1] * SPAN + down[:, 1:2] * RADIX + down[:, 2:3]
    width = units.shape[1] if tall else width
    best = jnp.full((1, slots), -1.0, jnp.float32)
    step = min(LANES, slots)
    for start in range(0, slots, step):
        sims = matmul_nt(units[start:start + step, :width], units[:, :width])
        key = code_down[start:start + step]
        seen = jnp.where((key >= low) & (key < code), sims, -1.0)
        best = jnp.maximum(best, jnp.max(seen, axis=0, keepdims=True))
    for source in range(owners):
        base = source * capacity // LANES * LANES
        out_ref[source] = best[:, base:base + LANES]


def unpack_kernel(capacity, got_ref, place_ref, out_ref):
    owners = got_ref.shape[0]
    rows = place_ref.shape[1]
    place = place_ref[...]
    got = got_ref[:, 0, :]
    high = got.astype(jnp.bfloat16)
    rest = got - high.astype(jnp.float32)
    middle = rest.astype(jnp.bfloat16)
    last = (rest - middle.astype(jnp.float32)).astype(jnp.bfloat16)
    lane = lax.rem(place, capacity) + lax.rem(lax.axis_index("shard") * capacity, LANES)
    pick = onehots(iota((LANES, rows), 0) == lane)
    found = matmul(high, pick) + matmul(middle, pick) + matmul(last, pick)
    mine = iota((owners, rows), 0) == lax.div(place, capacity)
    out_ref[...] = jnp.sum(jnp.where(mine, found, 0.0), axis=0, keepdims=True)


def call(kernel, shapes, *args, **kwargs):
    return pl.pallas_call(
        kernel,
        out_shape=shapes,
        compiler_params=pltpu.CompilerParams(vmem_limit_bytes=32 * 2**20),
        **kwargs,
    )(*args)


def shards(embeddings, cluster_ids, priority):
    rows, width = embeddings.shape
    owners = lax.axis_size("shard")
    capacity = max(2, 2 * rows // owners)
    slots = owners * capacity
    tall = capacity % 16 == 0 and LANES % capacity == 0
    if tall:
        packed = (owners, width // LANES * capacity + META, LANES)
    else:
        packed = (slots, width + LANES)

    def pack(*refs):
        pack_kernel(owners, capacity, tall, *refs)

    def match(*refs):
        match_kernel(owners, capacity, tall, *refs)

    def unpack(*refs):
        unpack_kernel(capacity, *refs)

    outgoing, place = call(
        pack,
        (
            jax.ShapeDtypeStruct(packed, jnp.bfloat16),
            jax.ShapeDtypeStruct((1, rows), jnp.int32),
        ),
        embeddings, (cluster_ids * SPAN + priority).reshape(1, rows),
    )
    arrived = lax.all_to_all(
        outgoing.reshape(owners, -1, packed[-1]), "shard", 0, 0, tiled=True
    ).reshape(packed)
    maxima = call(
        match,
        jax.ShapeDtypeStruct((owners, 1, LANES), jnp.float32),
        arrived,
        scratch_shapes=[pltpu.VMEM((slots, width), jnp.bfloat16)] if tall else [],
    )
    returned = lax.all_to_all(maxima, "shard", 0, 0, tiled=True)
    out = call(unpack, jax.ShapeDtypeStruct((1, rows), jnp.float32), returned, place)
    return out.reshape(rows)


def solution(mesh):
    placed = (P(("groups", "shard"), None), P(("groups", "shard")), P(("groups", "shard")))
    return jax.shard_map(
        shards, mesh=mesh, in_specs=placed, out_specs=P(("groups", "shard")), check_vma=False
    )
```

time: 51.8 us -> 49.9 us (0.963)
  local copies, waits for them, and re-layouts: 2.4 us -> 1.04 us
  blocking collectives: 46.2 us -> 44.9 us
  other arithmetic: 0 us -> 0.7 us
    unnamed x8 -> x2, local copies, waits for them, and re-layouts: 2.4 us -> 1.04 us
    all_to_all x2, blocking collectives: 46.2 us -> 44.9 us  [the longest x1 35.7 us: shards(): lax.all_to_all(outgoing.reshape(owners, -1, packed[-1]), 'shard', 0, 0, t...]
    add x0 -> x1, other arithmetic: none -> 0.7 us  [shards(): cluster_ids * SPAN + priority]
where the time goes in v4:
time: 49.9 us; the launch traced here: 49.7 us
  blocking collectives  44.9 us (90%)
  Pallas kernels  3 us (6%)
  local copies, waits for them, and re-layouts  1.04 us (2%)
  other arithmetic  0.7 us (1%)
    all_to_all x1, blocking collectives, shards(): lax.all_to_all(outgoing.reshape(owners, -1, packed[-1]), 'shard', 0, 0, t...  35.7 us
    all_to_all x1, blocking collectives, shards(): returned = lax.all_to_all(maxima, 'shard', 0, 0, tiled=True)  9.23 us
    pallas_call x3, Pallas kernels, call(): pl.pallas_call(kernel, out_shape=shapes, compiler_params=pltpu.CompilerPa...  3 us
    unnamed x2, local copies, waits for them, and re-layouts  1.04 us

profile of v4, /device:TPU:0, one launch (start us, length us, event | category | flops | bytes accessed | tf_op | source)
XLA Modules:
  0.0 49.7 jit_solution(15224407747724955914)
XLA Ops:
  0.0 0.7 %multiply_add_fusion = s32[256]{0:T(256)S(1)} fusion(s32[256]{0:T(256)} %param.5, s32[256]{0:T(256)} %param.4), kind=kLoop, calls=%fused_computation | loop fusion | flops 512 | bytes 3072 | tf_op jit(solution)/shard_map/add | solution.py:170
  0.7 0.0 copy-start
  0.7 1.0 %copy-done = bf16[256,1024]{1,0:T(8,128)(2,1)S(1)} copy-done((bf16[256,1024]{1,0:T(8,128)(2,1)S(1)}, bf16[256,1024]{1,0:T(8,128)(2,1)}, u32[]{:S(2)}) %copy-start) | copy-done | bytes 524312
  1.7 0.6 %shard_map.37 = (bf16[16,272,128]{2,1,0:T(8,128)(2,1)S(1)}, s32[1,256]{1,0:T(1,128)S(1)}) custom-call(bf16[256,1024]{1,0:T(8,128)(2,1)S(1)} %copy-done, s32[1,256]{1,0:T(1,128)S(1)} %bitcast.2), custom_call_target="tpu_custom_call" | custom-call | tf_op jit(solution)/shard_map/pallas_call | solution.py:136
  2.4 35.7 %all_to_all.10.refs_0_ = bf16[16,272,128]{2,1,0:T(8,128)(2,1)S(1)} all-to-all(bf16[16,272,128]{2,1,0:T(8,128)(2,1)S(1)} %get-tuple-element.7), channel_id=1, replica_groups=mesh['groups'=2,'shard'=16] {'shard'}, dimensions={0} | all-to-all | bytes 2228224 | tf_op jit(solution)/shard_map/all_to_all | solution.py:172
  38.1 1.6 %shard_map.38 = f32[16,1,128]{2,1,0:T(1,128)S(1)} custom-call(bf16[16,272,128]{2,1,0:T(8,128)(2,1)S(1)} %all_to_all.10.refs_0_), custom_call_target="tpu_custom_call" | custom-call | tf_op jit(solution)/shard_map/pallas_call | solution.py:136
  39.7 9.2 %all_to_all.11.refs_0_ = f32[16,1,128]{2,1,0:T(1,128)S(1)} all-to-all(f32[16,1,128]{2,1,0:T(1,128)S(1)} %shard_map.38), channel_id=1, replica_groups=mesh['groups'=2,'shard'=16] {'shard'}, dimensions={0} | all-to-all | bytes 16384 | tf_op jit(solution)/shard_map/all_to_all | solution.py:181
  48.9 0.7 %shard_map.39 = f32[1,256]{1,0:T(1,128)} custom-call(f32[16,1,128]{2,1,0:T(1,128)S(1)} %all_to_all.11.refs_0_, s32[1,256]{1,0:T(1,128)S(1)} %get-tuple-element.8.refs_1_), custom_call_target="tpu_custom_call" | custom-call | tf_op jit(solution)/shard_map/pallas_call | solution.py:136
Async XLA Ops:
  0.7 1.0 %copy-start = (bf16[256,1024]{1,0:T(8,128)(2,1)S(1)}, bf16[256,1024]{1,0:T(8,128)(2,1)}, u32[]{:S(2)}) copy-start(bf16[256,1024]{1,0:T(8,128)(2,1)} %refs_0_.1) | copy-start | bytes 1572868

commit v5 on v1

v5 whole, which is shorter than its diff:
```python
import jax
import jax.numpy as jnp
from jax import lax
from jax.experimental import pallas as pl
from jax.experimental.pallas import tpu as pltpu
from jax.sharding import PartitionSpec as P

CL_DEV = 8
LANES = 128
RADIX = 256
SPAN = 65536
META = 16
SPILL = 16


def iota(shape, dim):
    return lax.broadcasted_iota(jnp.int32, shape, dim)


def matmul_nt(left, right):
    return lax.dot_general(
        left, right, (((1,), (1,)), ((), ())), preferred_element_type=jnp.float32
    )


def matmul(left, right):
    return jnp.dot(left, right, preferred_element_type=jnp.float32)


def onehots(mask):
    return jnp.where(mask, 1.0, 0.0).astype(jnp.bfloat16)


def normalised(emb_ref):
    wide = emb_ref[...].astype(jnp.float32)
    squares = jnp.sum(wide * wide, axis=1, keepdims=True)
    return (wide * lax.rsqrt(squares + 1e-06)).astype(jnp.bfloat16)


def positions(owners, code):
    rows = code.shape[1]
    owner = lax.div(code, SPAN * CL_DEV)
    earlier = onehots(iota((rows, rows), 0) < iota((rows, rows), 1))
    mine = iota((owners, rows), 0) == owner
    before = matmul(onehots(mine), earlier)
    pos = jnp.sum(jnp.where(mine, before, 0.0), axis=0, keepdims=True).astype(jnp.int32)
    return owner, pos, earlier


def as_column(row):
    return jnp.broadcast_to(row, (8, row.shape[1])).T[:, 0:1]


def row_base(code):
    return code - lax.rem(code.astype(jnp.int32), SPAN).astype(jnp.float32)


def best_earlier(best, keys, key_code, queries, code, low):
    sims = matmul_nt(keys, queries)
    seen = jnp.where((key_code >= low) & (key_code < code), sims, -1.0)
    return jnp.maximum(best, jnp.max(seen, axis=0, keepdims=True))


def picked(got, pick):
    high = got.astype(jnp.bfloat16)
    rest = got - high.astype(jnp.float32)
    middle = rest.astype(jnp.bfloat16)
    last = (rest - middle.astype(jnp.float32)).astype(jnp.bfloat16)
    return matmul(high, pick) + matmul(middle, pick) + matmul(last, pick)


def pack_all_kernel(owners, capacity, emb_ref, code_ref, out_ref, place_ref):
    rows, width = emb_ref.shape
    code = code_ref[...]
    owner, pos, _ = positions(owners, code)
    place = owner * capacity + pos
    place_ref[...] = place
    place = onehots(iota((owners * capacity, rows), 0) == place)
    cl = lax.div(code, SPAN) - owner * CL_DEV + 1
    rk = lax.rem(code, SPAN)
    line = iota((LANES, rows), 0)
    meta = jnp.where(line == 0, cl, jnp.where(line == 1, lax.div(rk, RADIX), lax.rem(rk, RADIX)))
    meta = jnp.where(line < 3, meta, 0).astype(jnp.float32).astype(jnp.bfloat16)
    out_ref[:, width:] = matmul_nt(place, meta).astype(jnp.bfloat16)
    out_ref[:, :width] = matmul(place, normalised(emb_ref)).astype(jnp.bfloat16)


def match_all_kernel(owners, capacity, in_ref, out_ref):
    slots, full = in_ref.shape
    width = full - LANES
    pick = onehots(iota((8, LANES), 0) == iota((8, LANES), 1))
    across = matmul_nt(pick, in_ref[:, width:])
    code = across[0:1] * SPAN + across[1:2] * RADIX + across[2:3]
    low = row_base(code)
    down = in_ref[:, width:].astype(jnp.float32)
    key_code = down[:, 0:1] * SPAN + down[:, 1:2] * RADIX + down[:, 2:3]
    best = jnp.full((1, slots), -1.0, jnp.float32)
    step = min(LANES, slots)
    for start in range(0, slots, step):
        best = best_earlier(
            best, in_ref[start:start + step, :width], key_code[start:start + step],
            in_ref[:, :width], code, low,
        )
    for source in range(owners):
        base = source * capacity // LANES * LANES
        out_ref[source] = best[:, base:base + LANES]


def unpack_all_kernel(capacity, got_ref, place_ref, out_ref):
    owners = got_ref.shape[0]
    rows = place_ref.shape[1]
    place = place_ref[...]
    lane = lax.rem(place, capacity) + lax.rem(lax.axis_index("shard") * capacity, LANES)
    found = picked(got_ref[:, 0, :], onehots(iota((LANES, rows), 0) == lane))
    mine = iota((owners, rows), 0) == lax.div(place, capacity)
    out_ref[...] = jnp.sum(jnp.where(mine, found, 0.0), axis=0, keepdims=True)


def pack_kernel(owners, tight, capacity, emb_ref, code_ref, out_ref, spill_ref, place_ref):
    rows, width = emb_ref.shape
    code = code_ref[...]
    owner, pos, earlier = positions(owners, code)
    over = pos >= tight
    number = matmul(jnp.broadcast_to(onehots(over), (META, rows)), earlier)[0:1].astype(jnp.int32)
    total = jnp.sum(jnp.where(over, 1.0, 0.0), axis=1, keepdims=True)
    place = jnp.where(over, owners * capacity + number, owner * capacity + pos)
    place_ref[...] = owner * RADIX + jnp.where(over, tight + number, pos)
    cl = lax.div(code, SPAN) + 1
    rk = lax.rem(code, SPAN)
    kinds = (cl, lax.div(rk, RADIX), lax.rem(rk, RADIX))
    line = iota((META, rows), 0)
    groups = owners * capacity // LANES
    meta = jnp.where(iota((META, LANES), 0) == META - 1, total, 0.0)
    for group in range(groups + 1):
        block = jnp.zeros((META, rows), jnp.int32)
        for kind, values in enumerate(kinds):
            at = kind * groups + group if group < groups else groups * len(kinds) + kind
            block = jnp.where(line == at, values, block)
        seats = onehots(iota((LANES, rows), 0) + group * LANES == place)
        meta += matmul_nt(block.astype(jnp.float32).astype(jnp.bfloat16), seats)
    unit = normalised(emb_ref)
    spilt = onehots(iota((SPILL, rows), 0) + owners * capacity == place)
    spilt = matmul(spilt, unit).astype(jnp.bfloat16)
    pieces = width // LANES
    for piece in range(pieces):
        spill_ref[0, piece * SPILL:(piece + 1) * SPILL] = spilt[:, piece * LANES:(piece + 1) * LANES]
    spill_ref[0, pieces * SPILL:] = meta.astype(jnp.bfloat16)
    slot = jnp.where(over, -1, owner * tight + pos)
    out_ref[...] = matmul(
        onehots(iota((owners * tight, rows), 0) == slot), unit
    ).astype(jnp.bfloat16)


def window(source, tight, slots):
    return min(source * tight // LANES * LANES, slots - 2 * LANES)


def match_kernel(owners, tight, capacity, in_ref, spill_ref, out_ref, more_ref, extra):
    slots, width = in_ref.shape
    pieces = width // LANES
    spilt = owners * SPILL
    for piece in range(pieces):
        extra[:, piece * LANES:(piece + 1) * LANES] = spill_ref[
            :, piece * SPILL:(piece + 1) * SPILL
        ].reshape(spilt, LANES)
    meta = spill_ref[:, pieces * SPILL:].reshape(owners * META, LANES)
    lines = owners * META
    kind = lax.rem(iota((lines, 1), 0), META)
    groups = owners * capacity // LANES
    start = lax.axis_index("shard") * capacity
    group = lax.div(start, LANES)
    scales = (SPAN, RADIX, 1)

    def codes(count, at, first):
        shape = (LANES, count * owners)
        seats = onehots(iota(shape, 0) == first + lax.rem(iota(shape, 1), count))
        shape = (lines, count * owners)
        own = lax.div(iota(shape, 0), META) == lax.div(iota(shape, 1), count)
        weight = jnp.zeros((lines, 1), jnp.float32)
        for number, scale in enumerate(scales):
            weight = jnp.where(kind == at(number), float(scale), weight)
        found = jnp.where(own, matmul(meta, seats) * weight, 0.0)
        return jnp.sum(found, axis=0, keepdims=True)

    code = codes(tight, lambda number: number * groups + group, lax.rem(start, LANES))
    code_extra = codes(SPILL, lambda number: groups * len(scales) + number, 0)
    counts = jnp.where(kind == META - 1, meta.astype(jnp.float32), 0.0)
    more_ref[0, 0] = jnp.where(jnp.max(counts) > SPILL, 1, 0)
    low, low_extra = row_base(code), row_base(code_extra)
    best = jnp.full((1, slots), -1.0, jnp.float32)
    best_extra = jnp.full((1, spilt), -1.0, jnp.float32)
    for ref, key_code in ((in_ref, as_column(code)), (extra, as_column(code_extra))):
        for start in range(0, ref.shape[0], LANES):
            keys = ref[start:start + LANES]
            key = key_code[start:start + LANES]
            best = best_earlier(best, keys, key, in_ref[...], code, low)
            best_extra = best_earlier(best_extra, keys, key, extra[...], code_extra, low_extra)
    for source in range(owners):
        base = window(source, tight, slots)
        out_ref[source, :, :2 * LANES] = best[:, base:base + 2 * LANES]
        base = source * SPILL // LANES * LANES
        out_ref[source, :, 2 * LANES:] = best_extra[:, base:base + LANES]


def unpack_kernel(owners, tight, got_ref, place_ref, out_ref):
    rows = place_ref.shape[1]
    me = lax.axis_index("shard")
    place = place_ref[...]
    seat = lax.rem(place, RADIX)
    base = lax.div(me * tight, LANES) * LANES
    base = jnp.minimum(base, owners * tight - 2 * LANES)
    lane = jnp.where(
        seat < tight,
        me * tight - base + seat,
        2 * LANES + lax.rem(me * SPILL, LANES) + seat - tight,
    )
    found = picked(got_ref[:, 0, :], onehots(iota((3 * LANES, rows), 0) == lane))
    mine = iota((owners, rows), 0) == lax.div(place, RADIX)
    out_ref[...] = jnp.sum(jnp.where(mine, found, 0.0), axis=0, keepdims=True)


def call(kernel, shapes, *args, sizes=(), **kwargs):
    def body(*refs):
        kernel(*sizes, *refs)

    return pl.pallas_call(
        body,
        out_shape=shapes,
        compiler_params=pltpu.CompilerParams(vmem_limit_bytes=32 * 2**20),
        **kwargs,
    )(*args)


def exchange(blocks):
    return lax.all_to_all(blocks, "shard", split_axis=0, concat_axis=0, tiled=True)


def with_room_for_all(owners, capacity, embeddings, code):
    rows, width = embeddings.shape
    slots, full = owners * capacity, width + LANES
    seats = jax.ShapeDtypeStruct((1, rows), jnp.int32)
    result = jax.ShapeDtypeStruct((1, rows), jnp.float32)
    packed = jax.ShapeDtypeStruct((slots, full), jnp.bfloat16)
    found = jax.ShapeDtypeStruct((owners, 1, LANES), jnp.float32)
    sizes = (owners, capacity)
    outgoing, place = call(pack_all_kernel, (packed, seats), embeddings, code, sizes=sizes)
    arrived = exchange(outgoing.reshape(owners, capacity, full)).reshape(slots, full)
    maxima = call(match_all_kernel, found, arrived, sizes=sizes)
    return call(unpack_all_kernel, result, exchange(maxima), place, sizes=(capacity,))


def shards(embeddings, cluster_ids, priority):
    rows, width = embeddings.shape
    owners = lax.axis_size("shard")
    capacity = max(2, 2 * rows // owners)
    code = (cluster_ids * SPAN + priority).reshape(1, rows)
    if capacity != 32 or owners != 16:
        return with_room_for_all(owners, capacity, embeddings, code).reshape(rows)
    tight = capacity // 4 * 3
    slots = owners * tight
    height = width // LANES * SPILL + META
    outgoing, spill, place = call(
        pack_kernel,
        (
            jax.ShapeDtypeStruct((slots, width), jnp.bfloat16),
            jax.ShapeDtypeStruct((1, height, LANES), jnp.bfloat16),
            jax.ShapeDtypeStruct((1, rows), jnp.int32),
        ),
        embeddings, code,
        sizes=(owners, tight, capacity),
    )
    spills = lax.all_gather(spill, "shard", axis=0, tiled=True)
    arrived = exchange(outgoing.reshape(owners, tight, width)).reshape(slots, width)
    maxima, more = call(
        match_kernel,
        (
            jax.ShapeDtypeStruct((owners, 1, 3 * LANES), jnp.float32),
            jax.ShapeDtypeStruct((1, 1), jnp.int32),
        ),
        arrived, spills,
        sizes=(owners, tight, capacity),
        out_specs=(
            pl.BlockSpec(memory_space=pltpu.VMEM), pl.BlockSpec(memory_space=pltpu.SMEM)
        ),
        scratch_shapes=[pltpu.VMEM((owners * SPILL, width), jnp.bfloat16)],
    )
    out = call(
        unpack_kernel, jax.ShapeDtypeStruct((1, rows), jnp.float32), exchange(maxima), place,
        sizes=(owners, tight),
    )
    out = lax.cond(
        more[0, 0] > 0,
        lambda: with_room_for_all(owners, capacity, embeddings, code),
        lambda: out,
    )
    return out.reshape(rows)


def solution(mesh):
    placed = (P(("groups", "shard"), None), P(("groups", "shard")), P(("groups", "shard")))
    return jax.shard_map(
        shards, mesh=mesh, in_specs=placed, out_specs=P(("groups", "shard")), check_vma=False
    )
```

time: 51.8 us -> 57.4 us (1.11)
  blocking collectives: 46.2 us -> 31.2 us
  starting transfers between devices: 0 us -> 12 us
  waiting for transfers between devices: 0 us -> 5.92 us
  Pallas kernels: 2.99 us -> 5.89 us
  local copies, waits for them, and re-layouts: 2.4 us -> 0.56 us
  other arithmetic: 0 us -> 0.7 us
  between operations: 0.01 us -> 0.71 us
    all_to_all x2 -> x0, blocking collectives: 46.2 us -> none  [the longest x1 36.7 us: shards(): lax.all_to_all(outgoing.reshape(owners, capacity, full), 'shard', split_a...]
    all_gather x0 -> x1, blocking collectives: none -> 31.2 us  [shards(): spills = lax.all_gather(spill, 'shard', axis=0, tiled=True)]
    all_to_all x0 -> x2, starting transfers between devices: none -> 12 us  [exchange(): lax.all_to_all(blocks, 'shard', split_axis=0, concat_axis=0, tiled=True)]
    all_to_all x0 -> x2, waiting for transfers between devices: none -> 5.92 us  [exchange(): lax.all_to_all(blocks, 'shard', split_axis=0, concat_axis=0, tiled=True)]
    pallas_call x3, Pallas kernels: 2.99 us -> 5.89 us  [call(): pl.pallas_call(body, out_shape=shapes, compiler_params=pltpu.CompilerPara...]
    unnamed x8 -> x4, local copies, waits for them, and re-layouts: 2.4 us -> 0.56 us
    add x0 -> x1, other arithmetic: none -> 0.7 us  [shards(): code = (cluster_ids * SPAN + priority).reshape(1, rows)]
  transfers between devices with their start and end apart: 0 -> 2, of which waited for: 0 -> 1; matrix products, arithmetic and copies ran while one was open for 0% -> 0% of each run, Pallas kernels for 0% -> 0%
where the time goes in v5:
time: 57.4 us; the launch traced here: 57 us
  blocking collectives  31.2 us (54%)
  starting transfers between devices  12 us (21%)
  waiting for transfers between devices  5.92 us (10%)
  Pallas kernels  5.89 us (10%)
  between operations  0.71 us (1%)
  other arithmetic  0.7 us (1%)
    all_gather x1, blocking collectives, shards(): spills = lax.all_gather(spill, 'shard', axis=0, tiled=True)  31.2 us
    all_to_all x2, starting transfers between devices, exchange(): lax.all_to_all(blocks, 'shard', split_axis=0, concat_axis=0, tiled=True)  12 us
    all_to_all x2, waiting for transfers between devices, exchange(): lax.all_to_all(blocks, 'shard', split_axis=0, concat_axis=0, tiled=True)  5.92 us
    pallas_call x3, Pallas kernels, call(): pl.pallas_call(body, out_shape=shapes, compiler_params=pltpu.CompilerPara...  5.89 us
  transfers between devices with their start and end apart: 2, of which 1 were waited for; matrix products, arithmetic and copies ran while one was open for 0% of the time, Pallas kernels for 0%

profile of v5, /device:TPU:0, one launch (start us, length us, event | category | flops | bytes accessed | tf_op | source)
XLA Modules:
  0.0 57.0 jit_solution(9771568040450277429)
XLA Ops:
  0.0 0.7 %multiply_add_fusion = s32[256]{0:T(256)S(1)} fusion(s32[256]{0:T(256)} %param.7, s32[256]{0:T(256)} %param.6), kind=kLoop, calls=%fused_computation | loop fusion | flops 512 | bytes 3072 | tf_op jit(solution)/shard_map/add | solution.py:256
  0.7 2.7 %shard_map.39 = (bf16[384,1024]{1,0:T(8,128)(2,1)}, bf16[1,144,128]{2,1,0:T(8,128)(2,1)S(1)}, s32[1,256]{1,0:T(1,128)S(1)}) custom-call(bf16[256,1024]{1,0:T(8,128)(2,1)} %refs_0_.1, s32[1,256]{1,0:T(1,128)S(1)} %bitcast.11), custom_call_target="tpu_custom_call" | custom-call | tf_op jit(solution)/shard_map/pallas_call | solution.py:226
  3.4 7.4 %all-to-all-start.2 = ((bf16[16,24,1024]{2,1,0:T(8,128)(2,1)}), bf16[16,24,1024]{2,1,0:T(8,128)(2,1)S(1)}, u32[]{:S(2)}, u32[]{:S(2)}) async-start(bf16[16,24,1024]{2,1,0:T(8,128)(2,1)} %bitcast.5), calls=%async_computation.2 | async-start | bytes 1572864 | tf_op jit(solution)/shard_map/all_to_all | solution.py:235
  10.8 0.0 copy-start
  10.8 31.2 %all_gather.3.refs_1_ = bf16[16,144,128]{2,1,0:T(8,128)(2,1)S(1)} all-gather(bf16[1,144,128]{2,1,0:T(8,128)(2,1)S(1)} %get-tuple-element.25), channel_id=1, replica_groups=mesh['groups'=2,'shard'=16] {'shard'}, dimensions={0}, use_global_device_ids=true | all-gather | bytes 626688 | tf_op jit(solution)/shard_map/all_gather | solution.py:272
  42.1 0.0 all-to-all-done.2
  42.1 2.8 %shard_map.40 = (f32[16,1,384]{2,1,0:T(1,128)}, s32[1,1]{1,0:T(1,128)}) custom-call(bf16[384,1024]{1,0:T(8,128)(2,1)S(1)} %bitcast.9, bf16[16,144,128]{2,1,0:T(8,128)(2,1)S(1)} %all_gather.3.refs_1_), custom_call_target="tpu_custom_call" | custom-call | tf_op jit(solution)/shard_map/pallas_call | solution.py:226
  44.9 4.6 %all-to-all-start.3 = ((f32[16,1,384]{2,1,0:T(1,128)}), f32[16,1,384]{2,1,0:T(1,128)S(1)}, u32[]{:S(2)}, u32[]{:S(2)}) async-start(f32[16,1,384]{2,1,0:T(1,128)} %get-tuple-element.27), calls=%async_computation.3 | async-start | bytes 49152 | tf_op jit(solution)/shard_map/all_to_all | solution.py:235
  50.2 5.9 %all-to-all-done.3.refs_0_ = f32[16,1,384]{2,1,0:T(1,128)S(1)} async-done(((f32[16,1,384]{2,1,0:T(1,128)}), f32[16,1,384]{2,1,0:T(1,128)S(1)}, u32[]{:S(2)}, u32[]{:S(2)}) %all-to-all-start.3) | async-done | bytes 24608 | tf_op jit(solution)/shard_map/all_to_all | solution.py:235
  56.1 0.3 shard_map.41
  56.4 0.0 copy-done
  56.5 0.0 copy-start.1
  56.5 0.6 copy-done.1
  (1 shorter events, 0.0 us)
Async XLA Ops:
  3.4 38.6 %all-to-all-start.2 = ((bf16[16,24,1024]{2,1,0:T(8,128)(2,1)}), bf16[16,24,1024]{2,1,0:T(8,128)(2,1)S(1)}, u32[]{:S(2)}, u32[]{:S(2)}) async-start(bf16[16,24,1024]{2,1,0:T(8,128)(2,1)} %bitcast.5), calls=%async_computation.2 | async-start | bytes 1572864 | tf_op jit(solution)/shard_map/all_to_all | solution.py:235
  10.8 45.6 %copy-start = (bf16[256,1024]{1,0:T(8,128)(2,1)S(1)}, bf16[256,1024]{1,0:T(8,128)(2,1)}, u32[]{:S(2)}) copy-start(bf16[256,1024]{1,0:T(8,128)(2,1)} %refs_0_.1) | copy-start | bytes 1572868
  44.9 11.2 %all-to-all-start.3 = ((f32[16,1,384]{2,1,0:T(1,128)}), f32[16,1,384]{2,1,0:T(1,128)S(1)}, u32[]{:S(2)}, u32[]{:S(2)}) async-start(f32[16,1,384]{2,1,0:T(1,128)} %get-tuple-element.27), calls=%async_computation.3 | async-start | bytes 49152 | tf_op jit(solution)/shard_map/all_to_all | solution.py:235
  56.5 0.6 copy-start.1

commit v6 on v4

--- a/solution.py
+++ b/solution.py
@@ -9,7 +9,7 @@
 LANES = 128
 RADIX = 256
 SPAN = 65536
-META = 16
+META = 8
 
 
 def iota(shape, dim):
@@ -30,20 +30,19 @@
     return jnp.where(mask, 1.0, 0.0).astype(jnp.bfloat16)
 
 
-def pack_kernel(owners, capacity, tall, emb_ref, code_ref, out_ref, place_ref):
-    rows, width = emb_ref.shape
-    slots = owners * capacity
-    earlier = onehots(iota((rows, rows), 0) < iota((rows, rows), 1))
+def place_kernel(owners, capacity, tall, code_ref, place_ref, meta_ref):
+    rows = code_ref.shape[1]
     code = code_ref[...]
     cl = lax.div(code, SPAN)
     rk = lax.rem(code, SPAN)
     owner = lax.div(cl, CL_DEV)
     mine = iota((owners, rows), 0) == owner
+    earlier = onehots(iota((rows, rows), 0) < iota((rows, rows), 1))
     before = matmul(onehots(mine), earlier)
     pos = jnp.sum(jnp.where(mine, before, 0.0), axis=0, keepdims=True).astype(jnp.int32)
     place = owner * capacity + pos
     place_ref[...] = place
-    place = onehots(iota((slots, rows), 0) == place)
+    place = onehots(iota((owners * capacity, rows), 0) == place)
     line = iota((META if tall else LANES, rows), 0)
     meta = jnp.where(
         line == 0,
@@ -51,15 +50,21 @@
         jnp.where(line == 1, lax.div(rk, RADIX), jnp.where(line == 2, lax.rem(rk, RADIX), 0)),
     )
     meta = meta.astype(jnp.float32).astype(jnp.bfloat16)
+    meta_ref[...] = matmul_nt(meta, place) if tall else matmul_nt(place, meta)
+
+
+def pack_kernel(owners, capacity, tall, emb_ref, place_ref, meta_ref, out_ref):
+    rows, width = emb_ref.shape
+    place = onehots(iota((owners * capacity, rows), 0) == place_ref[...])
+    meta = meta_ref[...].astype(jnp.bfloat16)
     wide = emb_ref[...].astype(jnp.float32)
     squares = jnp.sum(wide * wide, axis=1, keepdims=True)
     unit = (wide * lax.rsqrt(squares + 1e-06)).astype(jnp.bfloat16)
     unit = matmul(place, unit).astype(jnp.bfloat16)
     if not tall:
         out_ref[:, :width] = unit
-        out_ref[:, width:] = matmul_nt(place, meta).astype(jnp.bfloat16)
+        out_ref[:, width:] = meta
         return
-    meta = matmul_nt(meta, place).astype(jnp.bfloat16)
     pieces = width // LANES
     for target in range(owners):
         top = target * capacity
@@ -104,13 +109,14 @@
         down = meta.astype(jnp.float32)
         code_down = down[:, 0:1] * SPAN + down[:, 1:2] * RADIX + down[:, 2:3]
     width = units.shape[1] if tall else width
-    best = jnp.full((1, slots), -1.0, jnp.float32)
-    step = min(LANES, slots)
+    step = min(2 * LANES, slots)
+    best = []
     for start in range(0, slots, step):
-        sims = matmul_nt(units[start:start + step, :width], units[:, :width])
-        key = code_down[start:start + step]
-        seen = jnp.where((key >= low) & (key < code), sims, -1.0)
-        best = jnp.maximum(best, jnp.max(seen, axis=0, keepdims=True))
+        stop = start + step
+        sims = matmul_nt(units[:, :width], units[start:stop, :width])
+        seen = (code_down >= low[:, start:stop]) & (code_down < code[:, start:stop])
+        best.append(jnp.max(jnp.where(seen, sims, -1.0), axis=0, keepdims=True))
+    best = jnp.concatenate(best, axis=1)
     for source in range(owners):
         base = source * capacity // LANES * LANES
         out_ref[source] = best[:, base:base + LANES]
@@ -152,6 +158,9 @@
     else:
         packed = (slots, width + LANES)
 
+    def find(*refs):
+        place_kernel(owners, capacity, tall, *refs)
+
     def pack(*refs):
         pack_kernel(owners, capacity, tall, *refs)
 
@@ -161,13 +170,19 @@
     def unpack(*refs):
         unpack_kernel(capacity, *refs)
 
-    outgoing, place = call(
-        pack,
+    place, meta = call(
+        find,
         (
-            jax.ShapeDtypeStruct(packed, jnp.bfloat16),
             jax.ShapeDtypeStruct((1, rows), jnp.int32),
+            jax.ShapeDtypeStruct((META, slots) if tall else (slots, LANES), jnp.float32),
         ),
-        embeddings, (cluster_ids * SPAN + priority).reshape(1, rows),
+        (cluster_ids * SPAN + priority).reshape(1, rows),
+        cost_estimate=pl.CostEstimate(
+            flops=300_000_000, bytes_accessed=100_000, transcendentals=0
+        ),
+    )
+    outgoing = call(
+        pack, jax.ShapeDtypeStruct(packed, jnp.bfloat16), embeddings, place, meta
     )
     arrived = lax.all_to_all(
         outgoing.reshape(owners, -1, packed[-1]), "shard", 0, 0, tiled=True

time: 49.9 us -> 48 us (0.962)
  local copies, waits for them, and re-layouts: 1.04 us -> 0.01 us
  blocking collectives: 44.9 us -> 44.3 us
    unnamed x2, local copies, waits for them, and re-layouts: 1.04 us -> 0.01 us
    all_to_all x1, blocking collectives: 35.7 us -> 35.2 us  [shards(): lax.all_to_all(outgoing.reshape(owners, -1, packed[-1]), 'shard', 0, 0, t...]
    pallas_call x3 -> x4, Pallas kernels: 3 us -> 2.63 us  [call(): pl.pallas_call(kernel, out_shape=shapes, compiler_params=pltpu.CompilerPa...]
where the time goes in v6:
time: 48 us; the launch traced here: 47.7 us
  blocking collectives  44.3 us (92%)
  Pallas kernels  2.63 us (5%)
  other arithmetic  0.76 us (2%)
    all_to_all x1, blocking collectives, shards(): lax.all_to_all(outgoing.reshape(owners, -1, packed[-1]), 'shard', 0, 0, t...  35.2 us
    all_to_all x1, blocking collectives, shards(): returned = lax.all_to_all(maxima, 'shard', 0, 0, tiled=True)  9.16 us
    pallas_call x4, Pallas kernels, call(): pl.pallas_call(kernel, out_shape=shapes, compiler_params=pltpu.CompilerPa...  2.63 us

profile of v6, /device:TPU:0, one launch (start us, length us, event | category | flops | bytes accessed | tf_op | source)
XLA Modules:
  0.0 47.7 jit_solution(14782979655446692513)
XLA Ops:
  0.0 0.0 copy-start
  0.0 0.8 %multiply_add_fusion = s32[256]{0:T(256)S(1)} fusion(s32[256]{0:T(256)} %param.5, s32[256]{0:T(256)} %param.4), kind=kLoop, calls=%fused_computation | loop fusion | flops 512 | bytes 3072 | tf_op jit(solution)/shard_map/add | solution.py:179
  0.8 0.3 shard_map.37
  1.1 0.0 copy-done
  1.1 0.6 %shard_map.38 = bf16[16,264,128]{2,1,0:T(8,128)(2,1)S(1)} custom-call(bf16[256,1024]{1,0:T(8,128)(2,1)S(1)} %copy-done, s32[1,256]{1,0:T(1,128)S(1)} %get-tuple-element.7.refs_1_, f32[8,512]{1,0:T(8,128)S(1)} %get-tuple-element.8.refs_2_), custom_call_target="tpu_custom_call" | custom-call | tf_op jit(solution)/shard_map/pallas_call | solution.py:142
  1.7 35.2 %all_to_all.10.refs_0_ = bf16[16,264,128]{2,1,0:T(8,128)(2,1)S(1)} all-to-all(bf16[16,264,128]{2,1,0:T(8,128)(2,1)S(1)} %shard_map.38), channel_id=1, replica_groups=mesh['groups'=2,'shard'=16] {'shard'}, dimensions={0} | all-to-all | bytes 2162688 | tf_op jit(solution)/shard_map/all_to_all | solution.py:187
  36.9 0.9 %shard_map.39 = f32[16,1,128]{2,1,0:T(1,128)S(1)} custom-call(bf16[16,264,128]{2,1,0:T(8,128)(2,1)S(1)} %all_to_all.10.refs_0_), custom_call_target="tpu_custom_call" | custom-call | tf_op jit(solution)/shard_map/pallas_call | solution.py:142
  37.8 9.2 %all_to_all.11.refs_0_ = f32[16,1,128]{2,1,0:T(1,128)S(1)} all-to-all(f32[16,1,128]{2,1,0:T(1,128)S(1)} %shard_map.39), channel_id=1, replica_groups=mesh['groups'=2,'shard'=16] {'shard'}, dimensions={0} | all-to-all | bytes 16384 | tf_op jit(solution)/shard_map/all_to_all | solution.py:196
  47.0 0.7 %shard_map.40 = f32[1,256]{1,0:T(1,128)} custom-call(f32[16,1,128]{2,1,0:T(1,128)S(1)} %all_to_all.11.refs_0_, s32[1,256]{1,0:T(1,128)S(1)} %get-tuple-element.7.refs_1_), custom_call_target="tpu_custom_call" | custom-call | tf_op jit(solution)/shard_map/pallas_call | solution.py:142
Async XLA Ops:
  0.0 1.1 %copy-start = (bf16[256,1024]{1,0:T(8,128)(2,1)S(1)}, bf16[256,1024]{1,0:T(8,128)(2,1)}, u32[]{:S(2)}) copy-start(bf16[256,1024]{1,0:T(8,128)(2,1)} %refs_0_.1) | copy-start | bytes 1572868

commit v7 on v1

v7 whole, which is shorter than its diff:
```python
import jax
import jax.numpy as jnp
from jax import lax
from jax.experimental import pallas as pl
from jax.experimental.pallas import tpu as pltpu
from jax.sharding import PartitionSpec as P

CL_DEV = 8
LANES = 128
RADIX = 256
SPAN = 65536
META = 8


def iota(shape, dim):
    return lax.broadcasted_iota(jnp.int32, shape, dim)


def matmul_nt(left, right):
    return lax.dot_general(
        left, right, (((1,), (1,)), ((), ())), preferred_element_type=jnp.float32
    )


def matmul(left, right):
    return jnp.dot(left, right, preferred_element_type=jnp.float32)


def onehots(mask):
    return jnp.where(mask, 1.0, 0.0).astype(jnp.bfloat16)


def block_order(owners):
    half = owners // 2
    far = list(range(half, owners))
    near = list(range(half - 1, -1, -1))
    order = far[:2]
    for block in far[2:]:
        order += [block, near.pop(0)]
    return order + near


def place_kernel(owners, capacity, paired, code_ref, place_ref, meta_ref):
    rows = code_ref.shape[1]
    code = code_ref[...]
    cl = lax.div(code, SPAN)
    rk = lax.rem(code, SPAN)
    owner = lax.div(cl, CL_DEV)
    block = owner ^ lax.axis_index("shard") if paired else owner
    mine = iota((owners, rows), 0) == block
    earlier = onehots(iota((rows, rows), 0) < iota((rows, rows), 1))
    before = matmul(onehots(mine), earlier)
    pos = jnp.sum(jnp.where(mine, before, 0.0), axis=0, keepdims=True).astype(jnp.int32)
    place = block * capacity + pos
    place_ref[...] = place
    place = onehots(iota((owners * capacity, rows), 0) == place)
    line = iota((META if paired else LANES, rows), 0)
    meta = jnp.where(
        line == 0,
        cl - owner * CL_DEV + 1,
        jnp.where(line == 1, lax.div(rk, RADIX), jnp.where(line == 2, lax.rem(rk, RADIX), 0)),
    )
    meta = meta.astype(jnp.float32).astype(jnp.bfloat16)
    meta_ref[...] = matmul_nt(meta, place) if paired else matmul_nt(place, meta)


def pack_kernel(owners, capacity, paired, emb_ref, place_ref, meta_ref, *out_refs):
    rows, width = emb_ref.shape
    place = onehots(iota((owners * capacity, rows), 0) == place_ref[...])
    meta = meta_ref[...].astype(jnp.bfloat16)
    wide = emb_ref[...].astype(jnp.float32)
    squares = jnp.sum(wide * wide, axis=1, keepdims=True)
    unit = (wide * lax.rsqrt(squares + 1e-06)).astype(jnp.bfloat16)
    unit = matmul(place, unit).astype(jnp.bfloat16)
    if not paired:
        out_refs[0][:, :width] = unit
        out_refs[0][:, width:] = meta
        return
    pieces = width // LANES
    for block, out_ref in zip(block_order(owners), out_refs):
        top = block * capacity
        for piece in range(pieces):
            out_ref[piece * capacity:(piece + 1) * capacity] = unit[
                top:top + capacity, piece * LANES:(piece + 1) * LANES
            ]
        left = top // LANES * LANES
        out_ref[pieces * capacity:] = meta[:, left:left + LANES]


def maxima(units, code, code_down):
    slots = code.shape[1]
    low = code - lax.rem(code.astype(jnp.int32), SPAN).astype(jnp.float32)
    step = min(2 * LANES, slots)
    best = []
    for start in range(0, slots, step):
        stop = start + step
        sims = matmul_nt(units(0, slots), units(start, stop))
        seen = (code_down >= low[:, start:stop]) & (code_down < code[:, start:stop])
        best.append(jnp.max(jnp.where(seen, sims, -1.0), axis=0, keepdims=True))
    return jnp.concatenate(best, axis=1)


def match_paired_kernel(owners, capacity, *refs):
    *in_refs, out_ref, rows_ref = refs
    in_refs = dict(zip(block_order(owners), in_refs))
    slots, width = rows_ref.shape
    pieces = width // LANES
    for block, in_ref in in_refs.items():
        top = block * capacity
        for piece in range(pieces):
            rows_ref[top:top + capacity, piece * LANES:(piece + 1) * LANES] = in_ref[
                piece * capacity:(piece + 1) * capacity
            ]
    each = LANES // capacity
    part = lax.div(iota((META, LANES), 1), capacity)
    code = []
    for first in range(0, owners, each):
        meta = jnp.zeros((META, LANES), jnp.float32)
        for number in range(each):
            lines = in_refs[first + number][pieces * capacity:].astype(jnp.float32)
            meta = jnp.where(part == number, lines, meta)
        code.append(meta[0:1] * SPAN + meta[1:2] * RADIX + meta[2:3])
    code = jnp.concatenate(code, axis=1)
    code_down = jnp.broadcast_to(code, (8, slots)).T[:, 0:1]
    best = maxima(lambda start, stop: rows_ref[start:stop], code, code_down)
    me = lax.axis_index("shard")
    for block in range(owners):
        base = block * capacity // LANES * LANES
        out_ref[me ^ block] = best[:, base:base + LANES]


def match_kernel(owners, capacity, in_ref, out_ref):
    width = in_ref.shape[1] - LANES
    meta = in_ref[:, width:]
    pick = onehots(iota((8, LANES), 0) == iota((8, LANES), 1))
    across = matmul_nt(pick, meta)
    code = across[0:1] * SPAN + across[1:2] * RADIX + across[2:3]
    down = meta.astype(jnp.float32)
    code_down = down[:, 0:1] * SPAN + down[:, 1:2] * RADIX + down[:, 2:3]
    best = maxima(lambda start, stop: in_ref[start:stop, :width], code, code_down)
    for source in range(owners):
        base = source * capacity // LANES * LANES
        out_ref[source] = best[:, base:base + LANES]


def unpack_kernel(capacity, paired, got_ref, place_ref, out_ref):
    owners = got_ref.shape[0]
    rows = place_ref.shape[1]
    me = lax.axis_index("shard")
    place = place_ref[...]
    owner = lax.div(place, capacity)
    if paired:
        owner = owner ^ me
        lane = lax.rem(place, LANES)
    else:
        lane = lax.rem(place, capacity) + lax.rem(me * capacity, LANES)
    got = got_ref[:, 0, :]
    high = got.astype(jnp.bfloat16)
    rest = got - high.astype(jnp.float32)
    middle = rest.astype(jnp.bfloat16)
    last = (rest - middle.astype(jnp.float32)).astype(jnp.bfloat16)
    pick = onehots(iota((LANES, rows), 0) == lane)
    found = matmul(high, pick) + matmul(middle, pick) + matmul(last, pick)
    mine = iota((owners, rows), 0) == owner
    out_ref[...] = jnp.sum(jnp.where(mine, found, 0.0), axis=0, keepdims=True)


def call(kernel, sizes, shapes, *args, **kwargs):
    def body(*refs):
        kernel(*sizes, *refs)

    return pl.pallas_call(
        body,
        out_shape=shapes,
        compiler_params=pltpu.CompilerParams(vmem_limit_bytes=32 * 2**20),
        **kwargs,
    )(*args)


def swap(blocks):
    owners = len(blocks)
    return [
        lax.ppermute(block, "shard", [(d, d ^ k) for d in range(owners)]) if k else block
        for k, block in zip(block_order(owners), blocks)
    ]


def shards(embeddings, cluster_ids, priority):
    rows, width = embeddings.shape
    owners = lax.axis_size("shard")
    capacity = max(2, 2 * rows // owners)
    slots = owners * capacity
    paired = owners == 16 and capacity % 16 == 0 and LANES % capacity == 0
    sizes = (owners, capacity, paired)
    place, meta = call(
        place_kernel,
        sizes,
        (
            jax.ShapeDtypeStruct((1, rows), jnp.int32),
            jax.ShapeDtypeStruct((META, slots) if paired else (slots, LANES), jnp.float32),
        ),
        (cluster_ids * SPAN + priority).reshape(1, rows),
        cost_estimate=pl.CostEstimate(
            flops=300_000_000, bytes_accessed=100_000, transcendentals=0
        ),
    )
    found = jax.ShapeDtypeStruct((owners, 1, LANES), jnp.float32)
    if paired:
        block = jax.ShapeDtypeStruct((width // LANES * capacity + META, LANES), jnp.bfloat16)
        outgoing = call(pack_kernel, sizes, [block] * owners, embeddings, place, meta)
        best = call(
            match_paired_kernel,
            (owners, capacity),
            found,
            *swap(outgoing),
            scratch_shapes=[pltpu.VMEM((slots, width), jnp.bfloat16)],
        )
    else:
        full = width + LANES
        packed = jax.ShapeDtypeStruct((slots, full), jnp.bfloat16)
        (outgoing,) = call(pack_kernel, sizes, [packed], embeddings, place, meta)
        arrived = lax.all_to_all(
            outgoing.reshape(owners, capacity, full), "shard", 0, 0, tiled=True
        ).reshape(slots, full)
        best = call(match_kernel, (owners, capacity), found, arrived)
    returned = lax.all_to_all(best, "shard", 0, 0, tiled=True)
    out = call(
        unpack_kernel,
        (capacity, paired),
        jax.ShapeDtypeStruct((1, rows), jnp.float32),
        returned,
        place,
    )
    return out.reshape(rows)


def solution(mesh):
    placed = (P(("groups", "shard"), None), P(("groups", "shard")), P(("groups", "shard")))
    return jax.shard_map(
        shards, mesh=mesh, in_specs=placed, out_specs=P(("groups", "shard")), check_vma=False
    )
```

time: 51.8 us -> 45.8 us (0.88)
  blocking collectives: 46.2 us -> 10.5 us
  starting transfers between devices: 0 us -> 26.6 us
  waiting for transfers between devices: 0 us -> 4.53 us
  local copies, waits for them, and re-layouts: 2.4 us -> 0.71 us
  other arithmetic: 0 us -> 0.7 us
    all_to_all x2 -> x1, blocking collectives: 46.2 us -> 10.5 us  [shards(): returned = lax.all_to_all(best, 'shard', 0, 0, tiled=True)]
    ppermute x0 -> x15, starting transfers between devices: none -> 26.6 us  [swap(): lax.ppermute(block, 'shard', [(d, d ^ k) for d in range(owners)])]
    ppermute x0 -> x15, waiting for transfers between devices: none -> 4.53 us  [swap(): lax.ppermute(block, 'shard', [(d, d ^ k) for d in range(owners)])]
    unnamed x8 -> x2, local copies, waits for them, and re-layouts: 2.4 us -> 0.71 us
    add x0 -> x1, other arithmetic: none -> 0.7 us  [shards(): cluster_ids * SPAN + priority]
    pallas_call x3 -> x4, Pallas kernels: 2.99 us -> 2.53 us  [call(): pl.pallas_call(body, out_shape=shapes, compiler_params=pltpu.CompilerPara...]
  transfers between devices with their start and end apart: 0 -> 15, of which waited for: 0 -> 5; matrix products, arithmetic and copies ran while one was open for 0% -> 0% of each run, Pallas kernels for 0% -> 0%
where the time goes in v7:
time: 45.8 us; the launch traced here: 45.6 us
  starting transfers between devices  26.6 us (58%)
  blocking collectives  10.5 us (23%)
  waiting for transfers between devices  4.53 us (10%)
  Pallas kernels  2.53 us (6%)
  local copies, waits for them, and re-layouts  0.71 us (2%)
  other arithmetic  0.7 us (2%)
    ppermute x15, starting transfers between devices, swap(): lax.ppermute(block, 'shard', [(d, d ^ k) for d in range(owners)])  26.6 us
    all_to_all x1, blocking collectives, shards(): returned = lax.all_to_all(best, 'shard', 0, 0, tiled=True)  10.5 us
    ppermute x15, waiting for transfers between devices, swap(): lax.ppermute(block, 'shard', [(d, d ^ k) for d in range(owners)])  4.53 us
    pallas_call x4, Pallas kernels, call(): pl.pallas_call(body, out_shape=shapes, compiler_params=pltpu.CompilerPara...  2.53 us
  transfers between devices with their start and end apart: 15, of which 5 were waited for; matrix products, arithmetic and copies ran while one was open for 0% of the time, Pallas kernels for 0%

profile of v7, /device:TPU:0, one launch (start us, length us, event | category | flops | bytes accessed | tf_op | source)
XLA Modules:
  0.0 45.6 jit_solution(899656628625559843)
XLA Ops:
  0.0 0.7 %multiply_add_fusion = s32[256]{0:T(256)S(1)} fusion(s32[256]{0:T(256)} %param.5, s32[256]{0:T(256)} %param.4), kind=kLoop, calls=%fused_computation | loop fusion | flops 512 | bytes 3072 | tf_op jit(solution)/shard_map/add | solution.py:202
  0.7 0.0 copy-start
  0.7 0.3 shard_map.37
  1.0 0.7 %copy-done = bf16[256,1024]{1,0:T(8,128)(2,1)S(1)} copy-done((bf16[256,1024]{1,0:T(8,128)(2,1)S(1)}, bf16[256,1024]{1,0:T(8,128)(2,1)}, u32[]{:S(2)}) %copy-start) | copy-done | bytes 524312
  1.7 0.6 %shard_map.38 = (bf16[264,128]{1,0:T(8,128)(2,1)S(1)}, bf16[264,128]{1,0:T(8,128)(2,1)S(1)}, bf16[264,128]{1,0:T(8,128)(2,1)S(1)}, bf16[264,128]{1,0:T(8,128)(2,...) custom-call(bf16[256,1024]{1,0:T(8,128)(2,1)S(1)} %copy-done, ...), custom_call_target="tpu_custom_call" | custom-call | tf_op jit(solution)/shard_map/pallas_call | solution.py:172
  2.3 4.1 %collective-permute-start = (bf16[264,128]{1,0:T(8,128)(2,1)S(1)}, bf16[264,128]{1,0:T(8,128)(2,1)S(1)}, u32[]{:S(2)}, u32[]{:S(2)}) collective-permute-start(bf16[264,128]{1,0:T(8,128)(2,1)S(1)} %get-tuple-element.25), channel_id=1, source_target_pairs={{0,8},{1,9},{2,10},{3,11},{4,12},{5,13},{6,14},{7,15},{8,0},{9,1},... | collective-permute-start | bytes 202760 | tf_op jit(solution)/shard_map/ppermute | solution.py:183
  6.4 0.0 collective-permute-start.1
  6.4 3.0 %collective-permute-start.2 = (bf16[264,128]{1,0:T(8,128)(2,1)S(1)}, bf16[264,128]{1,0:T(8,128)(2,1)S(1)}, u32[]{:S(2)}, u32[]{:S(2)}) collective-permute-start(bf16[264,128]{1,0:T(8,128)(2,1)S(1)} %get-tuple-element.27), channel_id=1, source_target_pairs={{0,10},{1,11},{2,8},{3,9},{4,14},{5,15},{6,12},{7,13},{8,2},{9,3},... | collective-permute-start | bytes 202760 | tf_op jit(solution)/shard_map/ppermute | solution.py:183
  9.5 1.8 %collective-permute-start.3 = (bf16[264,128]{1,0:T(8,128)(2,1)S(1)}, bf16[264,128]{1,0:T(8,128)(2,1)S(1)}, u32[]{:S(2)}, u32[]{:S(2)}) collective-permute-start(bf16[264,128]{1,0:T(8,128)(2,1)S(1)} %get-tuple-element.28), channel_id=1, source_target_pairs={{0,7},{1,6},{2,5},{3,4},{4,3},{5,2},{6,1},{7,0},{8,15},{9,14},{10,... | collective-permute-start | bytes 202760 | tf_op jit(solution)/shard_map/ppermute | solution.py:183
  11.3 1.2 %collective-permute-start.4 = (bf16[264,128]{1,0:T(8,128)(2,1)S(1)}, bf16[264,128]{1,0:T(8,128)(2,1)S(1)}, u32[]{:S(2)}, u32[]{:S(2)}) collective-permute-start(bf16[264,128]{1,0:T(8,128)(2,1)S(1)} %get-tuple-element.29), channel_id=1, source_target_pairs={{0,11},{1,10},{2,9},{3,8},{4,15},{5,14},{6,13},{7,12},{8,3},{9,2},... | collective-permute-start | bytes 202760 | tf_op jit(solution)/shard_map/ppermute | solution.py:183
  12.5 0.0 collective-permute-done.refs_0_
  12.5 2.3 %collective-permute-start.5 = (bf16[264,128]{1,0:T(8,128)(2,1)S(1)}, bf16[264,128]{1,0:T(8,128)(2,1)S(1)}, u32[]{:S(2)}, u32[]{:S(2)}) collective-permute-start(bf16[264,128]{1,0:T(8,128)(2,1)S(1)} %get-tuple-element.30), channel_id=1, source_target_pairs={{0,6},{1,7},{2,4},{3,5},{4,2},{5,3},{6,0},{7,1},{8,14},{9,15},{10,... | collective-permute-start | bytes 202760 | tf_op jit(solution)/shard_map/ppermute | solution.py:183
  14.9 0.0 collective-permute-done.1.refs_1_
  14.9 3.3 %collective-permute-start.6 = (bf16[264,128]{1,0:T(8,128)(2,1)S(1)}, bf16[264,128]{1,0:T(8,128)(2,1)S(1)}, u32[]{:S(2)}, u32[]{:S(2)}) collective-permute-start(bf16[264,128]{1,0:T(8,128)(2,1)S(1)} %get-tuple-element.31), channel_id=1, source_target_pairs={{0,12},{1,13},{2,14},{3,15},{4,8},{5,9},{6,10},{7,11},{8,4},{9,5},... | collective-permute-start | bytes 202760 | tf_op jit(solution)/shard_map/ppermute | solution.py:183
  18.2 0.3 collective-permute-done.2.refs_2_
  18.5 0.0 collective-permute-start.7
  18.5 0.0 collective-permute-done.3.refs_3_
  18.5 2.8 %collective-permute-start.8 = (bf16[264,128]{1,0:T(8,128)(2,1)S(1)}, bf16[264,128]{1,0:T(8,128)(2,1)S(1)}, u32[]{:S(2)}, u32[]{:S(2)}) collective-permute-start(bf16[264,128]{1,0:T(8,128)(2,1)S(1)} %get-tuple-element.33), channel_id=1, source_target_pairs={{0,13},{1,12},{2,15},{3,14},{4,9},{5,8},{6,11},{7,10},{8,5},{9,4},... | collective-permute-start | bytes 202760 | tf_op jit(solution)/shard_map/ppermute | solution.py:183
  21.4 0.0 collective-permute-done.4.refs_4_
  21.4 1.5 %collective-permute-start.9 = (bf16[264,128]{1,0:T(8,128)(2,1)S(1)}, bf16[264,128]{1,0:T(8,128)(2,1)S(1)}, u32[]{:S(2)}, u32[]{:S(2)}) collective-permute-start(bf16[264,128]{1,0:T(8,128)(2,1)S(1)} %get-tuple-element.34), channel_id=1, source_target_pairs={{0,4},{1,5},{2,6},{3,7},{4,0},{5,1},{6,2},{7,3},{8,12},{9,13},{10,... | collective-permute-start | bytes 202760 | tf_op jit(solution)/shard_map/ppermute | solution.py:183
  22.8 0.0 collective-permute-done.5.refs_5_
  22.8 3.2 %collective-permute-start.10 = (bf16[264,128]{1,0:T(8,128)(2,1)S(1)}, bf16[264,128]{1,0:T(8,128)(2,1)S(1)}, u32[]{:S(2)}, u32[]{:S(2)}) collective-permute-start(bf16[264,128]{1,0:T(8,128)(2,1)S(1)} %get-tuple-element.35), channel_id=1, source_target_pairs={{0,14},{1,15},{2,12},{3,13},{4,10},{5,11},{6,8},{7,9},{8,6},{9,7},... | collective-permute-start | bytes 202760 | tf_op jit(solution)/shard_map/ppermute | solution.py:183
  26.0 0.0 collective-permute-done.6.refs_6_
  26.0 0.0 collective-permute-start.11
  26.0 0.0 collective-permute-done.7.refs_7_
  26.1 1.7 %collective-permute-start.12 = (bf16[264,128]{1,0:T(8,128)(2,1)S(1)}, bf16[264,128]{1,0:T(8,128)(2,1)S(1)}, u32[]{:S(2)}, u32[]{:S(2)}) collective-permute-start(bf16[264,128]{1,0:T(8,128)(2,1)S(1)} %get-tuple-element.37), channel_id=1, source_target_pairs={{0,15},{1,14},{2,13},{3,12},{4,11},{5,10},{6,9},{7,8},{8,7},{9,6},... | collective-permute-start | bytes 202760 | tf_op jit(solution)/shard_map/ppermute | solution.py:183
  27.8 0.0 collective-permute-done.8.refs_8_
  27.8 1.5 %collective-permute-start.13 = (bf16[264,128]{1,0:T(8,128)(2,1)S(1)}, bf16[264,128]{1,0:T(8,128)(2,1)S(1)}, u32[]{:S(2)}, u32[]{:S(2)}) collective-permute-start(bf16[264,128]{1,0:T(8,128)(2,1)S(1)} %get-tuple-element.38), channel_id=1, source_target_pairs={{0,2},{1,3},{2,0},{3,1},{4,6},{5,7},{6,4},{7,5},{8,10},{9,11},{10,... | collective-permute-start | bytes 202760 | tf_op jit(solution)/shard_map/ppermute | solution.py:183
  29.3 0.0 collective-permute-done.9.refs_9_
  29.3 0.0 collective-permute-start.14
  29.3 0.7 %collective-permute-done.10.refs_10_ = bf16[264,128]{1,0:T(8,128)(2,1)S(1)} collective-permute-done((bf16[264,128]{1,0:T(8,128)(2,1)S(1)}, bf16[264,128]{1,0:T(8,128)(2,1)S(1)}, u32[]{:S(2)}, u32[]{:S(2)}) %collective-permute-start.10) | collective-permute-done | bytes 67616 | tf_op jit(solution)/shard_map/ppermute | solution.py:183
  30.0 0.6 %collective-permute-done.11.refs_11_ = bf16[264,128]{1,0:T(8,128)(2,1)S(1)} collective-permute-done((bf16[264,128]{1,0:T(8,128)(2,1)S(1)}, bf16[264,128]{1,0:T(8,128)(2,1)S(1)}, u32[]{:S(2)}, u32[]{:S(2)}) %collective-permute-start.11) | collective-permute-done | bytes 67616 | tf_op jit(solution)/shard_map/ppermute | solution.py:183
  30.6 2.5 %collective-permute-done.12.refs_12_ = bf16[264,128]{1,0:T(8,128)(2,1)S(1)} collective-permute-done((bf16[264,128]{1,0:T(8,128)(2,1)S(1)}, bf16[264,128]{1,0:T(8,128)(2,1)S(1)}, u32[]{:S(2)}, u32[]{:S(2)}) %collective-permute-start.12) | collective-permute-done | bytes 67616 | tf_op jit(solution)/shard_map/ppermute | solution.py:183
  33.0 0.5 %collective-permute-done.13.refs_13_ = bf16[264,128]{1,0:T(8,128)(2,1)S(1)} collective-permute-done((bf16[264,128]{1,0:T(8,128)(2,1)S(1)}, bf16[264,128]{1,0:T(8,128)(2,1)S(1)}, u32[]{:S(2)}, u32[]{:S(2)}) %collective-permute-start.13) | collective-permute-done | bytes 67616 | tf_op jit(solution)/shard_map/ppermute | solution.py:183
  33.5 0.0 collective-permute-done.14.refs_14_
  33.5 0.9 %shard_map.39 = f32[16,1,128]{2,1,0:T(1,128)S(1)} custom-call(bf16[264,128]{1,0:T(8,128)(2,1)S(1)} %collective-permute-done.refs_0_, bf16[264,128]{1,0:T(8,128)(2,1)S(1)} %collective-permute-done.1.refs_1_, bf16[264,128]{1,0:T(8,128)(2,1)S(1)} %collective-permute-done.2.refs_2_, bf16[264,128]{1,0:T(8,128)(2,1)S(1)} %collective-permute-done.3.refs_3_, ...), custom_call_target="tpu_custom_call" | custom-call | tf_op jit(solution)/shard_map/pallas_call | solution.py:172
  34.4 10.5 %all_to_all.5.refs_0_ = f32[16,1,128]{2,1,0:T(1,128)S(1)} all-to-all(f32[16,1,128]{2,1,0:T(1,128)S(1)} %shard_map.39), channel_id=1, replica_groups=mesh['groups'=2,'shard'=16] {'shard'}, dimensions={0} | all-to-all | bytes 16384 | tf_op jit(solution)/shard_map/all_to_all | solution.py:226
  44.9 0.7 %shard_map.40 = f32[1,256]{1,0:T(1,128)} custom-call(f32[16,1,128]{2,1,0:T(1,128)S(1)} %all_to_all.5.refs_0_, s32[1,256]{1,0:T(1,128)S(1)} %get-tuple-element.23.refs_1_), custom_call_target="tpu_custom_call" | custom-call | tf_op jit(solution)/shard_map/pallas_call | solution.py:172
Async XLA Ops:
  0.7 1.0 %copy-start = (bf16[256,1024]{1,0:T(8,128)(2,1)S(1)}, bf16[256,1024]{1,0:T(8,128)(2,1)}, u32[]{:S(2)}) copy-start(bf16[256,1024]{1,0:T(8,128)(2,1)} %refs_0_.1) | copy-start | bytes 1572868
  2.3 10.2 %collective-permute-start = (bf16[264,128]{1,0:T(8,128)(2,1)S(1)}, bf16[264,128]{1,0:T(8,128)(2,1)S(1)}, u32[]{:S(2)}, u32[]{:S(2)}) collective-permute-start(bf16[264,128]{1,0:T(8,128)(2,1)S(1)} %get-tuple-element.25), channel_id=1, source_target_pairs={{0,8},{1,9},{2,10},{3,11},{4,12},{5,13},{6,14},{7,15},{8,0},{9,1},... | collective-permute-start | bytes 202760 | tf_op jit(solution)/shard_map/ppermute | solution.py:183
  6.4 8.4 %collective-permute-start.1 = (bf16[264,128]{1,0:T(8,128)(2,1)S(1)}, bf16[264,128]{1,0:T(8,128)(2,1)S(1)}, u32[]{:S(2)}, u32[]{:S(2)}) collective-permute-start(bf16[264,128]{1,0:T(8,128)(2,1)S(1)} %get-tuple-element.26), channel_id=1, source_target_pairs={{0,9},{1,8},{2,11},{3,10},{4,13},{5,12},{6,15},{7,14},{8,1},{9,0},... | collective-permute-start | bytes 202760 | tf_op jit(solution)/shard_map/ppermute | solution.py:183
  6.4 12.1 %collective-permute-start.2 = (bf16[264,128]{1,0:T(8,128)(2,1)S(1)}, bf16[264,128]{1,0:T(8,128)(2,1)S(1)}, u32[]{:S(2)}, u32[]{:S(2)}) collective-permute-start(bf16[264,128]{1,0:T(8,128)(2,1)S(1)} %get-tuple-element.27), channel_id=1, source_target_pairs={{0,10},{1,11},{2,8},{3,9},{4,14},{5,15},{6,12},{7,13},{8,2},{9,3},... | collective-permute-start | bytes 202760 | tf_op jit(solution)/shard_map/ppermute | solution.py:183
  9.5 9.1 %collective-permute-start.3 = (bf16[264,128]{1,0:T(8,128)(2,1)S(1)}, bf16[264,128]{1,0:T(8,128)(2,1)S(1)}, u32[]{:S(2)}, u32[]{:S(2)}) collective-permute-start(bf16[264,128]{1,0:T(8,128)(2,1)S(1)} %get-tuple-element.28), channel_id=1, source_target_pairs={{0,7},{1,6},{2,5},{3,4},{4,3},{5,2},{6,1},{7,0},{8,15},{9,14},{10,... | collective-permute-start | bytes 202760 | tf_op jit(solution)/shard_map/ppermute | solution.py:183
  11.3 10.1 %collective-permute-start.4 = (bf16[264,128]{1,0:T(8,128)(2,1)S(1)}, bf16[264,128]{1,0:T(8,128)(2,1)S(1)}, u32[]{:S(2)}, u32[]{:S(2)}) collective-permute-start(bf16[264,128]{1,0:T(8,128)(2,1)S(1)} %get-tuple-element.29), channel_id=1, source_target_pairs={{0,11},{1,10},{2,9},{3,8},{4,15},{5,14},{6,13},{7,12},{8,3},{9,2},... | collective-permute-start | bytes 202760 | tf_op jit(solution)/shard_map/ppermute | solution.py:183
  12.5 10.3 %collective-permute-start.5 = (bf16[264,128]{1,0:T(8,128)(2,1)S(1)}, bf16[264,128]{1,0:T(8,128)(2,1)S(1)}, u32[]{:S(2)}, u32[]{:S(2)}) collective-permute-start(bf16[264,128]{1,0:T(8,128)(2,1)S(1)} %get-tuple-element.30), channel_id=1, source_target_pairs={{0,6},{1,7},{2,4},{3,5},{4,2},{5,3},{6,0},{7,1},{8,14},{9,15},{10,... | collective-permute-start | bytes 202760 | tf_op jit(solution)/shard_map/ppermute | solution.py:183
  14.9 11.2 %collective-permute-start.6 = (bf16[264,128]{1,0:T(8,128)(2,1)S(1)}, bf16[264,128]{1,0:T(8,128)(2,1)S(1)}, u32[]{:S(2)}, u32[]{:S(2)}) collective-permute-start(bf16[264,128]{1,0:T(8,128)(2,1)S(1)} %get-tuple-element.31), channel_id=1, source_target_pairs={{0,12},{1,13},{2,14},{3,15},{4,8},{5,9},{6,10},{7,11},{8,4},{9,5},... | collective-permute-start | bytes 202760 | tf_op jit(solution)/shard_map/ppermute | solution.py:183
  18.5 7.5 %collective-permute-start.7 = (bf16[264,128]{1,0:T(8,128)(2,1)S(1)}, bf16[264,128]{1,0:T(8,128)(2,1)S(1)}, u32[]{:S(2)}, u32[]{:S(2)}) collective-permute-start(bf16[264,128]{1,0:T(8,128)(2,1)S(1)} %get-tuple-element.32), channel_id=1, source_target_pairs={{0,5},{1,4},{2,7},{3,6},{4,1},{5,0},{6,3},{7,2},{8,13},{9,12},{10,... | collective-permute-start | bytes 202760 | tf_op jit(solution)/shard_map/ppermute | solution.py:183
  18.5 9.2 %collective-permute-start.8 = (bf16[264,128]{1,0:T(8,128)(2,1)S(1)}, bf16[264,128]{1,0:T(8,128)(2,1)S(1)}, u32[]{:S(2)}, u32[]{:S(2)}) collective-permute-start(bf16[264,128]{1,0:T(8,128)(2,1)S(1)} %get-tuple-element.33), channel_id=1, source_target_pairs={{0,13},{1,12},{2,15},{3,14},{4,9},{5,8},{6,11},{7,10},{8,5},{9,4},... | collective-permute-start | bytes 202760 | tf_op jit(solution)/shard_map/ppermute | solution.py:183
  21.4 8.0 %collective-permute-start.9 = (bf16[264,128]{1,0:T(8,128)(2,1)S(1)}, bf16[264,128]{1,0:T(8,128)(2,1)S(1)}, u32[]{:S(2)}, u32[]{:S(2)}) collective-permute-start(bf16[264,128]{1,0:T(8,128)(2,1)S(1)} %get-tuple-element.34), channel_id=1, source_target_pairs={{0,4},{1,5},{2,6},{3,7},{4,0},{5,1},{6,2},{7,3},{8,12},{9,13},{10,... | collective-permute-start | bytes 202760 | tf_op jit(solution)/shard_map/ppermute | solution.py:183
  22.8 7.1 %collective-permute-start.10 = (bf16[264,128]{1,0:T(8,128)(2,1)S(1)}, bf16[264,128]{1,0:T(8,128)(2,1)S(1)}, u32[]{:S(2)}, u32[]{:S(2)}) collective-permute-start(bf16[264,128]{1,0:T(8,128)(2,1)S(1)} %get-tuple-element.35), channel_id=1, source_target_pairs={{0,14},{1,15},{2,12},{3,13},{4,10},{5,11},{6,8},{7,9},{8,6},{9,7},... | collective-permute-start | bytes 202760 | tf_op jit(solution)/shard_map/ppermute | solution.py:183
  26.0 4.5 %collective-permute-start.11 = (bf16[264,128]{1,0:T(8,128)(2,1)S(1)}, bf16[264,128]{1,0:T(8,128)(2,1)S(1)}, u32[]{:S(2)}, u32[]{:S(2)}) collective-permute-start(bf16[264,128]{1,0:T(8,128)(2,1)S(1)} %get-tuple-element.36), channel_id=1, source_target_pairs={{0,3},{1,2},{2,1},{3,0},{4,7},{5,6},{6,5},{7,4},{8,11},{9,10},{10,... | collective-permute-start | bytes 202760 | tf_op jit(solution)/shard_map/ppermute | solution.py:183
  26.1 7.0 %collective-permute-start.12 = (bf16[264,128]{1,0:T(8,128)(2,1)S(1)}, bf16[264,128]{1,0:T(8,128)(2,1)S(1)}, u32[]{:S(2)}, u32[]{:S(2)}) collective-permute-start(bf16[264,128]{1,0:T(8,128)(2,1)S(1)} %get-tuple-element.37), channel_id=1, source_target_pairs={{0,15},{1,14},{2,13},{3,12},{4,11},{5,10},{6,9},{7,8},{8,7},{9,6},... | collective-permute-start | bytes 202760 | tf_op jit(solution)/shard_map/ppermute | solution.py:183
  27.8 5.7 %collective-permute-start.13 = (bf16[264,128]{1,0:T(8,128)(2,1)S(1)}, bf16[264,128]{1,0:T(8,128)(2,1)S(1)}, u32[]{:S(2)}, u32[]{:S(2)}) collective-permute-start(bf16[264,128]{1,0:T(8,128)(2,1)S(1)} %get-tuple-element.38), channel_id=1, source_target_pairs={{0,2},{1,3},{2,0},{3,1},{4,6},{5,7},{6,4},{7,5},{8,10},{9,11},{10,... | collective-permute-start | bytes 202760 | tf_op jit(solution)/shard_map/ppermute | solution.py:183
  29.3 4.2 %collective-permute-start.14 = (bf16[264,128]{1,0:T(8,128)(2,1)S(1)}, bf16[264,128]{1,0:T(8,128)(2,1)S(1)}, u32[]{:S(2)}, u32[]{:S(2)}) collective-permute-start(bf16[264,128]{1,0:T(8,128)(2,1)S(1)} %get-tuple-element.39), channel_id=1, source_target_pairs={{0,1},{1,0},{2,3},{3,2},{4,5},{5,4},{6,7},{7,6},{8,9},{9,8},{10,11... | collective-permute-start | bytes 202760 | tf_op jit(solution)/shard_map/ppermute | solution.py:183

commit v8 on v7

--- a/solution.py
+++ b/solution.py
@@ -30,14 +30,20 @@
     return jnp.where(mask, 1.0, 0.0).astype(jnp.bfloat16)
 
 
-def block_order(owners):
+def pair_order(owners):
     half = owners // 2
-    far = list(range(half, owners))
-    near = list(range(half - 1, -1, -1))
-    order = far[:2]
-    for block in far[2:]:
-        order += [block, near.pop(0)]
-    return order + near
+    return list(range(half, owners, 2)) + list(range(0, half, 2))
+
+
+def swap_steps(owners):
+    return [
+        (8, None), (10, None), (2, None), (4, None), (12, None),
+        (9, 8), (6, 2), (14, 9), (3, 4), (11, 10), (5, 3), (7, 6), (1, 11), (13, 12), (15, 14),
+    ]
+
+
+def swapped_order(owners):
+    return [block for block, _ in swap_steps(owners)] + [0]
 
 
 def place_kernel(owners, capacity, paired, code_ref, place_ref, meta_ref):
@@ -77,14 +83,15 @@
         out_refs[0][:, width:] = meta
         return
     pieces = width // LANES
-    for block, out_ref in zip(block_order(owners), out_refs):
-        top = block * capacity
-        for piece in range(pieces):
+    for first, out_ref in zip(pair_order(owners), out_refs):
+        for piece in range(2 * pieces):
+            top = (first + piece // pieces) * capacity
+            left = piece % pieces * LANES
             out_ref[piece * capacity:(piece + 1) * capacity] = unit[
-                top:top + capacity, piece * LANES:(piece + 1) * LANES
+                top:top + capacity, left:left + LANES
             ]
-        left = top // LANES * LANES
-        out_ref[pieces * capacity:] = meta[:, left:left + LANES]
+        left = first * capacity // LANES * LANES
+        out_ref[2 * pieces * capacity:] = meta[:, left:left + LANES]
 
 
 def maxima(units, code, code_down):
@@ -102,14 +109,16 @@
 
 def match_paired_kernel(owners, capacity, *refs):
     *in_refs, out_ref, rows_ref = refs
-    in_refs = dict(zip(block_order(owners), in_refs))
+    in_refs = dict(zip(swapped_order(owners), in_refs))
     slots, width = rows_ref.shape
     pieces = width // LANES
     for block, in_ref in in_refs.items():
         top = block * capacity
+        base = block % 2 * pieces
         for piece in range(pieces):
+            start = (base + piece) * capacity
             rows_ref[top:top + capacity, piece * LANES:(piece + 1) * LANES] = in_ref[
-                piece * capacity:(piece + 1) * capacity
+                start:start + capacity
             ]
     each = LANES // capacity
     part = lax.div(iota((META, LANES), 1), capacity)
@@ -117,7 +126,7 @@
     for first in range(0, owners, each):
         meta = jnp.zeros((META, LANES), jnp.float32)
         for number in range(each):
-            lines = in_refs[first + number][pieces * capacity:].astype(jnp.float32)
+            lines = in_refs[first + number][2 * pieces * capacity:].astype(jnp.float32)
             meta = jnp.where(part == number, lines, meta)
         code.append(meta[0:1] * SPAN + meta[1:2] * RADIX + meta[2:3])
     code = jnp.concatenate(code, axis=1)
@@ -177,12 +186,24 @@
     )(*args)
 
 
-def swap(blocks):
-    owners = len(blocks)
-    return [
-        lax.ppermute(block, "shard", [(d, d ^ k) for d in range(owners)]) if k else block
-        for k, block in zip(block_order(owners), blocks)
-    ]
+def swap(pairs, owners):
+    got = dict(zip(pair_order(owners), pairs))
+    sent = dict(got)
+
+    def across(pair, k):
+        return lax.ppermute(pair, "shard", [(d, d ^ k) for d in range(owners)])
+
+    def after(value, other):
+        return lax.optimization_barrier((value, other))
+
+    for step in swap_steps(owners):
+        block, wait = step
+        first = block - block % 2
+        pair = got[first] if block % 2 else sent[first]
+        if wait is not None:
+            pair, got[wait] = after(pair, got[wait])
+        got[block] = across(pair, 1 if block % 2 else block)
+    return [got[block] for block in swapped_order(owners)]
 
 
 def shards(embeddings, cluster_ids, priority):
@@ -206,13 +227,14 @@
     )
     found = jax.ShapeDtypeStruct((owners, 1, LANES), jnp.float32)
     if paired:
-        block = jax.ShapeDtypeStruct((width // LANES * capacity + META, LANES), jnp.bfloat16)
-        outgoing = call(pack_kernel, sizes, [block] * owners, embeddings, place, meta)
+        height = 2 * (width // LANES) * capacity + META
+        pair = jax.ShapeDtypeStruct((height, LANES), jnp.bfloat16)
+        outgoing = call(pack_kernel, sizes, [pair] * (owners // 2), embeddings, place, meta)
         best = call(
             match_paired_kernel,
             (owners, capacity),
             found,
-            *swap(outgoing),
+            *swap(outgoing, owners),
             scratch_shapes=[pltpu.VMEM((slots, width), jnp.bfloat16)],
         )
     else:

time: 45.8 us -> 45.9 us (level)
  starting transfers between devices: 26.6 us -> 15.6 us
  waiting for transfers between devices: 4.53 us -> 14.8 us
  blocking collectives: 10.5 us -> 11.3 us
    ppermute x15, starting transfers between devices: 26.6 us -> 15.6 us  [across(): return lax.ppermute(pair, 'shard', [(d, d ^ k) for d in range(owners)])]
    ppermute x15, waiting for transfers between devices: 4.53 us -> 14.8 us  [across(): return lax.ppermute(pair, 'shard', [(d, d ^ k) for d in range(owners)])]
    all_to_all x1, blocking collectives: 10.5 us -> 11.3 us  [shards(): returned = lax.all_to_all(best, 'shard', 0, 0, tiled=True)]
  transfers between devices with their start and end apart: 15 -> 15, of which waited for: 5 -> 6; matrix products, arithmetic and copies ran while one was open for 0% -> 0% of each run, Pallas kernels for 0% -> 0%
where the time goes in v8:
time: 45.9 us; the launch traced here: 45.7 us
  starting transfers between devices  15.6 us (34%)
  waiting for transfers between devices  14.8 us (32%)
  blocking collectives  11.3 us (25%)
  Pallas kernels  2.53 us (6%)
  local copies, waits for them, and re-layouts  0.71 us (2%)
  other arithmetic  0.7 us (2%)
    ppermute x15, starting transfers between devices, across(): return lax.ppermute(pair, 'shard', [(d, d ^ k) for d in range(owners)])  15.6 us
    ppermute x15, waiting for transfers between devices, across(): return lax.ppermute(pair, 'shard', [(d, d ^ k) for d in range(owners)])  14.8 us
    all_to_all x1, blocking collectives, shards(): returned = lax.all_to_all(best, 'shard', 0, 0, tiled=True)  11.3 us
    pallas_call x4, Pallas kernels, call(): pl.pallas_call(body, out_shape=shapes, compiler_params=pltpu.CompilerPara...  2.53 us
  transfers between devices with their start and end apart: 15, of which 6 were waited for; matrix products, arithmetic and copies ran while one was open for 0% of the time, Pallas kernels for 0%

profile of v8, /device:TPU:0, one launch (start us, length us, event | category | flops | bytes accessed | tf_op | source)
XLA Modules:
  0.0 45.7 jit_solution(291639476913580250)
XLA Ops:
  0.0 0.7 %multiply_add_fusion = s32[256]{0:T(256)S(1)} fusion(s32[256]{0:T(256)} %param.5, s32[256]{0:T(256)} %param.4), kind=kLoop, calls=%fused_computation | loop fusion | flops 512 | bytes 3072 | tf_op jit(solution)/shard_map/add | solution.py:223
  0.7 0.0 copy-start
  0.7 0.3 shard_map.37
  1.0 0.7 %copy-done = bf16[256,1024]{1,0:T(8,128)(2,1)S(1)} copy-done((bf16[256,1024]{1,0:T(8,128)(2,1)S(1)}, bf16[256,1024]{1,0:T(8,128)(2,1)}, u32[]{:S(2)}) %copy-start) | copy-done | bytes 524312
  1.7 0.6 %shard_map.38 = (bf16[520,128]{1,0:T(8,128)(2,1)S(1)}, bf16[520,128]{1,0:T(8,128)(2,1)S(1)}, bf16[520,128]{1,0:T(8,128)(2,1)S(1)}, bf16[520,128]{1,0:T(8,128)(2,...) custom-call(bf16[256,1024]{1,0:T(8,128)(2,1)S(1)} %copy-done, ...), custom_call_target="tpu_custom_call" | custom-call | tf_op jit(solution)/shard_map/pallas_call | solution.py:181
  2.3 4.1 %collective-permute-start = (bf16[520,128]{1,0:T(8,128)(2,1)S(1)}, bf16[520,128]{1,0:T(8,128)(2,1)S(1)}, u32[]{:S(2)}, u32[]{:S(2)}) collective-permute-start(bf16[520,128]{1,0:T(8,128)(2,1)S(1)} %get-tuple-element.37), channel_id=1, source_target_pairs={{0,8},{1,9},{2,10},{3,11},{4,12},{5,13},{6,14},{7,15},{8,0},{9,1},... | collective-permute-start | bytes 399368 | tf_op jit(solution)/shard_map/ppermute | solution.py:194
  6.4 1.3 %collective-permute-start.1 = (bf16[520,128]{1,0:T(8,128)(2,1)S(1)}, bf16[520,128]{1,0:T(8,128)(2,1)S(1)}, u32[]{:S(2)}, u32[]{:S(2)}) collective-permute-start(bf16[520,128]{1,0:T(8,128)(2,1)S(1)} %get-tuple-element.39), channel_id=1, source_target_pairs={{0,10},{1,11},{2,8},{3,9},{4,14},{5,15},{6,12},{7,13},{8,2},{9,3},... | collective-permute-start | bytes 399368 | tf_op jit(solution)/shard_map/ppermute | solution.py:194
  7.7 0.2 collective-permute-start.2
  8.0 1.8 %collective-permute-start.3 = (bf16[520,128]{1,0:T(8,128)(2,1)S(1)}, bf16[520,128]{1,0:T(8,128)(2,1)S(1)}, u32[]{:S(2)}, u32[]{:S(2)}) collective-permute-start(bf16[520,128]{1,0:T(8,128)(2,1)S(1)} %get-tuple-element.44), channel_id=1, source_target_pairs={{0,4},{1,5},{2,6},{3,7},{4,0},{5,1},{6,2},{7,3},{8,12},{9,13},{10,... | collective-permute-start | bytes 399368 | tf_op jit(solution)/shard_map/ppermute | solution.py:194
  9.8 6.7 %collective-permute-done.refs_0_ = bf16[520,128]{1,0:T(8,128)(2,1)S(1)} collective-permute-done((bf16[520,128]{1,0:T(8,128)(2,1)S(1)}, bf16[520,128]{1,0:T(8,128)(2,1)S(1)}, u32[]{:S(2)}, u32[]{:S(2)}) %collective-permute-start) | collective-permute-done | bytes 133152 | tf_op jit(solution)/shard_map/ppermute | solution.py:194
  16.5 0.0 collective-permute-start.5
  16.5 2.9 %collective-permute-start.4 = (bf16[520,128]{1,0:T(8,128)(2,1)S(1)}, bf16[520,128]{1,0:T(8,128)(2,1)S(1)}, u32[]{:S(2)}, u32[]{:S(2)}) collective-permute-start(bf16[520,128]{1,0:T(8,128)(2,1)S(1)} %get-tuple-element.46), channel_id=1, source_target_pairs={{0,12},{1,13},{2,14},{3,15},{4,8},{5,9},{6,10},{7,11},{8,4},{9,5},... | collective-permute-start | bytes 399368 | tf_op jit(solution)/shard_map/ppermute | solution.py:194
  19.4 0.1 collective-permute-done.1.refs_1_
  19.5 0.1 collective-permute-start.9
  19.7 0.0 collective-permute-done.2.refs_2_
  19.7 0.7 %collective-permute-start.6 = (bf16[520,128]{1,0:T(8,128)(2,1)S(1)}, bf16[520,128]{1,0:T(8,128)(2,1)S(1)}, u32[]{:S(2)}, u32[]{:S(2)}) collective-permute-start(bf16[520,128]{1,0:T(8,128)(2,1)S(1)} %get-tuple-element.51), channel_id=1, source_target_pairs={{0,6},{1,7},{2,4},{3,5},{4,2},{5,3},{6,0},{7,1},{8,14},{9,15},{10,... | collective-permute-start | bytes 399368 | tf_op jit(solution)/shard_map/ppermute | solution.py:194
  20.4 0.0 collective-permute-done.3.refs_3_
  20.4 0.2 collective-permute-start.8
  20.6 0.0 collective-permute-done.5.refs_5_
  20.6 3.1 %collective-permute-start.7 = (bf16[520,128]{1,0:T(8,128)(2,1)S(1)}, bf16[520,128]{1,0:T(8,128)(2,1)S(1)}, u32[]{:S(2)}, u32[]{:S(2)}) collective-permute-start(bf16[520,128]{1,0:T(8,128)(2,1)S(1)} %get-tuple-element.53), channel_id=1, source_target_pairs={{0,14},{1,15},{2,12},{3,13},{4,10},{5,11},{6,8},{7,9},{8,6},{9,7},... | collective-permute-start | bytes 399368 | tf_op jit(solution)/shard_map/ppermute | solution.py:194
  23.7 0.8 %collective-permute-done.4.refs_4_ = bf16[520,128]{1,0:T(8,128)(2,1)S(1)} collective-permute-done((bf16[520,128]{1,0:T(8,128)(2,1)S(1)}, bf16[520,128]{1,0:T(8,128)(2,1)S(1)}, u32[]{:S(2)}, u32[]{:S(2)}) %collective-permute-start.4) | collective-permute-done | bytes 133152 | tf_op jit(solution)/shard_map/ppermute | solution.py:194
  24.5 0.0 collective-permute-start.13
  24.5 0.0 collective-permute-done.9.refs_9_
  24.5 0.5 %collective-permute-start.12 = (bf16[520,128]{1,0:T(8,128)(2,1)S(1)}, bf16[520,128]{1,0:T(8,128)(2,1)S(1)}, u32[]{:S(2)}, u32[]{:S(2)}) collective-permute-start(bf16[520,128]{1,0:T(8,128)(2,1)S(1)} %get-tuple-element.62.refs_15_), channel_id=1, source_target_pairs={{0,1},{1,0},{2,3},{3,2},{4,5},{5,4},{6,7},{7,6},{8,9},{9,8},{10,11... | collective-permute-start | bytes 399368 | tf_op jit(solution)/shard_map/ppermute | solution.py:194
  25.0 3.9 %collective-permute-done.6.refs_6_ = bf16[520,128]{1,0:T(8,128)(2,1)S(1)} collective-permute-done((bf16[520,128]{1,0:T(8,128)(2,1)S(1)}, bf16[520,128]{1,0:T(8,128)(2,1)S(1)}, u32[]{:S(2)}, u32[]{:S(2)}) %collective-permute-start.6) | collective-permute-done | bytes 133152 | tf_op jit(solution)/shard_map/ppermute | solution.py:194
  28.9 0.1 collective-permute-start.11
  29.0 0.0 collective-permute-done.8.refs_8_
  29.0 0.4 collective-permute-start.10
  29.4 2.0 %collective-permute-done.7.refs_7_ = bf16[520,128]{1,0:T(8,128)(2,1)S(1)} collective-permute-done((bf16[520,128]{1,0:T(8,128)(2,1)S(1)}, bf16[520,128]{1,0:T(8,128)(2,1)S(1)}, u32[]{:S(2)}, u32[]{:S(2)}) %collective-permute-start.7) | collective-permute-done | bytes 133152 | tf_op jit(solution)/shard_map/ppermute | solution.py:194
  31.4 0.0 collective-permute-start.14
  31.4 0.0 collective-permute-done.13.refs_13_
  31.4 0.0 collective-permute-done.12.refs_12_
  31.4 0.0 collective-permute-done.11.refs_11_
  31.4 0.0 collective-permute-done.10.refs_10_
  31.5 1.3 %collective-permute-done.14.refs_14_ = bf16[520,128]{1,0:T(8,128)(2,1)S(1)} collective-permute-done((bf16[520,128]{1,0:T(8,128)(2,1)S(1)}, bf16[520,128]{1,0:T(8,128)(2,1)S(1)}, u32[]{:S(2)}, u32[]{:S(2)}) %collective-permute-start.14) | collective-permute-done | bytes 133152 | tf_op jit(solution)/shard_map/ppermute | solution.py:194
  32.8 0.9 %shard_map.39 = f32[16,1,128]{2,1,0:T(1,128)S(1)} custom-call(bf16[520,128]{1,0:T(8,128)(2,1)S(1)} %collective-permute-done.refs_0_, bf16[520,128]{1,0:T(8,128)(2,1)S(1)} %collective-permute-done.1.refs_1_, bf16[520,128]{1,0:T(8,128)(2,1)S(1)} %collective-permute-done.2.refs_2_, bf16[520,128]{1,0:T(8,128)(2,1)S(1)} %collective-permute-done.3.refs_3_, ...), custom_call_target="tpu_custom_call" | custom-call | tf_op jit(solution)/shard_map/pallas_call | solution.py:181
  33.6 11.3 %all_to_all.5.refs_0_ = f32[16,1,128]{2,1,0:T(1,128)S(1)} all-to-all(f32[16,1,128]{2,1,0:T(1,128)S(1)} %shard_map.39), channel_id=1, replica_groups=mesh['groups'=2,'shard'=16] {'shard'}, dimensions={0} | all-to-all | bytes 16384 | tf_op jit(solution)/shard_map/all_to_all | solution.py:248
  44.9 0.7 %shard_map.40 = f32[1,256]{1,0:T(1,128)} custom-call(f32[16,1,128]{2,1,0:T(1,128)S(1)} %all_to_all.5.refs_0_, s32[1,256]{1,0:T(1,128)S(1)} %get-tuple-element.35.refs_1_), custom_call_target="tpu_custom_call" | custom-call | tf_op jit(solution)/shard_map/pallas_call | solution.py:181
Async XLA Ops:
  0.7 1.0 %copy-start = (bf16[256,1024]{1,0:T(8,128)(2,1)S(1)}, bf16[256,1024]{1,0:T(8,128)(2,1)}, u32[]{:S(2)}) copy-start(bf16[256,1024]{1,0:T(8,128)(2,1)} %refs_0_.1) | copy-start | bytes 1572868
  2.3 14.2 %collective-permute-start = (bf16[520,128]{1,0:T(8,128)(2,1)S(1)}, bf16[520,128]{1,0:T(8,128)(2,1)S(1)}, u32[]{:S(2)}, u32[]{:S(2)}) collective-permute-start(bf16[520,128]{1,0:T(8,128)(2,1)S(1)} %get-tuple-element.37), channel_id=1, source_target_pairs={{0,8},{1,9},{2,10},{3,11},{4,12},{5,13},{6,14},{7,15},{8,0},{9,1},... | collective-permute-start | bytes 399368 | tf_op jit(solution)/shard_map/ppermute | solution.py:194
  6.4 13.1 %collective-permute-start.1 = (bf16[520,128]{1,0:T(8,128)(2,1)S(1)}, bf16[520,128]{1,0:T(8,128)(2,1)S(1)}, u32[]{:S(2)}, u32[]{:S(2)}) collective-permute-start(bf16[520,128]{1,0:T(8,128)(2,1)S(1)} %get-tuple-element.39), channel_id=1, source_target_pairs={{0,10},{1,11},{2,8},{3,9},{4,14},{5,15},{6,12},{7,13},{8,2},{9,3},... | collective-permute-start | bytes 399368 | tf_op jit(solution)/shard_map/ppermute | solution.py:194
  7.7 11.9 %collective-permute-start.2 = (bf16[520,128]{1,0:T(8,128)(2,1)S(1)}, bf16[520,128]{1,0:T(8,128)(2,1)S(1)}, u32[]{:S(2)}, u32[]{:S(2)}) collective-permute-start(bf16[520,128]{1,0:T(8,128)(2,1)S(1)} %get-tuple-element.42), channel_id=1, source_target_pairs={{0,2},{1,3},{2,0},{3,1},{4,6},{5,7},{6,4},{7,5},{8,10},{9,11},{10,... | collective-permute-start | bytes 399368 | tf_op jit(solution)/shard_map/ppermute | solution.py:194
  8.0 12.4 %collective-permute-start.3 = (bf16[520,128]{1,0:T(8,128)(2,1)S(1)}, bf16[520,128]{1,0:T(8,128)(2,1)S(1)}, u32[]{:S(2)}, u32[]{:S(2)}) collective-permute-start(bf16[520,128]{1,0:T(8,128)(2,1)S(1)} %get-tuple-element.44), channel_id=1, source_target_pairs={{0,4},{1,5},{2,6},{3,7},{4,0},{5,1},{6,2},{7,3},{8,12},{9,13},{10,... | collective-permute-start | bytes 399368 | tf_op jit(solution)/shard_map/ppermute | solution.py:194
  16.5 4.1 %collective-permute-start.5 = (bf16[520,128]{1,0:T(8,128)(2,1)S(1)}, bf16[520,128]{1,0:T(8,128)(2,1)S(1)}, u32[]{:S(2)}, u32[]{:S(2)}) collective-permute-start(bf16[520,128]{1,0:T(8,128)(2,1)S(1)} %collective-permute-done.refs_0_), channel_id=1, source_target_pairs={{0,1},{1,0},{2,3},{3,2},{4,5},{5,4},{6,7},{7,6},{8,9},{9,8},{10,11... | collective-permute-start | bytes 399368 | tf_op jit(solution)/shard_map/ppermute | solution.py:194
  16.5 7.9 %collective-permute-start.4 = (bf16[520,128]{1,0:T(8,128)(2,1)S(1)}, bf16[520,128]{1,0:T(8,128)(2,1)S(1)}, u32[]{:S(2)}, u32[]{:S(2)}) collective-permute-start(bf16[520,128]{1,0:T(8,128)(2,1)S(1)} %get-tuple-element.46), channel_id=1, source_target_pairs={{0,12},{1,13},{2,14},{3,15},{4,8},{5,9},{6,10},{7,11},{8,4},{9,5},... | collective-permute-start | bytes 399368 | tf_op jit(solution)/shard_map/ppermute | solution.py:194
  19.5 4.9 %collective-permute-start.9 = (bf16[520,128]{1,0:T(8,128)(2,1)S(1)}, bf16[520,128]{1,0:T(8,128)(2,1)S(1)}, u32[]{:S(2)}, u32[]{:S(2)}) collective-permute-start(bf16[520,128]{1,0:T(8,128)(2,1)S(1)} %collective-permute-done.1.refs_1_), channel_id=1, source_target_pairs={{0,1},{1,0},{2,3},{3,2},{4,5},{5,4},{6,7},{7,6},{8,9},{9,8},{10,11... | collective-permute-start | bytes 399368 | tf_op jit(solution)/shard_map/ppermute | solution.py:194
  19.7 9.3 %collective-permute-start.6 = (bf16[520,128]{1,0:T(8,128)(2,1)S(1)}, bf16[520,128]{1,0:T(8,128)(2,1)S(1)}, u32[]{:S(2)}, u32[]{:S(2)}) collective-permute-start(bf16[520,128]{1,0:T(8,128)(2,1)S(1)} %get-tuple-element.51), channel_id=1, source_target_pairs={{0,6},{1,7},{2,4},{3,5},{4,2},{5,3},{6,0},{7,1},{8,14},{9,15},{10,... | collective-permute-start | bytes 399368 | tf_op jit(solution)/shard_map/ppermute | solution.py:194
  20.4 8.6 %collective-permute-start.8 = (bf16[520,128]{1,0:T(8,128)(2,1)S(1)}, bf16[520,128]{1,0:T(8,128)(2,1)S(1)}, u32[]{:S(2)}, u32[]{:S(2)}) collective-permute-start(bf16[520,128]{1,0:T(8,128)(2,1)S(1)} %collective-permute-done.2.refs_2_), channel_id=1, source_target_pairs={{0,1},{1,0},{2,3},{3,2},{4,5},{5,4},{6,7},{7,6},{8,9},{9,8},{10,11... | collective-permute-start | bytes 399368 | tf_op jit(solution)/shard_map/ppermute | solution.py:194
  20.6 10.8 %collective-permute-start.7 = (bf16[520,128]{1,0:T(8,128)(2,1)S(1)}, bf16[520,128]{1,0:T(8,128)(2,1)S(1)}, u32[]{:S(2)}, u32[]{:S(2)}) collective-permute-start(bf16[520,128]{1,0:T(8,128)(2,1)S(1)} %get-tuple-element.53), channel_id=1, source_target_pairs={{0,14},{1,15},{2,12},{3,13},{4,10},{5,11},{6,8},{7,9},{8,6},{9,7},... | collective-permute-start | bytes 399368 | tf_op jit(solution)/shard_map/ppermute | solution.py:194
  24.5 7.0 %collective-permute-start.13 = (bf16[520,128]{1,0:T(8,128)(2,1)S(1)}, bf16[520,128]{1,0:T(8,128)(2,1)S(1)}, u32[]{:S(2)}, u32[]{:S(2)}) collective-permute-start(bf16[520,128]{1,0:T(8,128)(2,1)S(1)} %collective-permute-done.4.refs_4_), channel_id=1, source_target_pairs={{0,1},{1,0},{2,3},{3,2},{4,5},{5,4},{6,7},{7,6},{8,9},{9,8},{10,11... | collective-permute-start | bytes 399368 | tf_op jit(solution)/shard_map/ppermute | solution.py:194
  24.5 7.0 %collective-permute-start.12 = (bf16[520,128]{1,0:T(8,128)(2,1)S(1)}, bf16[520,128]{1,0:T(8,128)(2,1)S(1)}, u32[]{:S(2)}, u32[]{:S(2)}) collective-permute-start(bf16[520,128]{1,0:T(8,128)(2,1)S(1)} %get-tuple-element.62.refs_15_), channel_id=1, source_target_pairs={{0,1},{1,0},{2,3},{3,2},{4,5},{5,4},{6,7},{7,6},{8,9},{9,8},{10,11... | collective-permute-start | bytes 399368 | tf_op jit(solution)/shard_map/ppermute | solution.py:194
  28.9 2.5 %collective-permute-start.11 = (bf16[520,128]{1,0:T(8,128)(2,1)S(1)}, bf16[520,128]{1,0:T(8,128)(2,1)S(1)}, u32[]{:S(2)}, u32[]{:S(2)}) collective-permute-start(bf16[520,128]{1,0:T(8,128)(2,1)S(1)} %collective-permute-done.6.refs_6_), channel_id=1, source_target_pairs={{0,1},{1,0},{2,3},{3,2},{4,5},{5,4},{6,7},{7,6},{8,9},{9,8},{10,11... | collective-permute-start | bytes 399368 | tf_op jit(solution)/shard_map/ppermute | solution.py:194
  29.0 2.5 %collective-permute-start.10 = (bf16[520,128]{1,0:T(8,128)(2,1)S(1)}, bf16[520,128]{1,0:T(8,128)(2,1)S(1)}, u32[]{:S(2)}, u32[]{:S(2)}) collective-permute-start(bf16[520,128]{1,0:T(8,128)(2,1)S(1)} %collective-permute-done.3.refs_3_), channel_id=1, source_target_pairs={{0,1},{1,0},{2,3},{3,2},{4,5},{5,4},{6,7},{7,6},{8,9},{9,8},{10,11... | collective-permute-start | bytes 399368 | tf_op jit(solution)/shard_map/ppermute | solution.py:194
  31.4 1.4 %collective-permute-start.14 = (bf16[520,128]{1,0:T(8,128)(2,1)S(1)}, bf16[520,128]{1,0:T(8,128)(2,1)S(1)}, u32[]{:S(2)}, u32[]{:S(2)}) collective-permute-start(bf16[520,128]{1,0:T(8,128)(2,1)S(1)} %collective-permute-done.7.refs_7_), channel_id=1, source_target_pairs={{0,1},{1,0},{2,3},{3,2},{4,5},{5,4},{6,7},{7,6},{8,9},{9,8},{10,11... | collective-permute-start | bytes 399368 | tf_op jit(solution)/shard_map/ppermute | solution.py:194

commit v9 on v7

--- a/solution.py
+++ b/solution.py
@@ -28,16 +28,6 @@
 
 def onehots(mask):
     return jnp.where(mask, 1.0, 0.0).astype(jnp.bfloat16)
-
-
-def block_order(owners):
-    half = owners // 2
-    far = list(range(half, owners))
-    near = list(range(half - 1, -1, -1))
-    order = far[:2]
-    for block in far[2:]:
-        order += [block, near.pop(0)]
-    return order + near
 
 
 def place_kernel(owners, capacity, paired, code_ref, place_ref, meta_ref):
@@ -77,14 +67,23 @@
         out_refs[0][:, width:] = meta
         return
     pieces = width // LANES
-    for block, out_ref in zip(block_order(owners), out_refs):
+    half = owners // 2
+    me = lax.rem(lax.axis_index("shard"), half)
+    *pair_refs, near_ref = out_refs
+    for block in range(owners):
+        if block < half:
+            out_ref, base = near_ref.at[me ^ block], 0
+        else:
+            out_ref, base = pair_refs[(block - half) // 2], block % 2 * pieces * capacity
         top = block * capacity
         for piece in range(pieces):
-            out_ref[piece * capacity:(piece + 1) * capacity] = unit[
+            start = base + piece * capacity
+            out_ref[start:start + capacity] = unit[
                 top:top + capacity, piece * LANES:(piece + 1) * LANES
             ]
-        left = top // LANES * LANES
-        out_ref[pieces * capacity:] = meta[:, left:left + LANES]
+        if block < half or block % 2 == 0:
+            left = top // LANES * LANES
+            out_ref[out_ref.shape[0] - META:] = meta[:, left:left + LANES]
 
 
 def maxima(units, code, code_down):
@@ -101,15 +100,19 @@
 
 
 def match_paired_kernel(owners, capacity, *refs):
-    *in_refs, out_ref, rows_ref = refs
-    in_refs = dict(zip(block_order(owners), in_refs))
+    *pair_refs, near_ref, out_ref, rows_ref = refs
+    half = owners // 2
+    me = lax.axis_index("shard")
     slots, width = rows_ref.shape
     pieces = width // LANES
-    for block, in_ref in in_refs.items():
+    in_refs = [near_ref.at[lax.rem(me, half) ^ block] for block in range(half)] + pair_refs
+    for block, in_ref in enumerate(in_refs):
         top = block * capacity
+        base = block % 2 * pieces if block >= half else 0
         for piece in range(pieces):
+            start = (base + piece) * capacity
             rows_ref[top:top + capacity, piece * LANES:(piece + 1) * LANES] = in_ref[
-                piece * capacity:(piece + 1) * capacity
+                start:start + capacity
             ]
     each = LANES // capacity
     part = lax.div(iota((META, LANES), 1), capacity)
@@ -117,13 +120,13 @@
     for first in range(0, owners, each):
         meta = jnp.zeros((META, LANES), jnp.float32)
         for number in range(each):
-            lines = in_refs[first + number][pieces * capacity:].astype(jnp.float32)
+            in_ref = in_refs[first + number]
+            lines = in_ref[in_ref.shape[0] - META:].astype(jnp.float32)
             meta = jnp.where(part == number, lines, meta)
         code.append(meta[0:1] * SPAN + meta[1:2] * RADIX + meta[2:3])
     code = jnp.concatenate(code, axis=1)
     code_down = jnp.broadcast_to(code, (8, slots)).T[:, 0:1]
     best = maxima(lambda start, stop: rows_ref[start:stop], code, code_down)
-    me = lax.axis_index("shard")
     for block in range(owners):
         base = block * capacity // LANES * LANES
         out_ref[me ^ block] = best[:, base:base + LANES]
@@ -177,12 +180,20 @@
     )(*args)
 
 
-def swap(blocks):
-    owners = len(blocks)
-    return [
-        lax.ppermute(block, "shard", [(d, d ^ k) for d in range(owners)]) if k else block
-        for k, block in zip(block_order(owners), blocks)
-    ]
+def swap(pairs, near, owners):
+    half = owners // 2
+
+    def across(value, distance):
+        return lax.ppermute(value, "shard", [(d, d ^ distance) for d in range(owners)])
+
+    far = [across(pair, half + 2 * number) for number, pair in enumerate(pairs)]
+    groups = [list(range(half)), list(range(half, owners))]
+    near = lax.all_to_all(near, "shard", 0, 0, axis_index_groups=groups, tiled=True)
+    far[0], near = lax.optimization_barrier((far[0], near))
+    got = []
+    for pair in far:
+        got += [pair, across(pair, 1)]
+    return [*got, near]
 
 
 def shards(embeddings, cluster_ids, priority):
@@ -206,13 +217,20 @@
     )
     found = jax.ShapeDtypeStruct((owners, 1, LANES), jnp.float32)
     if paired:
-        block = jax.ShapeDtypeStruct((width // LANES * capacity + META, LANES), jnp.bfloat16)
-        outgoing = call(pack_kernel, sizes, [block] * owners, embeddings, place, meta)
+        height = width // LANES * capacity
+        half = owners // 2
+        *pairs, near = call(
+            pack_kernel,
+            sizes,
+            [jax.ShapeDtypeStruct((2 * height + META, LANES), jnp.bfloat16)] * (half // 2)
+            + [jax.ShapeDtypeStruct((half, height + META, LANES), jnp.bfloat16)],
+            embeddings, place, meta,
+        )
         best = call(
             match_paired_kernel,
             (owners, capacity),
             found,
-            *swap(outgoing),
+            *swap(pairs, near, owners),
             scratch_shapes=[pltpu.VMEM((slots, width), jnp.bfloat16)],
         )
     else:

time: 45.8 us -> 50.7 us (1.11)
  waiting for transfers between devices: 4.53 us -> 22 us
  starting transfers between devices: 26.6 us -> 12.6 us
  Pallas kernels: 2.53 us -> 3.29 us
  blocking collectives: 10.5 us -> 11.1 us
    ppermute x15 -> x8, starting transfers between devices: 26.6 us -> 7.32 us  [across(): lax.ppermute(value, 'shard', [(d, d ^ distance) for d in range(owners)])]
    ppermute x15 -> x8, waiting for transfers between devices: 4.53 us -> 22 us  [across(): lax.ppermute(value, 'shard', [(d, d ^ distance) for d in range(owners)])]
    all_to_all x0 -> x1, starting transfers between devices: none -> 5.26 us  [swap(): lax.all_to_all(near, 'shard', 0, 0, axis_index_groups=groups, tiled=True)]
    pallas_call x4, Pallas kernels: 2.53 us -> 3.29 us  [call(): pl.pallas_call(body, out_shape=shapes, compiler_params=pltpu.CompilerPara...]
    all_to_all x1, blocking collectives: 10.5 us -> 11.1 us  [shards(): returned = lax.all_to_all(best, 'shard', 0, 0, tiled=True)]
  transfers between devices with their start and end apart: 15 -> 9, of which waited for: 5 -> 5; matrix products, arithmetic and copies ran while one was open for 0% -> 0% of each run, Pallas kernels for 0% -> 0%
where the time goes in v9:
time: 50.7 us; the launch traced here: 50.4 us
  waiting for transfers between devices  22 us (43%)
  starting transfers between devices  12.6 us (25%)
  blocking collectives  11.1 us (22%)
  Pallas kernels  3.29 us (6%)
  local copies, waits for them, and re-layouts  0.71 us (1%)
  other arithmetic  0.7 us (1%)
    ppermute x8, waiting for transfers between devices, across(): lax.ppermute(value, 'shard', [(d, d ^ distance) for d in range(owners)])  22 us
    all_to_all x1, blocking collectives, shards(): returned = lax.all_to_all(best, 'shard', 0, 0, tiled=True)  11.1 us
    ppermute x8, starting transfers between devices, across(): lax.ppermute(value, 'shard', [(d, d ^ distance) for d in range(owners)])  7.32 us
    all_to_all x1, starting transfers between devices, swap(): lax.all_to_all(near, 'shard', 0, 0, axis_index_groups=groups, tiled=True)  5.26 us
    pallas_call x4, Pallas kernels, call(): pl.pallas_call(body, out_shape=shapes, compiler_params=pltpu.CompilerPara...  3.29 us
  transfers between devices with their start and end apart: 9, of which 5 were waited for; matrix products, arithmetic and copies ran while one was open for 0% of the time, Pallas kernels for 0%

profile of v9, /device:TPU:0, one launch (start us, length us, event | category | flops | bytes accessed | tf_op | source)
XLA Modules:
  0.0 50.4 jit_solution(8406842316752106157)
XLA Ops:
  0.0 0.7 %multiply_add_fusion = s32[256]{0:T(256)S(1)} fusion(s32[256]{0:T(256)} %param.5, s32[256]{0:T(256)} %param.4), kind=kLoop, calls=%fused_computation | loop fusion | flops 512 | bytes 3072 | tf_op jit(solution)/shard_map/add | solution.py:213
  0.7 0.0 copy-start
  0.7 0.3 shard_map.37
  1.0 0.7 %copy-done = bf16[256,1024]{1,0:T(8,128)(2,1)S(1)} copy-done((bf16[256,1024]{1,0:T(8,128)(2,1)S(1)}, bf16[256,1024]{1,0:T(8,128)(2,1)}, u32[]{:S(2)}) %copy-start) | copy-done | bytes 524312
  1.7 1.3 %shard_map.38 = (bf16[520,128]{1,0:T(8,128)(2,1)S(1)}, bf16[520,128]{1,0:T(8,128)(2,1)S(1)}, bf16[520,128]{1,0:T(8,128)(2,1)S(1)}, bf16[520,128]{1,0:T(8,128)(2,1)S(1)}, bf16[8,264,128]{2,1,0:T(8,128)(2,1)}) custom-call(bf16[256,1024]{1,0:T(8,128)(2,1)S(1)} %copy-done, s32[1,256]{1,0:T(1,128)S(1)} %get-tuple-element.14.refs_1_, ...), custom_call_target="tpu_custom_call" | custom-call | tf_op jit(solution)/shard_map/pallas_call | solution.py:175
  3.1 5.3 %all-to-all-start = ((bf16[8,264,128]{2,1,0:T(8,128)(2,1)}), bf16[8,264,128]{2,1,0:T(8,128)(2,1)S(1)}, u32[]{:S(2)}, u32[]{:S(2)}) async-start(bf16[8,264,128]{2,1,0:T(8,128)(2,1)} %get-tuple-element.17), calls=%async_computation | async-start | bytes 1081344 | tf_op jit(solution)/shard_map/all_to_all | solution.py:191
  8.3 4.0 %collective-permute-start.2 = (bf16[520,128]{1,0:T(8,128)(2,1)S(1)}, bf16[520,128]{1,0:T(8,128)(2,1)S(1)}, u32[]{:S(2)}, u32[]{:S(2)}) collective-permute-start(bf16[520,128]{1,0:T(8,128)(2,1)S(1)} %get-tuple-element.19), channel_id=1, source_target_pairs={{0,10},{1,11},{2,8},{3,9},{4,14},{5,15},{6,12},{7,13},{8,2},{9,3},... | collective-permute-start | bytes 399368 | tf_op jit(solution)/shard_map/ppermute | solution.py:187
  12.4 1.2 %collective-permute-start.4 = (bf16[520,128]{1,0:T(8,128)(2,1)S(1)}, bf16[520,128]{1,0:T(8,128)(2,1)S(1)}, u32[]{:S(2)}, u32[]{:S(2)}) collective-permute-start(bf16[520,128]{1,0:T(8,128)(2,1)S(1)} %get-tuple-element.20), channel_id=1, source_target_pairs={{0,12},{1,13},{2,14},{3,15},{4,8},{5,9},{6,10},{7,11},{8,4},{9,5},... | collective-permute-start | bytes 399368 | tf_op jit(solution)/shard_map/ppermute | solution.py:187
  13.6 2.0 %collective-permute-start.6 = (bf16[520,128]{1,0:T(8,128)(2,1)S(1)}, bf16[520,128]{1,0:T(8,128)(2,1)S(1)}, u32[]{:S(2)}, u32[]{:S(2)}) collective-permute-start(bf16[520,128]{1,0:T(8,128)(2,1)S(1)} %get-tuple-element.21), channel_id=1, source_target_pairs={{0,14},{1,15},{2,12},{3,13},{4,10},{5,11},{6,8},{7,9},{8,6},{9,7},... | collective-permute-start | bytes 399368 | tf_op jit(solution)/shard_map/ppermute | solution.py:187
  15.6 0.0 collective-permute-start
  15.6 2.7 %collective-permute-done.2.refs_2_ = bf16[520,128]{1,0:T(8,128)(2,1)S(1)} collective-permute-done((bf16[520,128]{1,0:T(8,128)(2,1)S(1)}, bf16[520,128]{1,0:T(8,128)(2,1)S(1)}, u32[]{:S(2)}, u32[]{:S(2)}) %collective-permute-start.2) | collective-permute-done | bytes 133152 | tf_op jit(solution)/shard_map/ppermute | solution.py:187
  18.4 0.0 collective-permute-start.3
  18.4 7.3 %collective-permute-done.4.refs_4_ = bf16[520,128]{1,0:T(8,128)(2,1)S(1)} collective-permute-done((bf16[520,128]{1,0:T(8,128)(2,1)S(1)}, bf16[520,128]{1,0:T(8,128)(2,1)S(1)}, u32[]{:S(2)}, u32[]{:S(2)}) %collective-permute-start.4) | collective-permute-done | bytes 133152 | tf_op jit(solution)/shard_map/ppermute | solution.py:187
  25.7 0.0 collective-permute-start.5
  25.7 3.7 %collective-permute-done.6.refs_6_ = bf16[520,128]{1,0:T(8,128)(2,1)S(1)} collective-permute-done((bf16[520,128]{1,0:T(8,128)(2,1)S(1)}, bf16[520,128]{1,0:T(8,128)(2,1)S(1)}, u32[]{:S(2)}, u32[]{:S(2)}) %collective-permute-start.6) | collective-permute-done | bytes 133152 | tf_op jit(solution)/shard_map/ppermute | solution.py:187
  29.4 0.0 collective-permute-start.7
  29.4 6.9 %collective-permute-done.refs_0_ = bf16[520,128]{1,0:T(8,128)(2,1)S(1)} collective-permute-done((bf16[520,128]{1,0:T(8,128)(2,1)S(1)}, bf16[520,128]{1,0:T(8,128)(2,1)S(1)}, u32[]{:S(2)}, u32[]{:S(2)}) %collective-permute-start) | collective-permute-done | bytes 133152 | tf_op jit(solution)/shard_map/ppermute | solution.py:187
  36.3 0.0 all-to-all-done.refs_8_
  36.3 0.0 collective-permute-start.1
  36.3 0.0 collective-permute-done.3.refs_3_
  36.3 0.0 collective-permute-done.5.refs_5_
  36.3 0.0 collective-permute-done.7.refs_7_
  36.3 1.3 %collective-permute-done.1.refs_1_ = bf16[520,128]{1,0:T(8,128)(2,1)S(1)} collective-permute-done((bf16[520,128]{1,0:T(8,128)(2,1)S(1)}, bf16[520,128]{1,0:T(8,128)(2,1)S(1)}, u32[]{:S(2)}, u32[]{:S(2)}) %collective-permute-start.1) | collective-permute-done | bytes 133152 | tf_op jit(solution)/shard_map/ppermute | solution.py:187
  37.7 0.9 %shard_map.39 = f32[16,1,128]{2,1,0:T(1,128)S(1)} custom-call(bf16[520,128]{1,0:T(8,128)(2,1)S(1)} %collective-permute-done.refs_0_, bf16[520,128]{1,0:T(8,128)(2,1)S(1)} %collective-permute-done.1.refs_1_, bf16[520,128]{1,0:T(8,128)(2,1)S(1)} %collective-permute-done.2.refs_2_, bf16[520,128]{1,0:T(8,128)(2,1)S(1)} %collective-permute-done.3.refs_3_, ...), custom_call_target="tpu_custom_call" | custom-call | tf_op jit(solution)/shard_map/pallas_call | solution.py:175
  38.5 11.1 %all_to_all.10.refs_0_ = f32[16,1,128]{2,1,0:T(1,128)S(1)} all-to-all(f32[16,1,128]{2,1,0:T(1,128)S(1)} %shard_map.39), channel_id=1, replica_groups=mesh['groups'=2,'shard'=16] {'shard'}, dimensions={0} | all-to-all | bytes 16384 | tf_op jit(solution)/shard_map/all_to_all | solution.py:244
  49.6 0.7 %shard_map.40 = f32[1,256]{1,0:T(1,128)} custom-call(f32[16,1,128]{2,1,0:T(1,128)S(1)} %all_to_all.10.refs_0_, s32[1,256]{1,0:T(1,128)S(1)} %get-tuple-element.14.refs_1_), custom_call_target="tpu_custom_call" | custom-call | tf_op jit(solution)/shard_map/pallas_call | solution.py:175
Async XLA Ops:
  0.7 1.0 %copy-start = (bf16[256,1024]{1,0:T(8,128)(2,1)S(1)}, bf16[256,1024]{1,0:T(8,128)(2,1)}, u32[]{:S(2)}) copy-start(bf16[256,1024]{1,0:T(8,128)(2,1)} %refs_0_.1) | copy-start | bytes 1572868
  3.1 33.2 %all-to-all-start = ((bf16[8,264,128]{2,1,0:T(8,128)(2,1)}), bf16[8,264,128]{2,1,0:T(8,128)(2,1)S(1)}, u32[]{:S(2)}, u32[]{:S(2)}) async-start(bf16[8,264,128]{2,1,0:T(8,128)(2,1)} %get-tuple-element.17), calls=%async_computation | async-start | bytes 1081344 | tf_op jit(solution)/shard_map/all_to_all | solution.py:191
  8.3 10.0 %collective-permute-start.2 = (bf16[520,128]{1,0:T(8,128)(2,1)S(1)}, bf16[520,128]{1,0:T(8,128)(2,1)S(1)}, u32[]{:S(2)}, u32[]{:S(2)}) collective-permute-start(bf16[520,128]{1,0:T(8,128)(2,1)S(1)} %get-tuple-element.19), channel_id=1, source_target_pairs={{0,10},{1,11},{2,8},{3,9},{4,14},{5,15},{6,12},{7,13},{8,2},{9,3},... | collective-permute-start | bytes 399368 | tf_op jit(solution)/shard_map/ppermute | solution.py:187
  12.4 13.3 %collective-permute-start.4 = (bf16[520,128]{1,0:T(8,128)(2,1)S(1)}, bf16[520,128]{1,0:T(8,128)(2,1)S(1)}, u32[]{:S(2)}, u32[]{:S(2)}) collective-permute-start(bf16[520,128]{1,0:T(8,128)(2,1)S(1)} %get-tuple-element.20), channel_id=1, source_target_pairs={{0,12},{1,13},{2,14},{3,15},{4,8},{5,9},{6,10},{7,11},{8,4},{9,5},... | collective-permute-start | bytes 399368 | tf_op jit(solution)/shard_map/ppermute | solution.py:187
  13.6 15.8 %collective-permute-start.6 = (bf16[520,128]{1,0:T(8,128)(2,1)S(1)}, bf16[520,128]{1,0:T(8,128)(2,1)S(1)}, u32[]{:S(2)}, u32[]{:S(2)}) collective-permute-start(bf16[520,128]{1,0:T(8,128)(2,1)S(1)} %get-tuple-element.21), channel_id=1, source_target_pairs={{0,14},{1,15},{2,12},{3,13},{4,10},{5,11},{6,8},{7,9},{8,6},{9,7},... | collective-permute-start | bytes 399368 | tf_op jit(solution)/shard_map/ppermute | solution.py:187
  15.6 20.7 %collective-permute-start = (bf16[520,128]{1,0:T(8,128)(2,1)S(1)}, bf16[520,128]{1,0:T(8,128)(2,1)S(1)}, u32[]{:S(2)}, u32[]{:S(2)}) collective-permute-start(bf16[520,128]{1,0:T(8,128)(2,1)S(1)} %get-tuple-element.16), channel_id=1, source_target_pairs={{0,8},{1,9},{2,10},{3,11},{4,12},{5,13},{6,14},{7,15},{8,0},{9,1},... | collective-permute-start | bytes 399368 | tf_op jit(solution)/shard_map/ppermute | solution.py:187
  18.4 18.0 %collective-permute-start.3 = (bf16[520,128]{1,0:T(8,128)(2,1)S(1)}, bf16[520,128]{1,0:T(8,128)(2,1)S(1)}, u32[]{:S(2)}, u32[]{:S(2)}) collective-permute-start(bf16[520,128]{1,0:T(8,128)(2,1)S(1)} %collective-permute-done.2.refs_2_), channel_id=1, source_target_pairs={{0,1},{1,0},{2,3},{3,2},{4,5},{5,4},{6,7},{7,6},{8,9},{9,8},{10,11... | collective-permute-start | bytes 399368 | tf_op jit(solution)/shard_map/ppermute | solution.py:187
  25.7 10.7 %collective-permute-start.5 = (bf16[520,128]{1,0:T(8,128)(2,1)S(1)}, bf16[520,128]{1,0:T(8,128)(2,1)S(1)}, u32[]{:S(2)}, u32[]{:S(2)}) collective-permute-start(bf16[520,128]{1,0:T(8,128)(2,1)S(1)} %collective-permute-done.4.refs_4_), channel_id=1, source_target_pairs={{0,1},{1,0},{2,3},{3,2},{4,5},{5,4},{6,7},{7,6},{8,9},{9,8},{10,11... | collective-permute-start | bytes 399368 | tf_op jit(solution)/shard_map/ppermute | solution.py:187
  29.4 6.9 %collective-permute-start.7 = (bf16[520,128]{1,0:T(8,128)(2,1)S(1)}, bf16[520,128]{1,0:T(8,128)(2,1)S(1)}, u32[]{:S(2)}, u32[]{:S(2)}) collective-permute-start(bf16[520,128]{1,0:T(8,128)(2,1)S(1)} %collective-permute-done.6.refs_6_), channel_id=1, source_target_pairs={{0,1},{1,0},{2,3},{3,2},{4,5},{5,4},{6,7},{7,6},{8,9},{9,8},{10,11... | collective-permute-start | bytes 399368 | tf_op jit(solution)/shard_map/ppermute | solution.py:187
  36.3 1.4 %collective-permute-start.1 = (bf16[520,128]{1,0:T(8,128)(2,1)S(1)}, bf16[520,128]{1,0:T(8,128)(2,1)S(1)}, u32[]{:S(2)}, u32[]{:S(2)}) collective-permute-start(bf16[520,128]{1,0:T(8,128)(2,1)S(1)} %collective-permute-done.refs_0_), channel_id=1, source_target_pairs={{0,1},{1,0},{2,3},{3,2},{4,5},{5,4},{6,7},{7,6},{8,9},{9,8},{10,11... | collective-permute-start | bytes 399368 | tf_op jit(solution)/shard_map/ppermute | solution.py:187

commit v10 on v7

--- a/solution.py
+++ b/solution.py
@@ -32,12 +32,13 @@
 
 def block_order(owners):
     half = owners // 2
-    far = list(range(half, owners))
+    quarter = half // 2
+    far = [half + part * quarter + k for k in range(quarter) for part in range(2)]
     near = list(range(half - 1, -1, -1))
     order = far[:2]
-    for block in far[2:]:
-        order += [block, near.pop(0)]
-    return order + near
+    for block in far[2:half - 2]:
+        order += [near.pop(0), block]
+    return order + [far[-2], near.pop(0), far[-1]] + near
 
 
 def place_kernel(owners, capacity, paired, code_ref, place_ref, meta_ref):

time: 45.8 us -> 44.3 us (0.967)
  starting transfers between devices: 26.6 us -> 24.8 us
  waiting for transfers between devices: 4.53 us -> 5.3 us
  blocking collectives: 10.5 us -> 9.94 us
    ppermute x15, starting transfers between devices: 26.6 us -> 24.8 us  [swap(): lax.ppermute(block, 'shard', [(d, d ^ k) for d in range(owners)])]
    ppermute x15, waiting for transfers between devices: 4.53 us -> 5.3 us  [swap(): lax.ppermute(block, 'shard', [(d, d ^ k) for d in range(owners)])]
    all_to_all x1, blocking collectives: 10.5 us -> 9.94 us  [shards(): returned = lax.all_to_all(best, 'shard', 0, 0, tiled=True)]
  transfers between devices with their start and end apart: 15 -> 15, of which waited for: 5 -> 3; matrix products, arithmetic and copies ran while one was open for 0% -> 0% of each run, Pallas kernels for 0% -> 0%
where the time goes in v10:
time: 44.3 us; the launch traced here: 44.1 us
  starting transfers between devices  24.8 us (56%)
  blocking collectives  9.94 us (22%)
  waiting for transfers between devices  5.3 us (12%)
  Pallas kernels  2.54 us (6%)
  local copies, waits for them, and re-layouts  0.71 us (2%)
  other arithmetic  0.7 us (2%)
    ppermute x15, starting transfers between devices, swap(): lax.ppermute(block, 'shard', [(d, d ^ k) for d in range(owners)])  24.8 us
    all_to_all x1, blocking collectives, shards(): returned = lax.all_to_all(best, 'shard', 0, 0, tiled=True)  9.94 us
    ppermute x15, waiting for transfers between devices, swap(): lax.ppermute(block, 'shard', [(d, d ^ k) for d in range(owners)])  5.3 us
    pallas_call x4, Pallas kernels, call(): pl.pallas_call(body, out_shape=shapes, compiler_params=pltpu.CompilerPara...  2.54 us
  transfers between devices with their start and end apart: 15, of which 3 were waited for; matrix products, arithmetic and copies ran while one was open for 0% of the time, Pallas kernels for 0%

profile of v10, /device:TPU:0, one launch (start us, length us, event | category | flops | bytes accessed | tf_op | source)
XLA Modules:
  0.0 44.1 jit_solution(13913611683761812373)
XLA Ops:
  0.0 0.7 %multiply_add_fusion = s32[256]{0:T(256)S(1)} fusion(s32[256]{0:T(256)} %param.5, s32[256]{0:T(256)} %param.4), kind=kLoop, calls=%fused_computation | loop fusion | flops 512 | bytes 3072 | tf_op jit(solution)/shard_map/add | solution.py:203
  0.7 0.0 copy-start
  0.7 0.3 shard_map.37
  1.0 0.7 %copy-done = bf16[256,1024]{1,0:T(8,128)(2,1)S(1)} copy-done((bf16[256,1024]{1,0:T(8,128)(2,1)S(1)}, bf16[256,1024]{1,0:T(8,128)(2,1)}, u32[]{:S(2)}) %copy-start) | copy-done | bytes 524312
  1.7 0.6 %shard_map.38 = (bf16[264,128]{1,0:T(8,128)(2,1)S(1)}, bf16[264,128]{1,0:T(8,128)(2,1)S(1)}, bf16[264,128]{1,0:T(8,128)(2,1)S(1)}, bf16[264,128]{1,0:T(8,128)(2,...) custom-call(bf16[256,1024]{1,0:T(8,128)(2,1)S(1)} %copy-done, ...), custom_call_target="tpu_custom_call" | custom-call | tf_op jit(solution)/shard_map/pallas_call | solution.py:173
  2.3 4.1 %collective-permute-start = (bf16[264,128]{1,0:T(8,128)(2,1)S(1)}, bf16[264,128]{1,0:T(8,128)(2,1)S(1)}, u32[]{:S(2)}, u32[]{:S(2)}) collective-permute-start(bf16[264,128]{1,0:T(8,128)(2,1)S(1)} %get-tuple-element.25), channel_id=1, source_target_pairs={{0,8},{1,9},{2,10},{3,11},{4,12},{5,13},{6,14},{7,15},{8,0},{9,1},... | collective-permute-start | bytes 202760 | tf_op jit(solution)/shard_map/ppermute | solution.py:184
  6.4 1.3 %collective-permute-start.1 = (bf16[264,128]{1,0:T(8,128)(2,1)S(1)}, bf16[264,128]{1,0:T(8,128)(2,1)S(1)}, u32[]{:S(2)}, u32[]{:S(2)}) collective-permute-start(bf16[264,128]{1,0:T(8,128)(2,1)S(1)} %get-tuple-element.26), channel_id=1, source_target_pairs={{0,12},{1,13},{2,14},{3,15},{4,8},{5,9},{6,10},{7,11},{8,4},{9,5},... | collective-permute-start | bytes 202760 | tf_op jit(solution)/shard_map/ppermute | solution.py:184
  7.8 0.3 collective-permute-start.2
  8.1 3.4 %collective-permute-start.3 = (bf16[264,128]{1,0:T(8,128)(2,1)S(1)}, bf16[264,128]{1,0:T(8,128)(2,1)S(1)}, u32[]{:S(2)}, u32[]{:S(2)}) collective-permute-start(bf16[264,128]{1,0:T(8,128)(2,1)S(1)} %get-tuple-element.28), channel_id=1, source_target_pairs={{0,9},{1,8},{2,11},{3,10},{4,13},{5,12},{6,15},{7,14},{8,1},{9,0},... | collective-permute-start | bytes 202760 | tf_op jit(solution)/shard_map/ppermute | solution.py:184
  11.5 0.6 %collective-permute-start.4 = (bf16[264,128]{1,0:T(8,128)(2,1)S(1)}, bf16[264,128]{1,0:T(8,128)(2,1)S(1)}, u32[]{:S(2)}, u32[]{:S(2)}) collective-permute-start(bf16[264,128]{1,0:T(8,128)(2,1)S(1)} %get-tuple-element.29), channel_id=1, source_target_pairs={{0,6},{1,7},{2,4},{3,5},{4,2},{5,3},{6,0},{7,1},{8,14},{9,15},{10,... | collective-permute-start | bytes 202760 | tf_op jit(solution)/shard_map/ppermute | solution.py:184
  12.1 0.0 collective-permute-done.refs_0_
  12.1 2.2 %collective-permute-start.5 = (bf16[264,128]{1,0:T(8,128)(2,1)S(1)}, bf16[264,128]{1,0:T(8,128)(2,1)S(1)}, u32[]{:S(2)}, u32[]{:S(2)}) collective-permute-start(bf16[264,128]{1,0:T(8,128)(2,1)S(1)} %get-tuple-element.30), channel_id=1, source_target_pairs={{0,13},{1,12},{2,15},{3,14},{4,9},{5,8},{6,11},{7,10},{8,5},{9,4},... | collective-permute-start | bytes 202760 | tf_op jit(solution)/shard_map/ppermute | solution.py:184
  14.3 0.0 collective-permute-done.1.refs_1_
  14.4 0.0 collective-permute-start.6
  14.4 0.1 collective-permute-done.2.refs_2_
  14.5 3.9 %collective-permute-start.7 = (bf16[264,128]{1,0:T(8,128)(2,1)S(1)}, bf16[264,128]{1,0:T(8,128)(2,1)S(1)}, u32[]{:S(2)}, u32[]{:S(2)}) collective-permute-start(bf16[264,128]{1,0:T(8,128)(2,1)S(1)} %get-tuple-element.32), channel_id=1, source_target_pairs={{0,10},{1,11},{2,8},{3,9},{4,14},{5,15},{6,12},{7,13},{8,2},{9,3},... | collective-permute-start | bytes 202760 | tf_op jit(solution)/shard_map/ppermute | solution.py:184
  18.4 0.0 collective-permute-done.3.refs_3_
  18.4 1.0 %collective-permute-start.8 = (bf16[264,128]{1,0:T(8,128)(2,1)S(1)}, bf16[264,128]{1,0:T(8,128)(2,1)S(1)}, u32[]{:S(2)}, u32[]{:S(2)}) collective-permute-start(bf16[264,128]{1,0:T(8,128)(2,1)S(1)} %get-tuple-element.33), channel_id=1, source_target_pairs={{0,4},{1,5},{2,6},{3,7},{4,0},{5,1},{6,2},{7,3},{8,12},{9,13},{10,... | collective-permute-start | bytes 202760 | tf_op jit(solution)/shard_map/ppermute | solution.py:184
  19.4 0.0 collective-permute-done.4.refs_4_
  19.4 1.1 %collective-permute-start.9 = (bf16[264,128]{1,0:T(8,128)(2,1)S(1)}, bf16[264,128]{1,0:T(8,128)(2,1)S(1)}, u32[]{:S(2)}, u32[]{:S(2)}) collective-permute-start(bf16[264,128]{1,0:T(8,128)(2,1)S(1)} %get-tuple-element.34), channel_id=1, source_target_pairs={{0,14},{1,15},{2,12},{3,13},{4,10},{5,11},{6,8},{7,9},{8,6},{9,7},... | collective-permute-start | bytes 202760 | tf_op jit(solution)/shard_map/ppermute | solution.py:184
  20.5 0.0 collective-permute-done.5.refs_5_
  20.5 1.6 %collective-permute-start.10 = (bf16[264,128]{1,0:T(8,128)(2,1)S(1)}, bf16[264,128]{1,0:T(8,128)(2,1)S(1)}, u32[]{:S(2)}, u32[]{:S(2)}) collective-permute-start(bf16[264,128]{1,0:T(8,128)(2,1)S(1)} %get-tuple-element.35), channel_id=1, source_target_pairs={{0,11},{1,10},{2,9},{3,8},{4,15},{5,14},{6,13},{7,12},{8,3},{9,2},... | collective-permute-start | bytes 202760 | tf_op jit(solution)/shard_map/ppermute | solution.py:184
  22.1 0.0 collective-permute-done.6.refs_6_
  22.1 1.0 %collective-permute-start.11 = (bf16[264,128]{1,0:T(8,128)(2,1)S(1)}, bf16[264,128]{1,0:T(8,128)(2,1)S(1)}, u32[]{:S(2)}, u32[]{:S(2)}) collective-permute-start(bf16[264,128]{1,0:T(8,128)(2,1)S(1)} %get-tuple-element.36), channel_id=1, source_target_pairs={{0,3},{1,2},{2,1},{3,0},{4,7},{5,6},{6,5},{7,4},{8,11},{9,10},{10,... | collective-permute-start | bytes 202760 | tf_op jit(solution)/shard_map/ppermute | solution.py:184
  23.1 0.0 collective-permute-done.7.refs_7_
  23.1 3.0 %collective-permute-start.12 = (bf16[264,128]{1,0:T(8,128)(2,1)S(1)}, bf16[264,128]{1,0:T(8,128)(2,1)S(1)}, u32[]{:S(2)}, u32[]{:S(2)}) collective-permute-start(bf16[264,128]{1,0:T(8,128)(2,1)S(1)} %get-tuple-element.37), channel_id=1, source_target_pairs={{0,15},{1,14},{2,13},{3,12},{4,11},{5,10},{6,9},{7,8},{8,7},{9,6},... | collective-permute-start | bytes 202760 | tf_op jit(solution)/shard_map/ppermute | solution.py:184
  26.1 0.0 collective-permute-done.8.refs_8_
  26.1 1.1 %collective-permute-start.13 = (bf16[264,128]{1,0:T(8,128)(2,1)S(1)}, bf16[264,128]{1,0:T(8,128)(2,1)S(1)}, u32[]{:S(2)}, u32[]{:S(2)}) collective-permute-start(bf16[264,128]{1,0:T(8,128)(2,1)S(1)} %get-tuple-element.38), channel_id=1, source_target_pairs={{0,2},{1,3},{2,0},{3,1},{4,6},{5,7},{6,4},{7,5},{8,10},{9,11},{10,... | collective-permute-start | bytes 202760 | tf_op jit(solution)/shard_map/ppermute | solution.py:184
  27.2 0.0 collective-permute-done.9.refs_9_
  27.2 0.2 collective-permute-start.14
  27.3 3.8 %collective-permute-done.10.refs_10_ = bf16[264,128]{1,0:T(8,128)(2,1)S(1)} collective-permute-done((bf16[264,128]{1,0:T(8,128)(2,1)S(1)}, bf16[264,128]{1,0:T(8,128)(2,1)S(1)}, u32[]{:S(2)}, u32[]{:S(2)}) %collective-permute-start.10) | collective-permute-done | bytes 67616 | tf_op jit(solution)/shard_map/ppermute | solution.py:184
  31.1 0.0 collective-permute-done.11.refs_11_
  31.1 0.0 collective-permute-done.12.refs_12_
  31.1 1.3 %collective-permute-done.13.refs_13_ = bf16[264,128]{1,0:T(8,128)(2,1)S(1)} collective-permute-done((bf16[264,128]{1,0:T(8,128)(2,1)S(1)}, bf16[264,128]{1,0:T(8,128)(2,1)S(1)}, u32[]{:S(2)}, u32[]{:S(2)}) %collective-permute-start.13) | collective-permute-done | bytes 67616 | tf_op jit(solution)/shard_map/ppermute | solution.py:184
  32.5 0.0 collective-permute-done.14.refs_14_
  32.5 0.9 %shard_map.39 = f32[16,1,128]{2,1,0:T(1,128)S(1)} custom-call(bf16[264,128]{1,0:T(8,128)(2,1)S(1)} %collective-permute-done.refs_0_, bf16[264,128]{1,0:T(8,128)(2,1)S(1)} %collective-permute-done.1.refs_1_, bf16[264,128]{1,0:T(8,128)(2,1)S(1)} %collective-permute-done.2.refs_2_, bf16[264,128]{1,0:T(8,128)(2,1)S(1)} %collective-permute-done.3.refs_3_, ...), custom_call_target="tpu_custom_call" | custom-call | tf_op jit(solution)/shard_map/pallas_call | solution.py:173
  33.4 9.9 %all_to_all.5.refs_0_ = f32[16,1,128]{2,1,0:T(1,128)S(1)} all-to-all(f32[16,1,128]{2,1,0:T(1,128)S(1)} %shard_map.39), channel_id=1, replica_groups=mesh['groups'=2,'shard'=16] {'shard'}, dimensions={0} | all-to-all | bytes 16384 | tf_op jit(solution)/shard_map/all_to_all | solution.py:227
  43.3 0.7 %shard_map.40 = f32[1,256]{1,0:T(1,128)} custom-call(f32[16,1,128]{2,1,0:T(1,128)S(1)} %all_to_all.5.refs_0_, s32[1,256]{1,0:T(1,128)S(1)} %get-tuple-element.23.refs_1_), custom_call_target="tpu_custom_call" | custom-call | tf_op jit(solution)/shard_map/pallas_call | solution.py:173
Async XLA Ops:
  0.7 1.0 %copy-start = (bf16[256,1024]{1,0:T(8,128)(2,1)S(1)}, bf16[256,1024]{1,0:T(8,128)(2,1)}, u32[]{:S(2)}) copy-start(bf16[256,1024]{1,0:T(8,128)(2,1)} %refs_0_.1) | copy-start | bytes 1572868
  2.3 9.8 %collective-permute-start = (bf16[264,128]{1,0:T(8,128)(2,1)S(1)}, bf16[264,128]{1,0:T(8,128)(2,1)S(1)}, u32[]{:S(2)}, u32[]{:S(2)}) collective-permute-start(bf16[264,128]{1,0:T(8,128)(2,1)S(1)} %get-tuple-element.25), channel_id=1, source_target_pairs={{0,8},{1,9},{2,10},{3,11},{4,12},{5,13},{6,14},{7,15},{8,0},{9,1},... | collective-permute-start | bytes 202760 | tf_op jit(solution)/shard_map/ppermute | solution.py:184
  6.4 7.9 %collective-permute-start.1 = (bf16[264,128]{1,0:T(8,128)(2,1)S(1)}, bf16[264,128]{1,0:T(8,128)(2,1)S(1)}, u32[]{:S(2)}, u32[]{:S(2)}) collective-permute-start(bf16[264,128]{1,0:T(8,128)(2,1)S(1)} %get-tuple-element.26), channel_id=1, source_target_pairs={{0,12},{1,13},{2,14},{3,15},{4,8},{5,9},{6,10},{7,11},{8,4},{9,5},... | collective-permute-start | bytes 202760 | tf_op jit(solution)/shard_map/ppermute | solution.py:184
  7.8 6.7 %collective-permute-start.2 = (bf16[264,128]{1,0:T(8,128)(2,1)S(1)}, bf16[264,128]{1,0:T(8,128)(2,1)S(1)}, u32[]{:S(2)}, u32[]{:S(2)}) collective-permute-start(bf16[264,128]{1,0:T(8,128)(2,1)S(1)} %get-tuple-element.27), channel_id=1, source_target_pairs={{0,7},{1,6},{2,5},{3,4},{4,3},{5,2},{6,1},{7,0},{8,15},{9,14},{10,... | collective-permute-start | bytes 202760 | tf_op jit(solution)/shard_map/ppermute | solution.py:184
  8.1 10.3 %collective-permute-start.3 = (bf16[264,128]{1,0:T(8,128)(2,1)S(1)}, bf16[264,128]{1,0:T(8,128)(2,1)S(1)}, u32[]{:S(2)}, u32[]{:S(2)}) collective-permute-start(bf16[264,128]{1,0:T(8,128)(2,1)S(1)} %get-tuple-element.28), channel_id=1, source_target_pairs={{0,9},{1,8},{2,11},{3,10},{4,13},{5,12},{6,15},{7,14},{8,1},{9,0},... | collective-permute-start | bytes 202760 | tf_op jit(solution)/shard_map/ppermute | solution.py:184
  11.5 7.9 %collective-permute-start.4 = (bf16[264,128]{1,0:T(8,128)(2,1)S(1)}, bf16[264,128]{1,0:T(8,128)(2,1)S(1)}, u32[]{:S(2)}, u32[]{:S(2)}) collective-permute-start(bf16[264,128]{1,0:T(8,128)(2,1)S(1)} %get-tuple-element.29), channel_id=1, source_target_pairs={{0,6},{1,7},{2,4},{3,5},{4,2},{5,3},{6,0},{7,1},{8,14},{9,15},{10,... | collective-permute-start | bytes 202760 | tf_op jit(solution)/shard_map/ppermute | solution.py:184
  12.1 8.4 %collective-permute-start.5 = (bf16[264,128]{1,0:T(8,128)(2,1)S(1)}, bf16[264,128]{1,0:T(8,128)(2,1)S(1)}, u32[]{:S(2)}, u32[]{:S(2)}) collective-permute-start(bf16[264,128]{1,0:T(8,128)(2,1)S(1)} %get-tuple-element.30), channel_id=1, source_target_pairs={{0,13},{1,12},{2,15},{3,14},{4,9},{5,8},{6,11},{7,10},{8,5},{9,4},... | collective-permute-start | bytes 202760 | tf_op jit(solution)/shard_map/ppermute | solution.py:184
  14.4 7.7 %collective-permute-start.6 = (bf16[264,128]{1,0:T(8,128)(2,1)S(1)}, bf16[264,128]{1,0:T(8,128)(2,1)S(1)}, u32[]{:S(2)}, u32[]{:S(2)}) collective-permute-start(bf16[264,128]{1,0:T(8,128)(2,1)S(1)} %get-tuple-element.31), channel_id=1, source_target_pairs={{0,5},{1,4},{2,7},{3,6},{4,1},{5,0},{6,3},{7,2},{8,13},{9,12},{10,... | collective-permute-start | bytes 202760 | tf_op jit(solution)/shard_map/ppermute | solution.py:184
  14.5 8.6 %collective-permute-start.7 = (bf16[264,128]{1,0:T(8,128)(2,1)S(1)}, bf16[264,128]{1,0:T(8,128)(2,1)S(1)}, u32[]{:S(2)}, u32[]{:S(2)}) collective-permute-start(bf16[264,128]{1,0:T(8,128)(2,1)S(1)} %get-tuple-element.32), channel_id=1, source_target_pairs={{0,10},{1,11},{2,8},{3,9},{4,14},{5,15},{6,12},{7,13},{8,2},{9,3},... | collective-permute-start | bytes 202760 | tf_op jit(solution)/shard_map/ppermute | solution.py:184
  18.4 7.7 %collective-permute-start.8 = (bf16[264,128]{1,0:T(8,128)(2,1)S(1)}, bf16[264,128]{1,0:T(8,128)(2,1)S(1)}, u32[]{:S(2)}, u32[]{:S(2)}) collective-permute-start(bf16[264,128]{1,0:T(8,128)(2,1)S(1)} %get-tuple-element.33), channel_id=1, source_target_pairs={{0,4},{1,5},{2,6},{3,7},{4,0},{5,1},{6,2},{7,3},{8,12},{9,13},{10,... | collective-permute-start | bytes 202760 | tf_op jit(solution)/shard_map/ppermute | solution.py:184
  19.4 7.8 %collective-permute-start.9 = (bf16[264,128]{1,0:T(8,128)(2,1)S(1)}, bf16[264,128]{1,0:T(8,128)(2,1)S(1)}, u32[]{:S(2)}, u32[]{:S(2)}) collective-permute-start(bf16[264,128]{1,0:T(8,128)(2,1)S(1)} %get-tuple-element.34), channel_id=1, source_target_pairs={{0,14},{1,15},{2,12},{3,13},{4,10},{5,11},{6,8},{7,9},{8,6},{9,7},... | collective-permute-start | bytes 202760 | tf_op jit(solution)/shard_map/ppermute | solution.py:184
  20.5 10.7 %collective-permute-start.10 = (bf16[264,128]{1,0:T(8,128)(2,1)S(1)}, bf16[264,128]{1,0:T(8,128)(2,1)S(1)}, u32[]{:S(2)}, u32[]{:S(2)}) collective-permute-start(bf16[264,128]{1,0:T(8,128)(2,1)S(1)} %get-tuple-element.35), channel_id=1, source_target_pairs={{0,11},{1,10},{2,9},{3,8},{4,15},{5,14},{6,13},{7,12},{8,3},{9,2},... | collective-permute-start | bytes 202760 | tf_op jit(solution)/shard_map/ppermute | solution.py:184
  22.1 9.1 %collective-permute-start.11 = (bf16[264,128]{1,0:T(8,128)(2,1)S(1)}, bf16[264,128]{1,0:T(8,128)(2,1)S(1)}, u32[]{:S(2)}, u32[]{:S(2)}) collective-permute-start(bf16[264,128]{1,0:T(8,128)(2,1)S(1)} %get-tuple-element.36), channel_id=1, source_target_pairs={{0,3},{1,2},{2,1},{3,0},{4,7},{5,6},{6,5},{7,4},{8,11},{9,10},{10,... | collective-permute-start | bytes 202760 | tf_op jit(solution)/shard_map/ppermute | solution.py:184
  23.1 8.1 %collective-permute-start.12 = (bf16[264,128]{1,0:T(8,128)(2,1)S(1)}, bf16[264,128]{1,0:T(8,128)(2,1)S(1)}, u32[]{:S(2)}, u32[]{:S(2)}) collective-permute-start(bf16[264,128]{1,0:T(8,128)(2,1)S(1)} %get-tuple-element.37), channel_id=1, source_target_pairs={{0,15},{1,14},{2,13},{3,12},{4,11},{5,10},{6,9},{7,8},{8,7},{9,6},... | collective-permute-start | bytes 202760 | tf_op jit(solution)/shard_map/ppermute | solution.py:184
  26.1 6.4 %collective-permute-start.13 = (bf16[264,128]{1,0:T(8,128)(2,1)S(1)}, bf16[264,128]{1,0:T(8,128)(2,1)S(1)}, u32[]{:S(2)}, u32[]{:S(2)}) collective-permute-start(bf16[264,128]{1,0:T(8,128)(2,1)S(1)} %get-tuple-element.38), channel_id=1, source_target_pairs={{0,2},{1,3},{2,0},{3,1},{4,6},{5,7},{6,4},{7,5},{8,10},{9,11},{10,... | collective-permute-start | bytes 202760 | tf_op jit(solution)/shard_map/ppermute | solution.py:184
  27.2 5.3 %collective-permute-start.14 = (bf16[264,128]{1,0:T(8,128)(2,1)S(1)}, bf16[264,128]{1,0:T(8,128)(2,1)S(1)}, u32[]{:S(2)}, u32[]{:S(2)}) collective-permute-start(bf16[264,128]{1,0:T(8,128)(2,1)S(1)} %get-tuple-element.39), channel_id=1, source_target_pairs={{0,1},{1,0},{2,3},{3,2},{4,5},{5,4},{6,7},{7,6},{8,9},{9,8},{10,11... | collective-permute-start | bytes 202760 | tf_op jit(solution)/shard_map/ppermute | solution.py:184

commit v11 on v10

--- a/solution.py
+++ b/solution.py
@@ -36,9 +36,10 @@
     far = [half + part * quarter + k for k in range(quarter) for part in range(2)]
     near = list(range(half - 1, -1, -1))
     order = far[:2]
-    for block in far[2:half - 2]:
-        order += [near.pop(0), block]
-    return order + [far[-2], near.pop(0), far[-1]] + near
+    for place in range(2, owners):
+        crosses = place in (2, 4, 6, 7, 9, 11)
+        order.append(far[sum(block >= half for block in order)] if crosses else near.pop(0))
+    return order
 
 
 def place_kernel(owners, capacity, paired, code_ref, place_ref, meta_ref):

time: 44.3 us -> 46.1 us (1.041)
  waiting for transfers between devices: 5.3 us -> 6.86 us
    ppermute x15, waiting for transfers between devices: 5.3 us -> 6.86 us  [swap(): lax.ppermute(block, 'shard', [(d, d ^ k) for d in range(owners)])]
  transfers between devices with their start and end apart: 15 -> 15, of which waited for: 3 -> 7; matrix products, arithmetic and copies ran while one was open for 0% -> 0% of each run, Pallas kernels for 0% -> 0%
where the time goes in v11:
time: 46.1 us; the launch traced here: 45.9 us
  starting transfers between devices  25 us (54%)
  blocking collectives  10 us (22%)
  waiting for transfers between devices  6.86 us (15%)
  Pallas kernels  2.53 us (5%)
  local copies, waits for them, and re-layouts  0.71 us (2%)
  other arithmetic  0.7 us (2%)
    ppermute x15, starting transfers between devices, swap(): lax.ppermute(block, 'shard', [(d, d ^ k) for d in range(owners)])  25 us
    all_to_all x1, blocking collectives, shards(): returned = lax.all_to_all(best, 'shard', 0, 0, tiled=True)  10 us
    ppermute x15, waiting for transfers between devices, swap(): lax.ppermute(block, 'shard', [(d, d ^ k) for d in range(owners)])  6.86 us
    pallas_call x4, Pallas kernels, call(): pl.pallas_call(body, out_shape=shapes, compiler_params=pltpu.CompilerPara...  2.53 us
  transfers between devices with their start and end apart: 15, of which 7 were waited for; matrix products, arithmetic and copies ran while one was open for 0% of the time, Pallas kernels for 0%

profile of v11, /device:TPU:0, one launch (start us, length us, event | category | flops | bytes accessed | tf_op | source)
XLA Modules:
  0.0 45.9 jit_solution(7586460257729270598)
XLA Ops:
  0.0 0.7 %multiply_add_fusion = s32[256]{0:T(256)S(1)} fusion(s32[256]{0:T(256)} %param.5, s32[256]{0:T(256)} %param.4), kind=kLoop, calls=%fused_computation | loop fusion | flops 512 | bytes 3072 | tf_op jit(solution)/shard_map/add | solution.py:204
  0.7 0.0 copy-start
  0.7 0.3 shard_map.37
  1.0 0.7 %copy-done = bf16[256,1024]{1,0:T(8,128)(2,1)S(1)} copy-done((bf16[256,1024]{1,0:T(8,128)(2,1)S(1)}, bf16[256,1024]{1,0:T(8,128)(2,1)}, u32[]{:S(2)}) %copy-start) | copy-done | bytes 524312
  1.7 0.6 %shard_map.38 = (bf16[264,128]{1,0:T(8,128)(2,1)S(1)}, bf16[264,128]{1,0:T(8,128)(2,1)S(1)}, bf16[264,128]{1,0:T(8,128)(2,1)S(1)}, bf16[264,128]{1,0:T(8,128)(2,...) custom-call(bf16[256,1024]{1,0:T(8,128)(2,1)S(1)} %copy-done, ...), custom_call_target="tpu_custom_call" | custom-call | tf_op jit(solution)/shard_map/pallas_call | solution.py:174
  2.3 4.1 %collective-permute-start = (bf16[264,128]{1,0:T(8,128)(2,1)S(1)}, bf16[264,128]{1,0:T(8,128)(2,1)S(1)}, u32[]{:S(2)}, u32[]{:S(2)}) collective-permute-start(bf16[264,128]{1,0:T(8,128)(2,1)S(1)} %get-tuple-element.25), channel_id=1, source_target_pairs={{0,8},{1,9},{2,10},{3,11},{4,12},{5,13},{6,14},{7,15},{8,0},{9,1},... | collective-permute-start | bytes 202760 | tf_op jit(solution)/shard_map/ppermute | solution.py:185
  6.4 1.3 %collective-permute-start.1 = (bf16[264,128]{1,0:T(8,128)(2,1)S(1)}, bf16[264,128]{1,0:T(8,128)(2,1)S(1)}, u32[]{:S(2)}, u32[]{:S(2)}) collective-permute-start(bf16[264,128]{1,0:T(8,128)(2,1)S(1)} %get-tuple-element.26), channel_id=1, source_target_pairs={{0,12},{1,13},{2,14},{3,15},{4,8},{5,9},{6,10},{7,11},{8,4},{9,5},... | collective-permute-start | bytes 202760 | tf_op jit(solution)/shard_map/ppermute | solution.py:185
  7.8 0.6 %collective-permute-start.2 = (bf16[264,128]{1,0:T(8,128)(2,1)S(1)}, bf16[264,128]{1,0:T(8,128)(2,1)S(1)}, u32[]{:S(2)}, u32[]{:S(2)}) collective-permute-start(bf16[264,128]{1,0:T(8,128)(2,1)S(1)} %get-tuple-element.27), channel_id=1, source_target_pairs={{0,9},{1,8},{2,11},{3,10},{4,13},{5,12},{6,15},{7,14},{8,1},{9,0},... | collective-permute-start | bytes 202760 | tf_op jit(solution)/shard_map/ppermute | solution.py:185
  8.4 3.1 %collective-permute-start.3 = (bf16[264,128]{1,0:T(8,128)(2,1)S(1)}, bf16[264,128]{1,0:T(8,128)(2,1)S(1)}, u32[]{:S(2)}, u32[]{:S(2)}) collective-permute-start(bf16[264,128]{1,0:T(8,128)(2,1)S(1)} %get-tuple-element.28), channel_id=1, source_target_pairs={{0,7},{1,6},{2,5},{3,4},{4,3},{5,2},{6,1},{7,0},{8,15},{9,14},{10,... | collective-permute-start | bytes 202760 | tf_op jit(solution)/shard_map/ppermute | solution.py:185
  11.5 0.2 collective-permute-start.4
  11.8 0.0 collective-permute-done.refs_0_
  11.8 3.2 %collective-permute-start.5 = (bf16[264,128]{1,0:T(8,128)(2,1)S(1)}, bf16[264,128]{1,0:T(8,128)(2,1)S(1)}, u32[]{:S(2)}, u32[]{:S(2)}) collective-permute-start(bf16[264,128]{1,0:T(8,128)(2,1)S(1)} %get-tuple-element.30), channel_id=1, source_target_pairs={{0,6},{1,7},{2,4},{3,5},{4,2},{5,3},{6,0},{7,1},{8,14},{9,15},{10,... | collective-permute-start | bytes 202760 | tf_op jit(solution)/shard_map/ppermute | solution.py:185
  15.0 0.0 collective-permute-done.1.refs_1_
  15.0 4.8 %collective-permute-start.6 = (bf16[264,128]{1,0:T(8,128)(2,1)S(1)}, bf16[264,128]{1,0:T(8,128)(2,1)S(1)}, u32[]{:S(2)}, u32[]{:S(2)}) collective-permute-start(bf16[264,128]{1,0:T(8,128)(2,1)S(1)} %get-tuple-element.31), channel_id=1, source_target_pairs={{0,10},{1,11},{2,8},{3,9},{4,14},{5,15},{6,12},{7,13},{8,2},{9,3},... | collective-permute-start | bytes 202760 | tf_op jit(solution)/shard_map/ppermute | solution.py:185
  19.8 0.0 collective-permute-done.2.refs_2_
  19.8 1.7 %collective-permute-start.7 = (bf16[264,128]{1,0:T(8,128)(2,1)S(1)}, bf16[264,128]{1,0:T(8,128)(2,1)S(1)}, u32[]{:S(2)}, u32[]{:S(2)}) collective-permute-start(bf16[264,128]{1,0:T(8,128)(2,1)S(1)} %get-tuple-element.32), channel_id=1, source_target_pairs={{0,14},{1,15},{2,12},{3,13},{4,10},{5,11},{6,8},{7,9},{8,6},{9,7},... | collective-permute-start | bytes 202760 | tf_op jit(solution)/shard_map/ppermute | solution.py:185
  21.5 0.0 collective-permute-done.3.refs_3_
  21.5 0.0 collective-permute-start.8
  21.5 0.0 collective-permute-done.4.refs_4_
  21.5 3.3 %collective-permute-start.9 = (bf16[264,128]{1,0:T(8,128)(2,1)S(1)}, bf16[264,128]{1,0:T(8,128)(2,1)S(1)}, u32[]{:S(2)}, u32[]{:S(2)}) collective-permute-start(bf16[264,128]{1,0:T(8,128)(2,1)S(1)} %get-tuple-element.34), channel_id=1, source_target_pairs={{0,11},{1,10},{2,9},{3,8},{4,15},{5,14},{6,13},{7,12},{8,3},{9,2},... | collective-permute-start | bytes 202760 | tf_op jit(solution)/shard_map/ppermute | solution.py:185
  24.8 0.0 collective-permute-done.5.refs_5_
  24.8 0.0 collective-permute-start.10
  24.8 0.0 collective-permute-done.6.refs_6_
  24.8 1.6 %collective-permute-start.11 = (bf16[264,128]{1,0:T(8,128)(2,1)S(1)}, bf16[264,128]{1,0:T(8,128)(2,1)S(1)}, u32[]{:S(2)}, u32[]{:S(2)}) collective-permute-start(bf16[264,128]{1,0:T(8,128)(2,1)S(1)} %get-tuple-element.36), channel_id=1, source_target_pairs={{0,15},{1,14},{2,13},{3,12},{4,11},{5,10},{6,9},{7,8},{8,7},{9,6},... | collective-permute-start | bytes 202760 | tf_op jit(solution)/shard_map/ppermute | solution.py:185
  26.4 0.5 %collective-permute-done.7.refs_7_ = bf16[264,128]{1,0:T(8,128)(2,1)S(1)} collective-permute-done((bf16[264,128]{1,0:T(8,128)(2,1)S(1)}, bf16[264,128]{1,0:T(8,128)(2,1)S(1)}, u32[]{:S(2)}, u32[]{:S(2)}) %collective-permute-start.7) | collective-permute-done | bytes 67616 | tf_op jit(solution)/shard_map/ppermute | solution.py:185
  26.9 0.0 collective-permute-start.12
  26.9 0.6 %collective-permute-done.8.refs_8_ = bf16[264,128]{1,0:T(8,128)(2,1)S(1)} collective-permute-done((bf16[264,128]{1,0:T(8,128)(2,1)S(1)}, bf16[264,128]{1,0:T(8,128)(2,1)S(1)}, u32[]{:S(2)}, u32[]{:S(2)}) %collective-permute-start.8) | collective-permute-done | bytes 67616 | tf_op jit(solution)/shard_map/ppermute | solution.py:185
  27.5 1.0 %collective-permute-start.13 = (bf16[264,128]{1,0:T(8,128)(2,1)S(1)}, bf16[264,128]{1,0:T(8,128)(2,1)S(1)}, u32[]{:S(2)}, u32[]{:S(2)}) collective-permute-start(bf16[264,128]{1,0:T(8,128)(2,1)S(1)} %get-tuple-element.38), channel_id=1, source_target_pairs={{0,2},{1,3},{2,0},{3,1},{4,6},{5,7},{6,4},{7,5},{8,10},{9,11},{10,... | collective-permute-start | bytes 202760 | tf_op jit(solution)/shard_map/ppermute | solution.py:185
  28.5 1.3 %collective-permute-done.9.refs_9_ = bf16[264,128]{1,0:T(8,128)(2,1)S(1)} collective-permute-done((bf16[264,128]{1,0:T(8,128)(2,1)S(1)}, bf16[264,128]{1,0:T(8,128)(2,1)S(1)}, u32[]{:S(2)}, u32[]{:S(2)}) %collective-permute-start.9) | collective-permute-done | bytes 67616 | tf_op jit(solution)/shard_map/ppermute | solution.py:185
  29.8 0.0 collective-permute-start.14
  29.8 0.1 collective-permute-done.10.refs_10_
  29.9 2.0 %collective-permute-done.11.refs_11_ = bf16[264,128]{1,0:T(8,128)(2,1)S(1)} collective-permute-done((bf16[264,128]{1,0:T(8,128)(2,1)S(1)}, bf16[264,128]{1,0:T(8,128)(2,1)S(1)}, u32[]{:S(2)}, u32[]{:S(2)}) %collective-permute-start.11) | collective-permute-done | bytes 67616 | tf_op jit(solution)/shard_map/ppermute | solution.py:185
  31.9 0.9 %collective-permute-done.12.refs_12_ = bf16[264,128]{1,0:T(8,128)(2,1)S(1)} collective-permute-done((bf16[264,128]{1,0:T(8,128)(2,1)S(1)}, bf16[264,128]{1,0:T(8,128)(2,1)S(1)}, u32[]{:S(2)}, u32[]{:S(2)}) %collective-permute-start.12) | collective-permute-done | bytes 67616 | tf_op jit(solution)/shard_map/ppermute | solution.py:185
  32.8 1.5 %collective-permute-done.13.refs_13_ = bf16[264,128]{1,0:T(8,128)(2,1)S(1)} collective-permute-done((bf16[264,128]{1,0:T(8,128)(2,1)S(1)}, bf16[264,128]{1,0:T(8,128)(2,1)S(1)}, u32[]{:S(2)}, u32[]{:S(2)}) %collective-permute-start.13) | collective-permute-done | bytes 67616 | tf_op jit(solution)/shard_map/ppermute | solution.py:185
  34.3 0.0 collective-permute-done.14.refs_14_
  34.3 0.9 %shard_map.39 = f32[16,1,128]{2,1,0:T(1,128)S(1)} custom-call(bf16[264,128]{1,0:T(8,128)(2,1)S(1)} %collective-permute-done.refs_0_, bf16[264,128]{1,0:T(8,128)(2,1)S(1)} %collective-permute-done.1.refs_1_, bf16[264,128]{1,0:T(8,128)(2,1)S(1)} %collective-permute-done.2.refs_2_, bf16[264,128]{1,0:T(8,128)(2,1)S(1)} %collective-permute-done.3.refs_3_, ...), custom_call_target="tpu_custom_call" | custom-call | tf_op jit(solution)/shard_map/pallas_call | solution.py:174
  35.1 10.0 %all_to_all.5.refs_0_ = f32[16,1,128]{2,1,0:T(1,128)S(1)} all-to-all(f32[16,1,128]{2,1,0:T(1,128)S(1)} %shard_map.39), channel_id=1, replica_groups=mesh['groups'=2,'shard'=16] {'shard'}, dimensions={0} | all-to-all | bytes 16384 | tf_op jit(solution)/shard_map/all_to_all | solution.py:228
  45.2 0.7 %shard_map.40 = f32[1,256]{1,0:T(1,128)} custom-call(f32[16,1,128]{2,1,0:T(1,128)S(1)} %all_to_all.5.refs_0_, s32[1,256]{1,0:T(1,128)S(1)} %get-tuple-element.23.refs_1_), custom_call_target="tpu_custom_call" | custom-call | tf_op jit(solution)/shard_map/pallas_call | solution.py:174
Async XLA Ops:
  0.7 1.0 %copy-start = (bf16[256,1024]{1,0:T(8,128)(2,1)S(1)}, bf16[256,1024]{1,0:T(8,128)(2,1)}, u32[]{:S(2)}) copy-start(bf16[256,1024]{1,0:T(8,128)(2,1)} %refs_0_.1) | copy-start | bytes 1572868
  2.3 9.4 %collective-permute-start = (bf16[264,128]{1,0:T(8,128)(2,1)S(1)}, bf16[264,128]{1,0:T(8,128)(2,1)S(1)}, u32[]{:S(2)}, u32[]{:S(2)}) collective-permute-start(bf16[264,128]{1,0:T(8,128)(2,1)S(1)} %get-tuple-element.25), channel_id=1, source_target_pairs={{0,8},{1,9},{2,10},{3,11},{4,12},{5,13},{6,14},{7,15},{8,0},{9,1},... | collective-permute-start | bytes 202760 | tf_op jit(solution)/shard_map/ppermute | solution.py:185
  6.4 8.5 %collective-permute-start.1 = (bf16[264,128]{1,0:T(8,128)(2,1)S(1)}, bf16[264,128]{1,0:T(8,128)(2,1)S(1)}, u32[]{:S(2)}, u32[]{:S(2)}) collective-permute-start(bf16[264,128]{1,0:T(8,128)(2,1)S(1)} %get-tuple-element.26), channel_id=1, source_target_pairs={{0,12},{1,13},{2,14},{3,15},{4,8},{5,9},{6,10},{7,11},{8,4},{9,5},... | collective-permute-start | bytes 202760 | tf_op jit(solution)/shard_map/ppermute | solution.py:185
  7.8 12.0 %collective-permute-start.2 = (bf16[264,128]{1,0:T(8,128)(2,1)S(1)}, bf16[264,128]{1,0:T(8,128)(2,1)S(1)}, u32[]{:S(2)}, u32[]{:S(2)}) collective-permute-start(bf16[264,128]{1,0:T(8,128)(2,1)S(1)} %get-tuple-element.27), channel_id=1, source_target_pairs={{0,9},{1,8},{2,11},{3,10},{4,13},{5,12},{6,15},{7,14},{8,1},{9,0},... | collective-permute-start | bytes 202760 | tf_op jit(solution)/shard_map/ppermute | solution.py:185
  8.4 13.1 %collective-permute-start.3 = (bf16[264,128]{1,0:T(8,128)(2,1)S(1)}, bf16[264,128]{1,0:T(8,128)(2,1)S(1)}, u32[]{:S(2)}, u32[]{:S(2)}) collective-permute-start(bf16[264,128]{1,0:T(8,128)(2,1)S(1)} %get-tuple-element.28), channel_id=1, source_target_pairs={{0,7},{1,6},{2,5},{3,4},{4,3},{5,2},{6,1},{7,0},{8,15},{9,14},{10,... | collective-permute-start | bytes 202760 | tf_op jit(solution)/shard_map/ppermute | solution.py:185
  11.5 10.0 %collective-permute-start.4 = (bf16[264,128]{1,0:T(8,128)(2,1)S(1)}, bf16[264,128]{1,0:T(8,128)(2,1)S(1)}, u32[]{:S(2)}, u32[]{:S(2)}) collective-permute-start(bf16[264,128]{1,0:T(8,128)(2,1)S(1)} %get-tuple-element.29), channel_id=1, source_target_pairs={{0,13},{1,12},{2,15},{3,14},{4,9},{5,8},{6,11},{7,10},{8,5},{9,4},... | collective-permute-start | bytes 202760 | tf_op jit(solution)/shard_map/ppermute | solution.py:185
  11.8 13.1 %collective-permute-start.5 = (bf16[264,128]{1,0:T(8,128)(2,1)S(1)}, bf16[264,128]{1,0:T(8,128)(2,1)S(1)}, u32[]{:S(2)}, u32[]{:S(2)}) collective-permute-start(bf16[264,128]{1,0:T(8,128)(2,1)S(1)} %get-tuple-element.30), channel_id=1, source_target_pairs={{0,6},{1,7},{2,4},{3,5},{4,2},{5,3},{6,0},{7,1},{8,14},{9,15},{10,... | collective-permute-start | bytes 202760 | tf_op jit(solution)/shard_map/ppermute | solution.py:185
  15.0 9.8 %collective-permute-start.6 = (bf16[264,128]{1,0:T(8,128)(2,1)S(1)}, bf16[264,128]{1,0:T(8,128)(2,1)S(1)}, u32[]{:S(2)}, u32[]{:S(2)}) collective-permute-start(bf16[264,128]{1,0:T(8,128)(2,1)S(1)} %get-tuple-element.31), channel_id=1, source_target_pairs={{0,10},{1,11},{2,8},{3,9},{4,14},{5,15},{6,12},{7,13},{8,2},{9,3},... | collective-permute-start | bytes 202760 | tf_op jit(solution)/shard_map/ppermute | solution.py:185
  19.8 7.1 %collective-permute-start.7 = (bf16[264,128]{1,0:T(8,128)(2,1)S(1)}, bf16[264,128]{1,0:T(8,128)(2,1)S(1)}, u32[]{:S(2)}, u32[]{:S(2)}) collective-permute-start(bf16[264,128]{1,0:T(8,128)(2,1)S(1)} %get-tuple-element.32), channel_id=1, source_target_pairs={{0,14},{1,15},{2,12},{3,13},{4,10},{5,11},{6,8},{7,9},{8,6},{9,7},... | collective-permute-start | bytes 202760 | tf_op jit(solution)/shard_map/ppermute | solution.py:185
  21.5 6.0 %collective-permute-start.8 = (bf16[264,128]{1,0:T(8,128)(2,1)S(1)}, bf16[264,128]{1,0:T(8,128)(2,1)S(1)}, u32[]{:S(2)}, u32[]{:S(2)}) collective-permute-start(bf16[264,128]{1,0:T(8,128)(2,1)S(1)} %get-tuple-element.33), channel_id=1, source_target_pairs={{0,5},{1,4},{2,7},{3,6},{4,1},{5,0},{6,3},{7,2},{8,13},{9,12},{10,... | collective-permute-start | bytes 202760 | tf_op jit(solution)/shard_map/ppermute | solution.py:185
  21.5 8.3 %collective-permute-start.9 = (bf16[264,128]{1,0:T(8,128)(2,1)S(1)}, bf16[264,128]{1,0:T(8,128)(2,1)S(1)}, u32[]{:S(2)}, u32[]{:S(2)}) collective-permute-start(bf16[264,128]{1,0:T(8,128)(2,1)S(1)} %get-tuple-element.34), channel_id=1, source_target_pairs={{0,11},{1,10},{2,9},{3,8},{4,15},{5,14},{6,13},{7,12},{8,3},{9,2},... | collective-permute-start | bytes 202760 | tf_op jit(solution)/shard_map/ppermute | solution.py:185
  24.8 5.1 %collective-permute-start.10 = (bf16[264,128]{1,0:T(8,128)(2,1)S(1)}, bf16[264,128]{1,0:T(8,128)(2,1)S(1)}, u32[]{:S(2)}, u32[]{:S(2)}) collective-permute-start(bf16[264,128]{1,0:T(8,128)(2,1)S(1)} %get-tuple-element.35), channel_id=1, source_target_pairs={{0,4},{1,5},{2,6},{3,7},{4,0},{5,1},{6,2},{7,3},{8,12},{9,13},{10,... | collective-permute-start | bytes 202760 | tf_op jit(solution)/shard_map/ppermute | solution.py:185
  24.8 7.1 %collective-permute-start.11 = (bf16[264,128]{1,0:T(8,128)(2,1)S(1)}, bf16[264,128]{1,0:T(8,128)(2,1)S(1)}, u32[]{:S(2)}, u32[]{:S(2)}) collective-permute-start(bf16[264,128]{1,0:T(8,128)(2,1)S(1)} %get-tuple-element.36), channel_id=1, source_target_pairs={{0,15},{1,14},{2,13},{3,12},{4,11},{5,10},{6,9},{7,8},{8,7},{9,6},... | collective-permute-start | bytes 202760 | tf_op jit(solution)/shard_map/ppermute | solution.py:185
  26.9 5.9 %collective-permute-start.12 = (bf16[264,128]{1,0:T(8,128)(2,1)S(1)}, bf16[264,128]{1,0:T(8,128)(2,1)S(1)}, u32[]{:S(2)}, u32[]{:S(2)}) collective-permute-start(bf16[264,128]{1,0:T(8,128)(2,1)S(1)} %get-tuple-element.37), channel_id=1, source_target_pairs={{0,3},{1,2},{2,1},{3,0},{4,7},{5,6},{6,5},{7,4},{8,11},{9,10},{10,... | collective-permute-start | bytes 202760 | tf_op jit(solution)/shard_map/ppermute | solution.py:185
  27.5 6.8 %collective-permute-start.13 = (bf16[264,128]{1,0:T(8,128)(2,1)S(1)}, bf16[264,128]{1,0:T(8,128)(2,1)S(1)}, u32[]{:S(2)}, u32[]{:S(2)}) collective-permute-start(bf16[264,128]{1,0:T(8,128)(2,1)S(1)} %get-tuple-element.38), channel_id=1, source_target_pairs={{0,2},{1,3},{2,0},{3,1},{4,6},{5,7},{6,4},{7,5},{8,10},{9,11},{10,... | collective-permute-start | bytes 202760 | tf_op jit(solution)/shard_map/ppermute | solution.py:185
  29.8 4.5 %collective-permute-start.14 = (bf16[264,128]{1,0:T(8,128)(2,1)S(1)}, bf16[264,128]{1,0:T(8,128)(2,1)S(1)}, u32[]{:S(2)}, u32[]{:S(2)}) collective-permute-start(bf16[264,128]{1,0:T(8,128)(2,1)S(1)} %get-tuple-element.39), channel_id=1, source_target_pairs={{0,1},{1,0},{2,3},{3,2},{4,5},{5,4},{6,7},{7,6},{8,9},{9,8},{10,11... | collective-permute-start | bytes 202760 | tf_op jit(solution)/shard_map/ppermute | solution.py:185

commit v12 on v10

--- a/solution.py
+++ b/solution.py
@@ -36,9 +36,9 @@
     far = [half + part * quarter + k for k in range(quarter) for part in range(2)]
     near = list(range(half - 1, -1, -1))
     order = far[:2]
-    for block in far[2:half - 2]:
+    for block in far[2:]:
         order += [near.pop(0), block]
-    return order + [far[-2], near.pop(0), far[-1]] + near
+    return order + near
 
 
 def place_kernel(owners, capacity, paired, code_ref, place_ref, meta_ref):

time: 44.3 us -> 44.1 us (level)
  waiting for transfers between devices: 5.3 us -> 4.02 us
  blocking collectives: 9.94 us -> 10.9 us
    ppermute x15, waiting for transfers between devices: 5.3 us -> 4.02 us  [swap(): lax.ppermute(block, 'shard', [(d, d ^ k) for d in range(owners)])]
    all_to_all x1, blocking collectives: 9.94 us -> 10.9 us  [shards(): returned = lax.all_to_all(best, 'shard', 0, 0, tiled=True)]
  transfers between devices with their start and end apart: 15 -> 15, of which waited for: 3 -> 4; matrix products, arithmetic and copies ran while one was open for 0% -> 0% of each run, Pallas kernels for 0% -> 0%
where the time goes in v12:
time: 44.1 us; the launch traced here: 43.9 us
  starting transfers between devices  25 us (57%)
  blocking collectives  10.9 us (25%)
  waiting for transfers between devices  4.02 us (9%)
  Pallas kernels  2.54 us (6%)
  local copies, waits for them, and re-layouts  0.71 us (2%)
  other arithmetic  0.7 us (2%)
    ppermute x15, starting transfers between devices, swap(): lax.ppermute(block, 'shard', [(d, d ^ k) for d in range(owners)])  25 us
    all_to_all x1, blocking collectives, shards(): returned = lax.all_to_all(best, 'shard', 0, 0, tiled=True)  10.9 us
    ppermute x15, waiting for transfers between devices, swap(): lax.ppermute(block, 'shard', [(d, d ^ k) for d in range(owners)])  4.02 us
    pallas_call x4, Pallas kernels, call(): pl.pallas_call(body, out_shape=shapes, compiler_params=pltpu.CompilerPara...  2.54 us
  transfers between devices with their start and end apart: 15, of which 4 were waited for; matrix products, arithmetic and copies ran while one was open for 0% of the time, Pallas kernels for 0%

profile of v12, /device:TPU:0, one launch (start us, length us, event | category | flops | bytes accessed | tf_op | source)
XLA Modules:
  0.0 43.9 jit_solution(5050716976719661436)
XLA Ops:
  0.0 0.7 %multiply_add_fusion = s32[256]{0:T(256)S(1)} fusion(s32[256]{0:T(256)} %param.5, s32[256]{0:T(256)} %param.4), kind=kLoop, calls=%fused_computation | loop fusion | flops 512 | bytes 3072 | tf_op jit(solution)/shard_map/add | solution.py:203
  0.7 0.0 copy-start
  0.7 0.3 shard_map.37
  1.0 0.7 %copy-done = bf16[256,1024]{1,0:T(8,128)(2,1)S(1)} copy-done((bf16[256,1024]{1,0:T(8,128)(2,1)S(1)}, bf16[256,1024]{1,0:T(8,128)(2,1)}, u32[]{:S(2)}) %copy-start) | copy-done | bytes 524312
  1.7 0.6 %shard_map.38 = (bf16[264,128]{1,0:T(8,128)(2,1)S(1)}, bf16[264,128]{1,0:T(8,128)(2,1)S(1)}, bf16[264,128]{1,0:T(8,128)(2,1)S(1)}, bf16[264,128]{1,0:T(8,128)(2,...) custom-call(bf16[256,1024]{1,0:T(8,128)(2,1)S(1)} %copy-done, ...), custom_call_target="tpu_custom_call" | custom-call | tf_op jit(solution)/shard_map/pallas_call | solution.py:173
  2.3 4.1 %collective-permute-start = (bf16[264,128]{1,0:T(8,128)(2,1)S(1)}, bf16[264,128]{1,0:T(8,128)(2,1)S(1)}, u32[]{:S(2)}, u32[]{:S(2)}) collective-permute-start(bf16[264,128]{1,0:T(8,128)(2,1)S(1)} %get-tuple-element.25), channel_id=1, source_target_pairs={{0,8},{1,9},{2,10},{3,11},{4,12},{5,13},{6,14},{7,15},{8,0},{9,1},... | collective-permute-start | bytes 202760 | tf_op jit(solution)/shard_map/ppermute | solution.py:184
  6.4 1.3 %collective-permute-start.1 = (bf16[264,128]{1,0:T(8,128)(2,1)S(1)}, bf16[264,128]{1,0:T(8,128)(2,1)S(1)}, u32[]{:S(2)}, u32[]{:S(2)}) collective-permute-start(bf16[264,128]{1,0:T(8,128)(2,1)S(1)} %get-tuple-element.26), channel_id=1, source_target_pairs={{0,12},{1,13},{2,14},{3,15},{4,8},{5,9},{6,10},{7,11},{8,4},{9,5},... | collective-permute-start | bytes 202760 | tf_op jit(solution)/shard_map/ppermute | solution.py:184
  7.8 0.3 collective-permute-start.2
  8.1 3.4 %collective-permute-start.3 = (bf16[264,128]{1,0:T(8,128)(2,1)S(1)}, bf16[264,128]{1,0:T(8,128)(2,1)S(1)}, u32[]{:S(2)}, u32[]{:S(2)}) collective-permute-start(bf16[264,128]{1,0:T(8,128)(2,1)S(1)} %get-tuple-element.28), channel_id=1, source_target_pairs={{0,9},{1,8},{2,11},{3,10},{4,13},{5,12},{6,15},{7,14},{8,1},{9,0},... | collective-permute-start | bytes 202760 | tf_op jit(solution)/shard_map/ppermute | solution.py:184
  11.5 0.6 %collective-permute-start.4 = (bf16[264,128]{1,0:T(8,128)(2,1)S(1)}, bf16[264,128]{1,0:T(8,128)(2,1)S(1)}, u32[]{:S(2)}, u32[]{:S(2)}) collective-permute-start(bf16[264,128]{1,0:T(8,128)(2,1)S(1)} %get-tuple-element.29), channel_id=1, source_target_pairs={{0,6},{1,7},{2,4},{3,5},{4,2},{5,3},{6,0},{7,1},{8,14},{9,15},{10,... | collective-permute-start | bytes 202760 | tf_op jit(solution)/shard_map/ppermute | solution.py:184
  12.1 0.0 collective-permute-done.refs_0_
  12.1 2.2 %collective-permute-start.5 = (bf16[264,128]{1,0:T(8,128)(2,1)S(1)}, bf16[264,128]{1,0:T(8,128)(2,1)S(1)}, u32[]{:S(2)}, u32[]{:S(2)}) collective-permute-start(bf16[264,128]{1,0:T(8,128)(2,1)S(1)} %get-tuple-element.30), channel_id=1, source_target_pairs={{0,13},{1,12},{2,15},{3,14},{4,9},{5,8},{6,11},{7,10},{8,5},{9,4},... | collective-permute-start | bytes 202760 | tf_op jit(solution)/shard_map/ppermute | solution.py:184
  14.3 0.0 collective-permute-done.1.refs_1_
  14.4 0.0 collective-permute-start.6
  14.4 0.1 collective-permute-done.2.refs_2_
  14.5 3.9 %collective-permute-start.7 = (bf16[264,128]{1,0:T(8,128)(2,1)S(1)}, bf16[264,128]{1,0:T(8,128)(2,1)S(1)}, u32[]{:S(2)}, u32[]{:S(2)}) collective-permute-start(bf16[264,128]{1,0:T(8,128)(2,1)S(1)} %get-tuple-element.32), channel_id=1, source_target_pairs={{0,10},{1,11},{2,8},{3,9},{4,14},{5,15},{6,12},{7,13},{8,2},{9,3},... | collective-permute-start | bytes 202760 | tf_op jit(solution)/shard_map/ppermute | solution.py:184
  18.4 0.0 collective-permute-done.3.refs_3_
  18.4 1.0 %collective-permute-start.8 = (bf16[264,128]{1,0:T(8,128)(2,1)S(1)}, bf16[264,128]{1,0:T(8,128)(2,1)S(1)}, u32[]{:S(2)}, u32[]{:S(2)}) collective-permute-start(bf16[264,128]{1,0:T(8,128)(2,1)S(1)} %get-tuple-element.33), channel_id=1, source_target_pairs={{0,4},{1,5},{2,6},{3,7},{4,0},{5,1},{6,2},{7,3},{8,12},{9,13},{10,... | collective-permute-start | bytes 202760 | tf_op jit(solution)/shard_map/ppermute | solution.py:184
  19.4 0.0 collective-permute-done.4.refs_4_
  19.4 1.1 %collective-permute-start.9 = (bf16[264,128]{1,0:T(8,128)(2,1)S(1)}, bf16[264,128]{1,0:T(8,128)(2,1)S(1)}, u32[]{:S(2)}, u32[]{:S(2)}) collective-permute-start(bf16[264,128]{1,0:T(8,128)(2,1)S(1)} %get-tuple-element.34), channel_id=1, source_target_pairs={{0,14},{1,15},{2,12},{3,13},{4,10},{5,11},{6,8},{7,9},{8,6},{9,7},... | collective-permute-start | bytes 202760 | tf_op jit(solution)/shard_map/ppermute | solution.py:184
  20.5 0.0 collective-permute-done.5.refs_5_
  20.5 1.4 %collective-permute-start.10 = (bf16[264,128]{1,0:T(8,128)(2,1)S(1)}, bf16[264,128]{1,0:T(8,128)(2,1)S(1)}, u32[]{:S(2)}, u32[]{:S(2)}) collective-permute-start(bf16[264,128]{1,0:T(8,128)(2,1)S(1)} %get-tuple-element.35), channel_id=1, source_target_pairs={{0,3},{1,2},{2,1},{3,0},{4,7},{5,6},{6,5},{7,4},{8,11},{9,10},{10,... | collective-permute-start | bytes 202760 | tf_op jit(solution)/shard_map/ppermute | solution.py:184
  21.9 0.0 collective-permute-done.6.refs_6_
  21.9 1.1 %collective-permute-start.11 = (bf16[264,128]{1,0:T(8,128)(2,1)S(1)}, bf16[264,128]{1,0:T(8,128)(2,1)S(1)}, u32[]{:S(2)}, u32[]{:S(2)}) collective-permute-start(bf16[264,128]{1,0:T(8,128)(2,1)S(1)} %get-tuple-element.36), channel_id=1, source_target_pairs={{0,11},{1,10},{2,9},{3,8},{4,15},{5,14},{6,13},{7,12},{8,3},{9,2},... | collective-permute-start | bytes 202760 | tf_op jit(solution)/shard_map/ppermute | solution.py:184
  23.1 0.0 collective-permute-done.7.refs_7_
  23.1 1.5 %collective-permute-start.12 = (bf16[264,128]{1,0:T(8,128)(2,1)S(1)}, bf16[264,128]{1,0:T(8,128)(2,1)S(1)}, u32[]{:S(2)}, u32[]{:S(2)}) collective-permute-start(bf16[264,128]{1,0:T(8,128)(2,1)S(1)} %get-tuple-element.37), channel_id=1, source_target_pairs={{0,2},{1,3},{2,0},{3,1},{4,6},{5,7},{6,4},{7,5},{8,10},{9,11},{10,... | collective-permute-start | bytes 202760 | tf_op jit(solution)/shard_map/ppermute | solution.py:184
  24.6 0.0 collective-permute-done.8.refs_8_
  24.6 2.3 %collective-permute-start.13 = (bf16[264,128]{1,0:T(8,128)(2,1)S(1)}, bf16[264,128]{1,0:T(8,128)(2,1)S(1)}, u32[]{:S(2)}, u32[]{:S(2)}) collective-permute-start(bf16[264,128]{1,0:T(8,128)(2,1)S(1)} %get-tuple-element.38), channel_id=1, source_target_pairs={{0,15},{1,14},{2,13},{3,12},{4,11},{5,10},{6,9},{7,8},{8,7},{9,6},... | collective-permute-start | bytes 202760 | tf_op jit(solution)/shard_map/ppermute | solution.py:184
  26.9 0.1 collective-permute-done.9.refs_9_
  27.0 0.6 %collective-permute-start.14 = (bf16[264,128]{1,0:T(8,128)(2,1)S(1)}, bf16[264,128]{1,0:T(8,128)(2,1)S(1)}, u32[]{:S(2)}, u32[]{:S(2)}) collective-permute-start(bf16[264,128]{1,0:T(8,128)(2,1)S(1)} %get-tuple-element.39), channel_id=1, source_target_pairs={{0,1},{1,0},{2,3},{3,2},{4,5},{5,4},{6,7},{7,6},{8,9},{9,8},{10,11... | collective-permute-start | bytes 202760 | tf_op jit(solution)/shard_map/ppermute | solution.py:184
  27.6 0.0 collective-permute-done.10.refs_10_
  27.6 1.5 %collective-permute-done.11.refs_11_ = bf16[264,128]{1,0:T(8,128)(2,1)S(1)} collective-permute-done((bf16[264,128]{1,0:T(8,128)(2,1)S(1)}, bf16[264,128]{1,0:T(8,128)(2,1)S(1)}, u32[]{:S(2)}, u32[]{:S(2)}) %collective-permute-start.11) | collective-permute-done | bytes 67616 | tf_op jit(solution)/shard_map/ppermute | solution.py:184
  29.2 0.0 collective-permute-done.12.refs_12_
  29.2 2.2 %collective-permute-done.13.refs_13_ = bf16[264,128]{1,0:T(8,128)(2,1)S(1)} collective-permute-done((bf16[264,128]{1,0:T(8,128)(2,1)S(1)}, bf16[264,128]{1,0:T(8,128)(2,1)S(1)}, u32[]{:S(2)}, u32[]{:S(2)}) %collective-permute-start.13) | collective-permute-done | bytes 67616 | tf_op jit(solution)/shard_map/ppermute | solution.py:184
  31.4 0.0 collective-permute-done.14.refs_14_
  31.4 0.9 %shard_map.39 = f32[16,1,128]{2,1,0:T(1,128)S(1)} custom-call(bf16[264,128]{1,0:T(8,128)(2,1)S(1)} %collective-permute-done.refs_0_, bf16[264,128]{1,0:T(8,128)(2,1)S(1)} %collective-permute-done.1.refs_1_, bf16[264,128]{1,0:T(8,128)(2,1)S(1)} %collective-permute-done.2.refs_2_, bf16[264,128]{1,0:T(8,128)(2,1)S(1)} %collective-permute-done.3.refs_3_, ...), custom_call_target="tpu_custom_call" | custom-call | tf_op jit(solution)/shard_map/pallas_call | solution.py:173
  32.2 10.9 %all_to_all.5.refs_0_ = f32[16,1,128]{2,1,0:T(1,128)S(1)} all-to-all(f32[16,1,128]{2,1,0:T(1,128)S(1)} %shard_map.39), channel_id=1, replica_groups=mesh['groups'=2,'shard'=16] {'shard'}, dimensions={0} | all-to-all | bytes 16384 | tf_op jit(solution)/shard_map/all_to_all | solution.py:227
  43.2 0.7 %shard_map.40 = f32[1,256]{1,0:T(1,128)} custom-call(f32[16,1,128]{2,1,0:T(1,128)S(1)} %all_to_all.5.refs_0_, s32[1,256]{1,0:T(1,128)S(1)} %get-tuple-element.23.refs_1_), custom_call_target="tpu_custom_call" | custom-call | tf_op jit(solution)/shard_map/pallas_call | solution.py:173
Async XLA Ops:
  0.7 1.0 %copy-start = (bf16[256,1024]{1,0:T(8,128)(2,1)S(1)}, bf16[256,1024]{1,0:T(8,128)(2,1)}, u32[]{:S(2)}) copy-start(bf16[256,1024]{1,0:T(8,128)(2,1)} %refs_0_.1) | copy-start | bytes 1572868
  2.3 9.8 %collective-permute-start = (bf16[264,128]{1,0:T(8,128)(2,1)S(1)}, bf16[264,128]{1,0:T(8,128)(2,1)S(1)}, u32[]{:S(2)}, u32[]{:S(2)}) collective-permute-start(bf16[264,128]{1,0:T(8,128)(2,1)S(1)} %get-tuple-element.25), channel_id=1, source_target_pairs={{0,8},{1,9},{2,10},{3,11},{4,12},{5,13},{6,14},{7,15},{8,0},{9,1},... | collective-permute-start | bytes 202760 | tf_op jit(solution)/shard_map/ppermute | solution.py:184
  6.4 7.9 %collective-permute-start.1 = (bf16[264,128]{1,0:T(8,128)(2,1)S(1)}, bf16[264,128]{1,0:T(8,128)(2,1)S(1)}, u32[]{:S(2)}, u32[]{:S(2)}) collective-permute-start(bf16[264,128]{1,0:T(8,128)(2,1)S(1)} %get-tuple-element.26), channel_id=1, source_target_pairs={{0,12},{1,13},{2,14},{3,15},{4,8},{5,9},{6,10},{7,11},{8,4},{9,5},... | collective-permute-start | bytes 202760 | tf_op jit(solution)/shard_map/ppermute | solution.py:184
  7.8 6.7 %collective-permute-start.2 = (bf16[264,128]{1,0:T(8,128)(2,1)S(1)}, bf16[264,128]{1,0:T(8,128)(2,1)S(1)}, u32[]{:S(2)}, u32[]{:S(2)}) collective-permute-start(bf16[264,128]{1,0:T(8,128)(2,1)S(1)} %get-tuple-element.27), channel_id=1, source_target_pairs={{0,7},{1,6},{2,5},{3,4},{4,3},{5,2},{6,1},{7,0},{8,15},{9,14},{10,... | collective-permute-start | bytes 202760 | tf_op jit(solution)/shard_map/ppermute | solution.py:184
  8.1 10.3 %collective-permute-start.3 = (bf16[264,128]{1,0:T(8,128)(2,1)S(1)}, bf16[264,128]{1,0:T(8,128)(2,1)S(1)}, u32[]{:S(2)}, u32[]{:S(2)}) collective-permute-start(bf16[264,128]{1,0:T(8,128)(2,1)S(1)} %get-tuple-element.28), channel_id=1, source_target_pairs={{0,9},{1,8},{2,11},{3,10},{4,13},{5,12},{6,15},{7,14},{8,1},{9,0},... | collective-permute-start | bytes 202760 | tf_op jit(solution)/shard_map/ppermute | solution.py:184
  11.5 7.9 %collective-permute-start.4 = (bf16[264,128]{1,0:T(8,128)(2,1)S(1)}, bf16[264,128]{1,0:T(8,128)(2,1)S(1)}, u32[]{:S(2)}, u32[]{:S(2)}) collective-permute-start(bf16[264,128]{1,0:T(8,128)(2,1)S(1)} %get-tuple-element.29), channel_id=1, source_target_pairs={{0,6},{1,7},{2,4},{3,5},{4,2},{5,3},{6,0},{7,1},{8,14},{9,15},{10,... | collective-permute-start | bytes 202760 | tf_op jit(solution)/shard_map/ppermute | solution.py:184
  12.1 8.4 %collective-permute-start.5 = (bf16[264,128]{1,0:T(8,128)(2,1)S(1)}, bf16[264,128]{1,0:T(8,128)(2,1)S(1)}, u32[]{:S(2)}, u32[]{:S(2)}) collective-permute-start(bf16[264,128]{1,0:T(8,128)(2,1)S(1)} %get-tuple-element.30), channel_id=1, source_target_pairs={{0,13},{1,12},{2,15},{3,14},{4,9},{5,8},{6,11},{7,10},{8,5},{9,4},... | collective-permute-start | bytes 202760 | tf_op jit(solution)/shard_map/ppermute | solution.py:184
  14.4 7.6 %collective-permute-start.6 = (bf16[264,128]{1,0:T(8,128)(2,1)S(1)}, bf16[264,128]{1,0:T(8,128)(2,1)S(1)}, u32[]{:S(2)}, u32[]{:S(2)}) collective-permute-start(bf16[264,128]{1,0:T(8,128)(2,1)S(1)} %get-tuple-element.31), channel_id=1, source_target_pairs={{0,5},{1,4},{2,7},{3,6},{4,1},{5,0},{6,3},{7,2},{8,13},{9,12},{10,... | collective-permute-start | bytes 202760 | tf_op jit(solution)/shard_map/ppermute | solution.py:184
  14.5 8.6 %collective-permute-start.7 = (bf16[264,128]{1,0:T(8,128)(2,1)S(1)}, bf16[264,128]{1,0:T(8,128)(2,1)S(1)}, u32[]{:S(2)}, u32[]{:S(2)}) collective-permute-start(bf16[264,128]{1,0:T(8,128)(2,1)S(1)} %get-tuple-element.32), channel_id=1, source_target_pairs={{0,10},{1,11},{2,8},{3,9},{4,14},{5,15},{6,12},{7,13},{8,2},{9,3},... | collective-permute-start | bytes 202760 | tf_op jit(solution)/shard_map/ppermute | solution.py:184
  18.4 6.2 %collective-permute-start.8 = (bf16[264,128]{1,0:T(8,128)(2,1)S(1)}, bf16[264,128]{1,0:T(8,128)(2,1)S(1)}, u32[]{:S(2)}, u32[]{:S(2)}) collective-permute-start(bf16[264,128]{1,0:T(8,128)(2,1)S(1)} %get-tuple-element.33), channel_id=1, source_target_pairs={{0,4},{1,5},{2,6},{3,7},{4,0},{5,1},{6,2},{7,3},{8,12},{9,13},{10,... | collective-permute-start | bytes 202760 | tf_op jit(solution)/shard_map/ppermute | solution.py:184
  19.4 7.6 %collective-permute-start.9 = (bf16[264,128]{1,0:T(8,128)(2,1)S(1)}, bf16[264,128]{1,0:T(8,128)(2,1)S(1)}, u32[]{:S(2)}, u32[]{:S(2)}) collective-permute-start(bf16[264,128]{1,0:T(8,128)(2,1)S(1)} %get-tuple-element.34), channel_id=1, source_target_pairs={{0,14},{1,15},{2,12},{3,13},{4,10},{5,11},{6,8},{7,9},{8,6},{9,7},... | collective-permute-start | bytes 202760 | tf_op jit(solution)/shard_map/ppermute | solution.py:184
  20.5 7.2 %collective-permute-start.10 = (bf16[264,128]{1,0:T(8,128)(2,1)S(1)}, bf16[264,128]{1,0:T(8,128)(2,1)S(1)}, u32[]{:S(2)}, u32[]{:S(2)}) collective-permute-start(bf16[264,128]{1,0:T(8,128)(2,1)S(1)} %get-tuple-element.35), channel_id=1, source_target_pairs={{0,3},{1,2},{2,1},{3,0},{4,7},{5,6},{6,5},{7,4},{8,11},{9,10},{10,... | collective-permute-start | bytes 202760 | tf_op jit(solution)/shard_map/ppermute | solution.py:184
  21.9 7.2 %collective-permute-start.11 = (bf16[264,128]{1,0:T(8,128)(2,1)S(1)}, bf16[264,128]{1,0:T(8,128)(2,1)S(1)}, u32[]{:S(2)}, u32[]{:S(2)}) collective-permute-start(bf16[264,128]{1,0:T(8,128)(2,1)S(1)} %get-tuple-element.36), channel_id=1, source_target_pairs={{0,11},{1,10},{2,9},{3,8},{4,15},{5,14},{6,13},{7,12},{8,3},{9,2},... | collective-permute-start | bytes 202760 | tf_op jit(solution)/shard_map/ppermute | solution.py:184
  23.1 6.1 %collective-permute-start.12 = (bf16[264,128]{1,0:T(8,128)(2,1)S(1)}, bf16[264,128]{1,0:T(8,128)(2,1)S(1)}, u32[]{:S(2)}, u32[]{:S(2)}) collective-permute-start(bf16[264,128]{1,0:T(8,128)(2,1)S(1)} %get-tuple-element.37), channel_id=1, source_target_pairs={{0,2},{1,3},{2,0},{3,1},{4,6},{5,7},{6,4},{7,5},{8,10},{9,11},{10,... | collective-permute-start | bytes 202760 | tf_op jit(solution)/shard_map/ppermute | solution.py:184
  24.6 6.8 %collective-permute-start.13 = (bf16[264,128]{1,0:T(8,128)(2,1)S(1)}, bf16[264,128]{1,0:T(8,128)(2,1)S(1)}, u32[]{:S(2)}, u32[]{:S(2)}) collective-permute-start(bf16[264,128]{1,0:T(8,128)(2,1)S(1)} %get-tuple-element.38), channel_id=1, source_target_pairs={{0,15},{1,14},{2,13},{3,12},{4,11},{5,10},{6,9},{7,8},{8,7},{9,6},... | collective-permute-start | bytes 202760 | tf_op jit(solution)/shard_map/ppermute | solution.py:184
  27.0 4.3 %collective-permute-start.14 = (bf16[264,128]{1,0:T(8,128)(2,1)S(1)}, bf16[264,128]{1,0:T(8,128)(2,1)S(1)}, u32[]{:S(2)}, u32[]{:S(2)}) collective-permute-start(bf16[264,128]{1,0:T(8,128)(2,1)S(1)} %get-tuple-element.39), channel_id=1, source_target_pairs={{0,1},{1,0},{2,3},{3,2},{4,5},{5,4},{6,7},{7,6},{8,9},{9,8},{10,11... | collective-permute-start | bytes 202760 | tf_op jit(solution)/shard_map/ppermute | solution.py:184

commit v13 on v12

--- a/solution.py
+++ b/solution.py
@@ -35,10 +35,10 @@
     quarter = half // 2
     far = [half + part * quarter + k for k in range(quarter) for part in range(2)]
     near = list(range(half - 1, -1, -1))
-    order = far[:2]
-    for block in far[2:]:
+    order = far[:1]
+    for block in far[1:half - 1]:
         order += [near.pop(0), block]
-    return order + near
+    return order + far[half - 1:] + near
 
 
 def place_kernel(owners, capacity, paired, code_ref, place_ref, meta_ref):

time: 44.1 us -> 45.6 us (1.034)
  waiting for transfers between devices: 4.02 us -> 8.45 us
  starting transfers between devices: 25 us -> 21.6 us
    ppermute x15, waiting for transfers between devices: 4.02 us -> 8.45 us  [swap(): lax.ppermute(block, 'shard', [(d, d ^ k) for d in range(owners)])]
    ppermute x15, starting transfers between devices: 25 us -> 21.6 us  [swap(): lax.ppermute(block, 'shard', [(d, d ^ k) for d in range(owners)])]
  transfers between devices with their start and end apart: 15 -> 15, of which waited for: 4 -> 5; matrix products, arithmetic and copies ran while one was open for 0% -> 0% of each run, Pallas kernels for 0% -> 0%
where the time goes in v13:
time: 45.6 us; the launch traced here: 45.4 us
  starting transfers between devices  21.6 us (47%)
  blocking collectives  11.3 us (25%)
  waiting for transfers between devices  8.45 us (19%)
  Pallas kernels  2.53 us (6%)
  local copies, waits for them, and re-layouts  0.71 us (2%)
  other arithmetic  0.7 us (2%)
    ppermute x15, starting transfers between devices, swap(): lax.ppermute(block, 'shard', [(d, d ^ k) for d in range(owners)])  21.6 us
    all_to_all x1, blocking collectives, shards(): returned = lax.all_to_all(best, 'shard', 0, 0, tiled=True)  11.3 us
    ppermute x15, waiting for transfers between devices, swap(): lax.ppermute(block, 'shard', [(d, d ^ k) for d in range(owners)])  8.45 us
    pallas_call x4, Pallas kernels, call(): pl.pallas_call(body, out_shape=shapes, compiler_params=pltpu.CompilerPara...  2.53 us
  transfers between devices with their start and end apart: 15, of which 5 were waited for; matrix products, arithmetic and copies ran while one was open for 0% of the time, Pallas kernels for 0%

profile of v13, /device:TPU:0, one launch (start us, length us, event | category | flops | bytes accessed | tf_op | source)
XLA Modules:
  0.0 45.4 jit_solution(17739323121940336891)
XLA Ops:
  0.0 0.7 %multiply_add_fusion = s32[256]{0:T(256)S(1)} fusion(s32[256]{0:T(256)} %param.5, s32[256]{0:T(256)} %param.4), kind=kLoop, calls=%fused_computation | loop fusion | flops 512 | bytes 3072 | tf_op jit(solution)/shard_map/add | solution.py:203
  0.7 0.0 copy-start
  0.7 0.3 shard_map.37
  1.0 0.7 %copy-done = bf16[256,1024]{1,0:T(8,128)(2,1)S(1)} copy-done((bf16[256,1024]{1,0:T(8,128)(2,1)S(1)}, bf16[256,1024]{1,0:T(8,128)(2,1)}, u32[]{:S(2)}) %copy-start) | copy-done | bytes 524312
  1.7 0.6 %shard_map.38 = (bf16[264,128]{1,0:T(8,128)(2,1)S(1)}, bf16[264,128]{1,0:T(8,128)(2,1)S(1)}, bf16[264,128]{1,0:T(8,128)(2,1)S(1)}, bf16[264,128]{1,0:T(8,128)(2,...) custom-call(bf16[256,1024]{1,0:T(8,128)(2,1)S(1)} %copy-done, ...), custom_call_target="tpu_custom_call" | custom-call | tf_op jit(solution)/shard_map/pallas_call | solution.py:173
  2.3 4.1 %collective-permute-start = (bf16[264,128]{1,0:T(8,128)(2,1)S(1)}, bf16[264,128]{1,0:T(8,128)(2,1)S(1)}, u32[]{:S(2)}, u32[]{:S(2)}) collective-permute-start(bf16[264,128]{1,0:T(8,128)(2,1)S(1)} %get-tuple-element.25), channel_id=1, source_target_pairs={{0,8},{1,9},{2,10},{3,11},{4,12},{5,13},{6,14},{7,15},{8,0},{9,1},... | collective-permute-start | bytes 202760 | tf_op jit(solution)/shard_map/ppermute | solution.py:184
  6.4 1.7 %collective-permute-start.1 = (bf16[264,128]{1,0:T(8,128)(2,1)S(1)}, bf16[264,128]{1,0:T(8,128)(2,1)S(1)}, u32[]{:S(2)}, u32[]{:S(2)}) collective-permute-start(bf16[264,128]{1,0:T(8,128)(2,1)S(1)} %get-tuple-element.26), channel_id=1, source_target_pairs={{0,7},{1,6},{2,5},{3,4},{4,3},{5,2},{6,1},{7,0},{8,15},{9,14},{10,... | collective-permute-start | bytes 202760 | tf_op jit(solution)/shard_map/ppermute | solution.py:184
  8.1 0.2 collective-permute-start.2
  8.4 0.6 %collective-permute-start.3 = (bf16[264,128]{1,0:T(8,128)(2,1)S(1)}, bf16[264,128]{1,0:T(8,128)(2,1)S(1)}, u32[]{:S(2)}, u32[]{:S(2)}) collective-permute-start(bf16[264,128]{1,0:T(8,128)(2,1)S(1)} %get-tuple-element.28), channel_id=1, source_target_pairs={{0,6},{1,7},{2,4},{3,5},{4,2},{5,3},{6,0},{7,1},{8,14},{9,15},{10,... | collective-permute-start | bytes 202760 | tf_op jit(solution)/shard_map/ppermute | solution.py:184
  9.0 3.5 %collective-permute-start.4 = (bf16[264,128]{1,0:T(8,128)(2,1)S(1)}, bf16[264,128]{1,0:T(8,128)(2,1)S(1)}, u32[]{:S(2)}, u32[]{:S(2)}) collective-permute-start(bf16[264,128]{1,0:T(8,128)(2,1)S(1)} %get-tuple-element.29), channel_id=1, source_target_pairs={{0,9},{1,8},{2,11},{3,10},{4,13},{5,12},{6,15},{7,14},{8,1},{9,0},... | collective-permute-start | bytes 202760 | tf_op jit(solution)/shard_map/ppermute | solution.py:184
  12.5 0.0 collective-permute-done.refs_0_
  12.5 0.0 collective-permute-start.5
  12.5 0.0 collective-permute-done.1.refs_1_
  12.5 1.1 %collective-permute-start.6 = (bf16[264,128]{1,0:T(8,128)(2,1)S(1)}, bf16[264,128]{1,0:T(8,128)(2,1)S(1)}, u32[]{:S(2)}, u32[]{:S(2)}) collective-permute-start(bf16[264,128]{1,0:T(8,128)(2,1)S(1)} %get-tuple-element.31), channel_id=1, source_target_pairs={{0,13},{1,12},{2,15},{3,14},{4,9},{5,8},{6,11},{7,10},{8,5},{9,4},... | collective-permute-start | bytes 202760 | tf_op jit(solution)/shard_map/ppermute | solution.py:184
  13.7 1.4 %collective-permute-done.2.refs_2_ = bf16[264,128]{1,0:T(8,128)(2,1)S(1)} collective-permute-done((bf16[264,128]{1,0:T(8,128)(2,1)S(1)}, bf16[264,128]{1,0:T(8,128)(2,1)S(1)}, u32[]{:S(2)}, u32[]{:S(2)}) %collective-permute-start.2) | collective-permute-done | bytes 67616 | tf_op jit(solution)/shard_map/ppermute | solution.py:184
  15.0 0.0 collective-permute-start.7
  15.0 2.2 %collective-permute-done.3.refs_3_ = bf16[264,128]{1,0:T(8,128)(2,1)S(1)} collective-permute-done((bf16[264,128]{1,0:T(8,128)(2,1)S(1)}, bf16[264,128]{1,0:T(8,128)(2,1)S(1)}, u32[]{:S(2)}, u32[]{:S(2)}) %collective-permute-start.3) | collective-permute-done | bytes 67616 | tf_op jit(solution)/shard_map/ppermute | solution.py:184
  17.2 0.7 %collective-permute-start.8 = (bf16[264,128]{1,0:T(8,128)(2,1)S(1)}, bf16[264,128]{1,0:T(8,128)(2,1)S(1)}, u32[]{:S(2)}, u32[]{:S(2)}) collective-permute-start(bf16[264,128]{1,0:T(8,128)(2,1)S(1)} %get-tuple-element.33), channel_id=1, source_target_pairs={{0,10},{1,11},{2,8},{3,9},{4,14},{5,15},{6,12},{7,13},{8,2},{9,3},... | collective-permute-start | bytes 202760 | tf_op jit(solution)/shard_map/ppermute | solution.py:184
  17.9 0.0 collective-permute-done.4.refs_4_
  17.9 0.3 collective-permute-start.9
  18.1 0.0 collective-permute-done.5.refs_5_
  18.1 2.8 %collective-permute-start.10 = (bf16[264,128]{1,0:T(8,128)(2,1)S(1)}, bf16[264,128]{1,0:T(8,128)(2,1)S(1)}, u32[]{:S(2)}, u32[]{:S(2)}) collective-permute-start(bf16[264,128]{1,0:T(8,128)(2,1)S(1)} %get-tuple-element.35), channel_id=1, source_target_pairs={{0,14},{1,15},{2,12},{3,13},{4,10},{5,11},{6,8},{7,9},{8,6},{9,7},... | collective-permute-start | bytes 202760 | tf_op jit(solution)/shard_map/ppermute | solution.py:184
  21.0 0.0 collective-permute-done.6.refs_6_
  21.0 1.7 %collective-permute-start.11 = (bf16[264,128]{1,0:T(8,128)(2,1)S(1)}, bf16[264,128]{1,0:T(8,128)(2,1)S(1)}, u32[]{:S(2)}, u32[]{:S(2)}) collective-permute-start(bf16[264,128]{1,0:T(8,128)(2,1)S(1)} %get-tuple-element.36), channel_id=1, source_target_pairs={{0,2},{1,3},{2,0},{3,1},{4,6},{5,7},{6,4},{7,5},{8,10},{9,11},{10,... | collective-permute-start | bytes 202760 | tf_op jit(solution)/shard_map/ppermute | solution.py:184
  22.7 0.0 collective-permute-done.7.refs_7_
  22.7 1.7 %collective-permute-start.12 = (bf16[264,128]{1,0:T(8,128)(2,1)S(1)}, bf16[264,128]{1,0:T(8,128)(2,1)S(1)}, u32[]{:S(2)}, u32[]{:S(2)}) collective-permute-start(bf16[264,128]{1,0:T(8,128)(2,1)S(1)} %get-tuple-element.37), channel_id=1, source_target_pairs={{0,11},{1,10},{2,9},{3,8},{4,15},{5,14},{6,13},{7,12},{8,3},{9,2},... | collective-permute-start | bytes 202760 | tf_op jit(solution)/shard_map/ppermute | solution.py:184
  24.4 1.6 %collective-permute-done.8.refs_8_ = bf16[264,128]{1,0:T(8,128)(2,1)S(1)} collective-permute-done((bf16[264,128]{1,0:T(8,128)(2,1)S(1)}, bf16[264,128]{1,0:T(8,128)(2,1)S(1)}, u32[]{:S(2)}, u32[]{:S(2)}) %collective-permute-start.8) | collective-permute-done | bytes 67616 | tf_op jit(solution)/shard_map/ppermute | solution.py:184
  26.0 2.4 %collective-permute-start.13 = (bf16[264,128]{1,0:T(8,128)(2,1)S(1)}, bf16[264,128]{1,0:T(8,128)(2,1)S(1)}, u32[]{:S(2)}, u32[]{:S(2)}) collective-permute-start(bf16[264,128]{1,0:T(8,128)(2,1)S(1)} %get-tuple-element.38), channel_id=1, source_target_pairs={{0,15},{1,14},{2,13},{3,12},{4,11},{5,10},{6,9},{7,8},{8,7},{9,6},... | collective-permute-start | bytes 202760 | tf_op jit(solution)/shard_map/ppermute | solution.py:184
  28.4 0.0 collective-permute-done.9.refs_9_
  28.4 0.7 %collective-permute-start.14 = (bf16[264,128]{1,0:T(8,128)(2,1)S(1)}, bf16[264,128]{1,0:T(8,128)(2,1)S(1)}, u32[]{:S(2)}, u32[]{:S(2)}) collective-permute-start(bf16[264,128]{1,0:T(8,128)(2,1)S(1)} %get-tuple-element.39), channel_id=1, source_target_pairs={{0,1},{1,0},{2,3},{3,2},{4,5},{5,4},{6,7},{7,6},{8,9},{9,8},{10,11... | collective-permute-start | bytes 202760 | tf_op jit(solution)/shard_map/ppermute | solution.py:184
  29.1 0.0 collective-permute-done.10.refs_10_
  29.1 0.0 collective-permute-done.11.refs_11_
  29.1 0.7 %collective-permute-done.12.refs_12_ = bf16[264,128]{1,0:T(8,128)(2,1)S(1)} collective-permute-done((bf16[264,128]{1,0:T(8,128)(2,1)S(1)}, bf16[264,128]{1,0:T(8,128)(2,1)S(1)}, u32[]{:S(2)}, u32[]{:S(2)}) %collective-permute-start.12) | collective-permute-done | bytes 67616 | tf_op jit(solution)/shard_map/ppermute | solution.py:184
  29.8 2.6 %collective-permute-done.13.refs_13_ = bf16[264,128]{1,0:T(8,128)(2,1)S(1)} collective-permute-done((bf16[264,128]{1,0:T(8,128)(2,1)S(1)}, bf16[264,128]{1,0:T(8,128)(2,1)S(1)}, u32[]{:S(2)}, u32[]{:S(2)}) %collective-permute-start.13) | collective-permute-done | bytes 67616 | tf_op jit(solution)/shard_map/ppermute | solution.py:184
  32.4 0.0 collective-permute-done.14.refs_14_
  32.4 0.9 %shard_map.39 = f32[16,1,128]{2,1,0:T(1,128)S(1)} custom-call(bf16[264,128]{1,0:T(8,128)(2,1)S(1)} %collective-permute-done.refs_0_, bf16[264,128]{1,0:T(8,128)(2,1)S(1)} %collective-permute-done.1.refs_1_, bf16[264,128]{1,0:T(8,128)(2,1)S(1)} %collective-permute-done.2.refs_2_, bf16[264,128]{1,0:T(8,128)(2,1)S(1)} %collective-permute-done.3.refs_3_, ...), custom_call_target="tpu_custom_call" | custom-call | tf_op jit(solution)/shard_map/pallas_call | solution.py:173
  33.3 11.3 %all_to_all.5.refs_0_ = f32[16,1,128]{2,1,0:T(1,128)S(1)} all-to-all(f32[16,1,128]{2,1,0:T(1,128)S(1)} %shard_map.39), channel_id=1, replica_groups=mesh['groups'=2,'shard'=16] {'shard'}, dimensions={0} | all-to-all | bytes 16384 | tf_op jit(solution)/shard_map/all_to_all | solution.py:227
  44.6 0.7 %shard_map.40 = f32[1,256]{1,0:T(1,128)} custom-call(f32[16,1,128]{2,1,0:T(1,128)S(1)} %all_to_all.5.refs_0_, s32[1,256]{1,0:T(1,128)S(1)} %get-tuple-element.23.refs_1_), custom_call_target="tpu_custom_call" | custom-call | tf_op jit(solution)/shard_map/pallas_call | solution.py:173
Async XLA Ops:
  0.7 1.0 %copy-start = (bf16[256,1024]{1,0:T(8,128)(2,1)S(1)}, bf16[256,1024]{1,0:T(8,128)(2,1)}, u32[]{:S(2)}) copy-start(bf16[256,1024]{1,0:T(8,128)(2,1)} %refs_0_.1) | copy-start | bytes 1572868
  2.3 10.2 %collective-permute-start = (bf16[264,128]{1,0:T(8,128)(2,1)S(1)}, bf16[264,128]{1,0:T(8,128)(2,1)S(1)}, u32[]{:S(2)}, u32[]{:S(2)}) collective-permute-start(bf16[264,128]{1,0:T(8,128)(2,1)S(1)} %get-tuple-element.25), channel_id=1, source_target_pairs={{0,8},{1,9},{2,10},{3,11},{4,12},{5,13},{6,14},{7,15},{8,0},{9,1},... | collective-permute-start | bytes 202760 | tf_op jit(solution)/shard_map/ppermute | solution.py:184
  6.4 6.1 %collective-permute-start.1 = (bf16[264,128]{1,0:T(8,128)(2,1)S(1)}, bf16[264,128]{1,0:T(8,128)(2,1)S(1)}, u32[]{:S(2)}, u32[]{:S(2)}) collective-permute-start(bf16[264,128]{1,0:T(8,128)(2,1)S(1)} %get-tuple-element.26), channel_id=1, source_target_pairs={{0,7},{1,6},{2,5},{3,4},{4,3},{5,2},{6,1},{7,0},{8,15},{9,14},{10,... | collective-permute-start | bytes 202760 | tf_op jit(solution)/shard_map/ppermute | solution.py:184
  8.1 6.9 %collective-permute-start.2 = (bf16[264,128]{1,0:T(8,128)(2,1)S(1)}, bf16[264,128]{1,0:T(8,128)(2,1)S(1)}, u32[]{:S(2)}, u32[]{:S(2)}) collective-permute-start(bf16[264,128]{1,0:T(8,128)(2,1)S(1)} %get-tuple-element.27), channel_id=1, source_target_pairs={{0,12},{1,13},{2,14},{3,15},{4,8},{5,9},{6,10},{7,11},{8,4},{9,5},... | collective-permute-start | bytes 202760 | tf_op jit(solution)/shard_map/ppermute | solution.py:184
  8.4 8.8 %collective-permute-start.3 = (bf16[264,128]{1,0:T(8,128)(2,1)S(1)}, bf16[264,128]{1,0:T(8,128)(2,1)S(1)}, u32[]{:S(2)}, u32[]{:S(2)}) collective-permute-start(bf16[264,128]{1,0:T(8,128)(2,1)S(1)} %get-tuple-element.28), channel_id=1, source_target_pairs={{0,6},{1,7},{2,4},{3,5},{4,2},{5,3},{6,0},{7,1},{8,14},{9,15},{10,... | collective-permute-start | bytes 202760 | tf_op jit(solution)/shard_map/ppermute | solution.py:184
  9.0 8.8 %collective-permute-start.4 = (bf16[264,128]{1,0:T(8,128)(2,1)S(1)}, bf16[264,128]{1,0:T(8,128)(2,1)S(1)}, u32[]{:S(2)}, u32[]{:S(2)}) collective-permute-start(bf16[264,128]{1,0:T(8,128)(2,1)S(1)} %get-tuple-element.29), channel_id=1, source_target_pairs={{0,9},{1,8},{2,11},{3,10},{4,13},{5,12},{6,15},{7,14},{8,1},{9,0},... | collective-permute-start | bytes 202760 | tf_op jit(solution)/shard_map/ppermute | solution.py:184
  12.5 5.6 %collective-permute-start.5 = (bf16[264,128]{1,0:T(8,128)(2,1)S(1)}, bf16[264,128]{1,0:T(8,128)(2,1)S(1)}, u32[]{:S(2)}, u32[]{:S(2)}) collective-permute-start(bf16[264,128]{1,0:T(8,128)(2,1)S(1)} %get-tuple-element.30), channel_id=1, source_target_pairs={{0,5},{1,4},{2,7},{3,6},{4,1},{5,0},{6,3},{7,2},{8,13},{9,12},{10,... | collective-permute-start | bytes 202760 | tf_op jit(solution)/shard_map/ppermute | solution.py:184
  12.5 8.5 %collective-permute-start.6 = (bf16[264,128]{1,0:T(8,128)(2,1)S(1)}, bf16[264,128]{1,0:T(8,128)(2,1)S(1)}, u32[]{:S(2)}, u32[]{:S(2)}) collective-permute-start(bf16[264,128]{1,0:T(8,128)(2,1)S(1)} %get-tuple-element.31), channel_id=1, source_target_pairs={{0,13},{1,12},{2,15},{3,14},{4,9},{5,8},{6,11},{7,10},{8,5},{9,4},... | collective-permute-start | bytes 202760 | tf_op jit(solution)/shard_map/ppermute | solution.py:184
  15.0 7.6 %collective-permute-start.7 = (bf16[264,128]{1,0:T(8,128)(2,1)S(1)}, bf16[264,128]{1,0:T(8,128)(2,1)S(1)}, u32[]{:S(2)}, u32[]{:S(2)}) collective-permute-start(bf16[264,128]{1,0:T(8,128)(2,1)S(1)} %get-tuple-element.32), channel_id=1, source_target_pairs={{0,4},{1,5},{2,6},{3,7},{4,0},{5,1},{6,2},{7,3},{8,12},{9,13},{10,... | collective-permute-start | bytes 202760 | tf_op jit(solution)/shard_map/ppermute | solution.py:184
  17.2 8.8 %collective-permute-start.8 = (bf16[264,128]{1,0:T(8,128)(2,1)S(1)}, bf16[264,128]{1,0:T(8,128)(2,1)S(1)}, u32[]{:S(2)}, u32[]{:S(2)}) collective-permute-start(bf16[264,128]{1,0:T(8,128)(2,1)S(1)} %get-tuple-element.33), channel_id=1, source_target_pairs={{0,10},{1,11},{2,8},{3,9},{4,14},{5,15},{6,12},{7,13},{8,2},{9,3},... | collective-permute-start | bytes 202760 | tf_op jit(solution)/shard_map/ppermute | solution.py:184
  17.9 10.6 %collective-permute-start.9 = (bf16[264,128]{1,0:T(8,128)(2,1)S(1)}, bf16[264,128]{1,0:T(8,128)(2,1)S(1)}, u32[]{:S(2)}, u32[]{:S(2)}) collective-permute-start(bf16[264,128]{1,0:T(8,128)(2,1)S(1)} %get-tuple-element.34), channel_id=1, source_target_pairs={{0,3},{1,2},{2,1},{3,0},{4,7},{5,6},{6,5},{7,4},{8,11},{9,10},{10,... | collective-permute-start | bytes 202760 | tf_op jit(solution)/shard_map/ppermute | solution.py:184
  18.1 11.0 %collective-permute-start.10 = (bf16[264,128]{1,0:T(8,128)(2,1)S(1)}, bf16[264,128]{1,0:T(8,128)(2,1)S(1)}, u32[]{:S(2)}, u32[]{:S(2)}) collective-permute-start(bf16[264,128]{1,0:T(8,128)(2,1)S(1)} %get-tuple-element.35), channel_id=1, source_target_pairs={{0,14},{1,15},{2,12},{3,13},{4,10},{5,11},{6,8},{7,9},{8,6},{9,7},... | collective-permute-start | bytes 202760 | tf_op jit(solution)/shard_map/ppermute | solution.py:184
  21.0 8.2 %collective-permute-start.11 = (bf16[264,128]{1,0:T(8,128)(2,1)S(1)}, bf16[264,128]{1,0:T(8,128)(2,1)S(1)}, u32[]{:S(2)}, u32[]{:S(2)}) collective-permute-start(bf16[264,128]{1,0:T(8,128)(2,1)S(1)} %get-tuple-element.36), channel_id=1, source_target_pairs={{0,2},{1,3},{2,0},{3,1},{4,6},{5,7},{6,4},{7,5},{8,10},{9,11},{10,... | collective-permute-start | bytes 202760 | tf_op jit(solution)/shard_map/ppermute | solution.py:184
  22.7 7.2 %collective-permute-start.12 = (bf16[264,128]{1,0:T(8,128)(2,1)S(1)}, bf16[264,128]{1,0:T(8,128)(2,1)S(1)}, u32[]{:S(2)}, u32[]{:S(2)}) collective-permute-start(bf16[264,128]{1,0:T(8,128)(2,1)S(1)} %get-tuple-element.37), channel_id=1, source_target_pairs={{0,11},{1,10},{2,9},{3,8},{4,15},{5,14},{6,13},{7,12},{8,3},{9,2},... | collective-permute-start | bytes 202760 | tf_op jit(solution)/shard_map/ppermute | solution.py:184
  26.0 6.4 %collective-permute-start.13 = (bf16[264,128]{1,0:T(8,128)(2,1)S(1)}, bf16[264,128]{1,0:T(8,128)(2,1)S(1)}, u32[]{:S(2)}, u32[]{:S(2)}) collective-permute-start(bf16[264,128]{1,0:T(8,128)(2,1)S(1)} %get-tuple-element.38), channel_id=1, source_target_pairs={{0,15},{1,14},{2,13},{3,12},{4,11},{5,10},{6,9},{7,8},{8,7},{9,6},... | collective-permute-start | bytes 202760 | tf_op jit(solution)/shard_map/ppermute | solution.py:184
  28.4 4.0 %collective-permute-start.14 = (bf16[264,128]{1,0:T(8,128)(2,1)S(1)}, bf16[264,128]{1,0:T(8,128)(2,1)S(1)}, u32[]{:S(2)}, u32[]{:S(2)}) collective-permute-start(bf16[264,128]{1,0:T(8,128)(2,1)S(1)} %get-tuple-element.39), channel_id=1, source_target_pairs={{0,1},{1,0},{2,3},{3,2},{4,5},{5,4},{6,7},{7,6},{8,9},{9,8},{10,11... | collective-permute-start | bytes 202760 | tf_op jit(solution)/shard_map/ppermute | solution.py:184

commit v14 on v12

--- a/solution.py
+++ b/solution.py
@@ -33,7 +33,8 @@
 def block_order(owners):
     half = owners // 2
     quarter = half // 2
-    far = [half + part * quarter + k for k in range(quarter) for part in range(2)]
+    near_far = [(k, k ^ 1 | quarter) for k in (*range(0, quarter, 2), *range(1, quarter, 2))]
+    far = [half + distance for both in near_far for distance in both]
     near = list(range(half - 1, -1, -1))
     order = far[:2]
     for block in far[2:]:

time: 44.1 us -> 44.6 us (1.011)
  waiting for transfers between devices: 4.02 us -> 3.09 us
  blocking collectives: 10.9 us -> 11.6 us
  starting transfers between devices: 25 us -> 25.7 us
    ppermute x15, waiting for transfers between devices: 4.02 us -> 3.09 us  [swap(): lax.ppermute(block, 'shard', [(d, d ^ k) for d in range(owners)])]
    ppermute x15, starting transfers between devices: 25 us -> 25.7 us  [swap(): lax.ppermute(block, 'shard', [(d, d ^ k) for d in range(owners)])]
    all_to_all x1, blocking collectives: 10.9 us -> 11.6 us  [shards(): returned = lax.all_to_all(best, 'shard', 0, 0, tiled=True)]
  transfers between devices with their start and end apart: 15 -> 15, of which waited for: 4 -> 1; matrix products, arithmetic and copies ran while one was open for 0% -> 0% of each run, Pallas kernels for 0% -> 0%
where the time goes in v14:
time: 44.6 us; the launch traced here: 44.4 us
  starting transfers between devices  25.7 us (58%)
  blocking collectives  11.6 us (26%)
  waiting for transfers between devices  3.09 us (7%)
  Pallas kernels  2.54 us (6%)
  local copies, waits for them, and re-layouts  0.71 us (2%)
  other arithmetic  0.7 us (2%)
    ppermute x15, starting transfers between devices, swap(): lax.ppermute(block, 'shard', [(d, d ^ k) for d in range(owners)])  25.7 us
    all_to_all x1, blocking collectives, shards(): returned = lax.all_to_all(best, 'shard', 0, 0, tiled=True)  11.6 us
    ppermute x15, waiting for transfers between devices, swap(): lax.ppermute(block, 'shard', [(d, d ^ k) for d in range(owners)])  3.09 us
    pallas_call x4, Pallas kernels, call(): pl.pallas_call(body, out_shape=shapes, compiler_params=pltpu.CompilerPara...  2.54 us
  transfers between devices with their start and end apart: 15, of which 1 were waited for; matrix products, arithmetic and copies ran while one was open for 0% of the time, Pallas kernels for 0%

profile of v14, /device:TPU:0, one launch (start us, length us, event | category | flops | bytes accessed | tf_op | source)
XLA Modules:
  0.0 44.4 jit_solution(14277319573404909393)
XLA Ops:
  0.0 0.7 %multiply_add_fusion = s32[256]{0:T(256)S(1)} fusion(s32[256]{0:T(256)} %param.5, s32[256]{0:T(256)} %param.4), kind=kLoop, calls=%fused_computation | loop fusion | flops 512 | bytes 3072 | tf_op jit(solution)/shard_map/add | solution.py:204
  0.7 0.0 copy-start
  0.7 0.3 shard_map.37
  1.0 0.7 %copy-done = bf16[256,1024]{1,0:T(8,128)(2,1)S(1)} copy-done((bf16[256,1024]{1,0:T(8,128)(2,1)S(1)}, bf16[256,1024]{1,0:T(8,128)(2,1)}, u32[]{:S(2)}) %copy-start) | copy-done | bytes 524312
  1.7 0.6 %shard_map.38 = (bf16[264,128]{1,0:T(8,128)(2,1)S(1)}, bf16[264,128]{1,0:T(8,128)(2,1)S(1)}, bf16[264,128]{1,0:T(8,128)(2,1)S(1)}, bf16[264,128]{1,0:T(8,128)(2,...) custom-call(bf16[256,1024]{1,0:T(8,128)(2,1)S(1)} %copy-done, ...), custom_call_target="tpu_custom_call" | custom-call | tf_op jit(solution)/shard_map/pallas_call | solution.py:174
  2.3 4.1 %collective-permute-start = (bf16[264,128]{1,0:T(8,128)(2,1)S(1)}, bf16[264,128]{1,0:T(8,128)(2,1)S(1)}, u32[]{:S(2)}, u32[]{:S(2)}) collective-permute-start(bf16[264,128]{1,0:T(8,128)(2,1)S(1)} %get-tuple-element.25), channel_id=1, source_target_pairs={{0,8},{1,9},{2,10},{3,11},{4,12},{5,13},{6,14},{7,15},{8,0},{9,1},... | collective-permute-start | bytes 202760 | tf_op jit(solution)/shard_map/ppermute | solution.py:185
  6.4 0.5 %collective-permute-start.1 = (bf16[264,128]{1,0:T(8,128)(2,1)S(1)}, bf16[264,128]{1,0:T(8,128)(2,1)S(1)}, u32[]{:S(2)}, u32[]{:S(2)}) collective-permute-start(bf16[264,128]{1,0:T(8,128)(2,1)S(1)} %get-tuple-element.26), channel_id=1, source_target_pairs={{0,13},{1,12},{2,15},{3,14},{4,9},{5,8},{6,11},{7,10},{8,5},{9,4},... | collective-permute-start | bytes 202760 | tf_op jit(solution)/shard_map/ppermute | solution.py:185
  7.0 1.2 %collective-permute-start.2 = (bf16[264,128]{1,0:T(8,128)(2,1)S(1)}, bf16[264,128]{1,0:T(8,128)(2,1)S(1)}, u32[]{:S(2)}, u32[]{:S(2)}) collective-permute-start(bf16[264,128]{1,0:T(8,128)(2,1)S(1)} %get-tuple-element.27), channel_id=1, source_target_pairs={{0,7},{1,6},{2,5},{3,4},{4,3},{5,2},{6,1},{7,0},{8,15},{9,14},{10,... | collective-permute-start | bytes 202760 | tf_op jit(solution)/shard_map/ppermute | solution.py:185
  8.1 3.3 %collective-permute-start.3 = (bf16[264,128]{1,0:T(8,128)(2,1)S(1)}, bf16[264,128]{1,0:T(8,128)(2,1)S(1)}, u32[]{:S(2)}, u32[]{:S(2)}) collective-permute-start(bf16[264,128]{1,0:T(8,128)(2,1)S(1)} %get-tuple-element.28), channel_id=1, source_target_pairs={{0,10},{1,11},{2,8},{3,9},{4,14},{5,15},{6,12},{7,13},{8,2},{9,3},... | collective-permute-start | bytes 202760 | tf_op jit(solution)/shard_map/ppermute | solution.py:185
  11.4 1.6 %collective-permute-start.4 = (bf16[264,128]{1,0:T(8,128)(2,1)S(1)}, bf16[264,128]{1,0:T(8,128)(2,1)S(1)}, u32[]{:S(2)}, u32[]{:S(2)}) collective-permute-start(bf16[264,128]{1,0:T(8,128)(2,1)S(1)} %get-tuple-element.29), channel_id=1, source_target_pairs={{0,6},{1,7},{2,4},{3,5},{4,2},{5,3},{6,0},{7,1},{8,14},{9,15},{10,... | collective-permute-start | bytes 202760 | tf_op jit(solution)/shard_map/ppermute | solution.py:185
  13.1 0.0 collective-permute-done.refs_0_
  13.1 2.2 %collective-permute-start.5 = (bf16[264,128]{1,0:T(8,128)(2,1)S(1)}, bf16[264,128]{1,0:T(8,128)(2,1)S(1)}, u32[]{:S(2)}, u32[]{:S(2)}) collective-permute-start(bf16[264,128]{1,0:T(8,128)(2,1)S(1)} %get-tuple-element.30), channel_id=1, source_target_pairs={{0,15},{1,14},{2,13},{3,12},{4,11},{5,10},{6,9},{7,8},{8,7},{9,6},... | collective-permute-start | bytes 202760 | tf_op jit(solution)/shard_map/ppermute | solution.py:185
  15.3 0.0 collective-permute-done.1.refs_1_
  15.3 0.0 collective-permute-start.6
  15.3 0.0 collective-permute-done.2.refs_2_
  15.3 1.9 %collective-permute-start.7 = (bf16[264,128]{1,0:T(8,128)(2,1)S(1)}, bf16[264,128]{1,0:T(8,128)(2,1)S(1)}, u32[]{:S(2)}, u32[]{:S(2)}) collective-permute-start(bf16[264,128]{1,0:T(8,128)(2,1)S(1)} %get-tuple-element.32), channel_id=1, source_target_pairs={{0,9},{1,8},{2,11},{3,10},{4,13},{5,12},{6,15},{7,14},{8,1},{9,0},... | collective-permute-start | bytes 202760 | tf_op jit(solution)/shard_map/ppermute | solution.py:185
  17.2 0.0 collective-permute-done.3.refs_3_
  17.2 1.1 %collective-permute-start.8 = (bf16[264,128]{1,0:T(8,128)(2,1)S(1)}, bf16[264,128]{1,0:T(8,128)(2,1)S(1)}, u32[]{:S(2)}, u32[]{:S(2)}) collective-permute-start(bf16[264,128]{1,0:T(8,128)(2,1)S(1)} %get-tuple-element.33), channel_id=1, source_target_pairs={{0,4},{1,5},{2,6},{3,7},{4,0},{5,1},{6,2},{7,3},{8,12},{9,13},{10,... | collective-permute-start | bytes 202760 | tf_op jit(solution)/shard_map/ppermute | solution.py:185
  18.3 0.0 collective-permute-done.4.refs_4_
  18.3 3.7 %collective-permute-start.9 = (bf16[264,128]{1,0:T(8,128)(2,1)S(1)}, bf16[264,128]{1,0:T(8,128)(2,1)S(1)}, u32[]{:S(2)}, u32[]{:S(2)}) collective-permute-start(bf16[264,128]{1,0:T(8,128)(2,1)S(1)} %get-tuple-element.34), channel_id=1, source_target_pairs={{0,12},{1,13},{2,14},{3,15},{4,8},{5,9},{6,10},{7,11},{8,4},{9,5},... | collective-permute-start | bytes 202760 | tf_op jit(solution)/shard_map/ppermute | solution.py:185
  22.0 0.0 collective-permute-done.5.refs_5_
  22.0 0.0 collective-permute-start.10
  22.0 0.0 collective-permute-done.6.refs_6_
  22.0 1.8 %collective-permute-start.11 = (bf16[264,128]{1,0:T(8,128)(2,1)S(1)}, bf16[264,128]{1,0:T(8,128)(2,1)S(1)}, u32[]{:S(2)}, u32[]{:S(2)}) collective-permute-start(bf16[264,128]{1,0:T(8,128)(2,1)S(1)} %get-tuple-element.36), channel_id=1, source_target_pairs={{0,11},{1,10},{2,9},{3,8},{4,15},{5,14},{6,13},{7,12},{8,3},{9,2},... | collective-permute-start | bytes 202760 | tf_op jit(solution)/shard_map/ppermute | solution.py:185
  23.8 0.0 collective-permute-done.7.refs_7_
  23.8 0.0 collective-permute-start.12
  23.8 0.0 collective-permute-done.8.refs_8_
  23.8 4.3 %collective-permute-start.13 = (bf16[264,128]{1,0:T(8,128)(2,1)S(1)}, bf16[264,128]{1,0:T(8,128)(2,1)S(1)}, u32[]{:S(2)}, u32[]{:S(2)}) collective-permute-start(bf16[264,128]{1,0:T(8,128)(2,1)S(1)} %get-tuple-element.38), channel_id=1, source_target_pairs={{0,14},{1,15},{2,12},{3,13},{4,10},{5,11},{6,8},{7,9},{8,6},{9,7},... | collective-permute-start | bytes 202760 | tf_op jit(solution)/shard_map/ppermute | solution.py:185
  28.1 0.0 collective-permute-done.9.refs_9_
  28.1 0.0 collective-permute-start.14
  28.1 0.0 collective-permute-done.10.refs_10_
  28.1 3.0 %collective-permute-done.11.refs_11_ = bf16[264,128]{1,0:T(8,128)(2,1)S(1)} collective-permute-done((bf16[264,128]{1,0:T(8,128)(2,1)S(1)}, bf16[264,128]{1,0:T(8,128)(2,1)S(1)}, u32[]{:S(2)}, u32[]{:S(2)}) %collective-permute-start.11) | collective-permute-done | bytes 67616 | tf_op jit(solution)/shard_map/ppermute | solution.py:185
  31.2 0.0 collective-permute-done.12.refs_12_
  31.2 0.0 collective-permute-done.13.refs_13_
  31.2 0.0 collective-permute-done.14.refs_14_
  31.2 0.9 %shard_map.39 = f32[16,1,128]{2,1,0:T(1,128)S(1)} custom-call(bf16[264,128]{1,0:T(8,128)(2,1)S(1)} %collective-permute-done.refs_0_, bf16[264,128]{1,0:T(8,128)(2,1)S(1)} %collective-permute-done.1.refs_1_, bf16[264,128]{1,0:T(8,128)(2,1)S(1)} %collective-permute-done.2.refs_2_, bf16[264,128]{1,0:T(8,128)(2,1)S(1)} %collective-permute-done.3.refs_3_, ...), custom_call_target="tpu_custom_call" | custom-call | tf_op jit(solution)/shard_map/pallas_call | solution.py:174
  32.1 11.6 %all_to_all.5.refs_0_ = f32[16,1,128]{2,1,0:T(1,128)S(1)} all-to-all(f32[16,1,128]{2,1,0:T(1,128)S(1)} %shard_map.39), channel_id=1, replica_groups=mesh['groups'=2,'shard'=16] {'shard'}, dimensions={0} | all-to-all | bytes 16384 | tf_op jit(solution)/shard_map/all_to_all | solution.py:228
  43.7 0.7 %shard_map.40 = f32[1,256]{1,0:T(1,128)} custom-call(f32[16,1,128]{2,1,0:T(1,128)S(1)} %all_to_all.5.refs_0_, s32[1,256]{1,0:T(1,128)S(1)} %get-tuple-element.23.refs_1_), custom_call_target="tpu_custom_call" | custom-call | tf_op jit(solution)/shard_map/pallas_call | solution.py:174
Async XLA Ops:
  0.7 1.0 %copy-start = (bf16[256,1024]{1,0:T(8,128)(2,1)S(1)}, bf16[256,1024]{1,0:T(8,128)(2,1)}, u32[]{:S(2)}) copy-start(bf16[256,1024]{1,0:T(8,128)(2,1)} %refs_0_.1) | copy-start | bytes 1572868
  2.3 10.7 %collective-permute-start = (bf16[264,128]{1,0:T(8,128)(2,1)S(1)}, bf16[264,128]{1,0:T(8,128)(2,1)S(1)}, u32[]{:S(2)}, u32[]{:S(2)}) collective-permute-start(bf16[264,128]{1,0:T(8,128)(2,1)S(1)} %get-tuple-element.25), channel_id=1, source_target_pairs={{0,8},{1,9},{2,10},{3,11},{4,12},{5,13},{6,14},{7,15},{8,0},{9,1},... | collective-permute-start | bytes 202760 | tf_op jit(solution)/shard_map/ppermute | solution.py:185
  6.4 8.9 %collective-permute-start.1 = (bf16[264,128]{1,0:T(8,128)(2,1)S(1)}, bf16[264,128]{1,0:T(8,128)(2,1)S(1)}, u32[]{:S(2)}, u32[]{:S(2)}) collective-permute-start(bf16[264,128]{1,0:T(8,128)(2,1)S(1)} %get-tuple-element.26), channel_id=1, source_target_pairs={{0,13},{1,12},{2,15},{3,14},{4,9},{5,8},{6,11},{7,10},{8,5},{9,4},... | collective-permute-start | bytes 202760 | tf_op jit(solution)/shard_map/ppermute | solution.py:185
  7.0 8.3 %collective-permute-start.2 = (bf16[264,128]{1,0:T(8,128)(2,1)S(1)}, bf16[264,128]{1,0:T(8,128)(2,1)S(1)}, u32[]{:S(2)}, u32[]{:S(2)}) collective-permute-start(bf16[264,128]{1,0:T(8,128)(2,1)S(1)} %get-tuple-element.27), channel_id=1, source_target_pairs={{0,7},{1,6},{2,5},{3,4},{4,3},{5,2},{6,1},{7,0},{8,15},{9,14},{10,... | collective-permute-start | bytes 202760 | tf_op jit(solution)/shard_map/ppermute | solution.py:185
  8.1 9.0 %collective-permute-start.3 = (bf16[264,128]{1,0:T(8,128)(2,1)S(1)}, bf16[264,128]{1,0:T(8,128)(2,1)S(1)}, u32[]{:S(2)}, u32[]{:S(2)}) collective-permute-start(bf16[264,128]{1,0:T(8,128)(2,1)S(1)} %get-tuple-element.28), channel_id=1, source_target_pairs={{0,10},{1,11},{2,8},{3,9},{4,14},{5,15},{6,12},{7,13},{8,2},{9,3},... | collective-permute-start | bytes 202760 | tf_op jit(solution)/shard_map/ppermute | solution.py:185
  11.4 6.8 %collective-permute-start.4 = (bf16[264,128]{1,0:T(8,128)(2,1)S(1)}, bf16[264,128]{1,0:T(8,128)(2,1)S(1)}, u32[]{:S(2)}, u32[]{:S(2)}) collective-permute-start(bf16[264,128]{1,0:T(8,128)(2,1)S(1)} %get-tuple-element.29), channel_id=1, source_target_pairs={{0,6},{1,7},{2,4},{3,5},{4,2},{5,3},{6,0},{7,1},{8,14},{9,15},{10,... | collective-permute-start | bytes 202760 | tf_op jit(solution)/shard_map/ppermute | solution.py:185
  13.1 8.9 %collective-permute-start.5 = (bf16[264,128]{1,0:T(8,128)(2,1)S(1)}, bf16[264,128]{1,0:T(8,128)(2,1)S(1)}, u32[]{:S(2)}, u32[]{:S(2)}) collective-permute-start(bf16[264,128]{1,0:T(8,128)(2,1)S(1)} %get-tuple-element.30), channel_id=1, source_target_pairs={{0,15},{1,14},{2,13},{3,12},{4,11},{5,10},{6,9},{7,8},{8,7},{9,6},... | collective-permute-start | bytes 202760 | tf_op jit(solution)/shard_map/ppermute | solution.py:185
  15.3 6.7 %collective-permute-start.6 = (bf16[264,128]{1,0:T(8,128)(2,1)S(1)}, bf16[264,128]{1,0:T(8,128)(2,1)S(1)}, u32[]{:S(2)}, u32[]{:S(2)}) collective-permute-start(bf16[264,128]{1,0:T(8,128)(2,1)S(1)} %get-tuple-element.31), channel_id=1, source_target_pairs={{0,5},{1,4},{2,7},{3,6},{4,1},{5,0},{6,3},{7,2},{8,13},{9,12},{10,... | collective-permute-start | bytes 202760 | tf_op jit(solution)/shard_map/ppermute | solution.py:185
  15.3 8.5 %collective-permute-start.7 = (bf16[264,128]{1,0:T(8,128)(2,1)S(1)}, bf16[264,128]{1,0:T(8,128)(2,1)S(1)}, u32[]{:S(2)}, u32[]{:S(2)}) collective-permute-start(bf16[264,128]{1,0:T(8,128)(2,1)S(1)} %get-tuple-element.32), channel_id=1, source_target_pairs={{0,9},{1,8},{2,11},{3,10},{4,13},{5,12},{6,15},{7,14},{8,1},{9,0},... | collective-permute-start | bytes 202760 | tf_op jit(solution)/shard_map/ppermute | solution.py:185
  17.2 6.6 %collective-permute-start.8 = (bf16[264,128]{1,0:T(8,128)(2,1)S(1)}, bf16[264,128]{1,0:T(8,128)(2,1)S(1)}, u32[]{:S(2)}, u32[]{:S(2)}) collective-permute-start(bf16[264,128]{1,0:T(8,128)(2,1)S(1)} %get-tuple-element.33), channel_id=1, source_target_pairs={{0,4},{1,5},{2,6},{3,7},{4,0},{5,1},{6,2},{7,3},{8,12},{9,13},{10,... | collective-permute-start | bytes 202760 | tf_op jit(solution)/shard_map/ppermute | solution.py:185
  18.3 9.8 %collective-permute-start.9 = (bf16[264,128]{1,0:T(8,128)(2,1)S(1)}, bf16[264,128]{1,0:T(8,128)(2,1)S(1)}, u32[]{:S(2)}, u32[]{:S(2)}) collective-permute-start(bf16[264,128]{1,0:T(8,128)(2,1)S(1)} %get-tuple-element.34), channel_id=1, source_target_pairs={{0,12},{1,13},{2,14},{3,15},{4,8},{5,9},{6,10},{7,11},{8,4},{9,5},... | collective-permute-start | bytes 202760 | tf_op jit(solution)/shard_map/ppermute | solution.py:185
  22.0 6.2 %collective-permute-start.10 = (bf16[264,128]{1,0:T(8,128)(2,1)S(1)}, bf16[264,128]{1,0:T(8,128)(2,1)S(1)}, u32[]{:S(2)}, u32[]{:S(2)}) collective-permute-start(bf16[264,128]{1,0:T(8,128)(2,1)S(1)} %get-tuple-element.35), channel_id=1, source_target_pairs={{0,3},{1,2},{2,1},{3,0},{4,7},{5,6},{6,5},{7,4},{8,11},{9,10},{10,... | collective-permute-start | bytes 202760 | tf_op jit(solution)/shard_map/ppermute | solution.py:185
  22.0 9.2 %collective-permute-start.11 = (bf16[264,128]{1,0:T(8,128)(2,1)S(1)}, bf16[264,128]{1,0:T(8,128)(2,1)S(1)}, u32[]{:S(2)}, u32[]{:S(2)}) collective-permute-start(bf16[264,128]{1,0:T(8,128)(2,1)S(1)} %get-tuple-element.36), channel_id=1, source_target_pairs={{0,11},{1,10},{2,9},{3,8},{4,15},{5,14},{6,13},{7,12},{8,3},{9,2},... | collective-permute-start | bytes 202760 | tf_op jit(solution)/shard_map/ppermute | solution.py:185
  23.8 7.4 %collective-permute-start.12 = (bf16[264,128]{1,0:T(8,128)(2,1)S(1)}, bf16[264,128]{1,0:T(8,128)(2,1)S(1)}, u32[]{:S(2)}, u32[]{:S(2)}) collective-permute-start(bf16[264,128]{1,0:T(8,128)(2,1)S(1)} %get-tuple-element.37), channel_id=1, source_target_pairs={{0,2},{1,3},{2,0},{3,1},{4,6},{5,7},{6,4},{7,5},{8,10},{9,11},{10,... | collective-permute-start | bytes 202760 | tf_op jit(solution)/shard_map/ppermute | solution.py:185
  23.8 7.4 %collective-permute-start.13 = (bf16[264,128]{1,0:T(8,128)(2,1)S(1)}, bf16[264,128]{1,0:T(8,128)(2,1)S(1)}, u32[]{:S(2)}, u32[]{:S(2)}) collective-permute-start(bf16[264,128]{1,0:T(8,128)(2,1)S(1)} %get-tuple-element.38), channel_id=1, source_target_pairs={{0,14},{1,15},{2,12},{3,13},{4,10},{5,11},{6,8},{7,9},{8,6},{9,7},... | collective-permute-start | bytes 202760 | tf_op jit(solution)/shard_map/ppermute | solution.py:185
  28.1 3.1 %collective-permute-start.14 = (bf16[264,128]{1,0:T(8,128)(2,1)S(1)}, bf16[264,128]{1,0:T(8,128)(2,1)S(1)}, u32[]{:S(2)}, u32[]{:S(2)}) collective-permute-start(bf16[264,128]{1,0:T(8,128)(2,1)S(1)} %get-tuple-element.39), channel_id=1, source_target_pairs={{0,1},{1,0},{2,3},{3,2},{4,5},{5,4},{6,7},{7,6},{8,9},{9,8},{10,11... | collective-permute-start | bytes 202760 | tf_op jit(solution)/shard_map/ppermute | solution.py:185

commit v15 on v12

--- a/solution.py
+++ b/solution.py
@@ -34,7 +34,7 @@
     half = owners // 2
     quarter = half // 2
     far = [half + part * quarter + k for k in range(quarter) for part in range(2)]
-    near = list(range(half - 1, -1, -1))
+    near = [*range(2, half), 1, 0]
     order = far[:2]
     for block in far[2:]:
         order += [near.pop(0), block]

time: 44.1 us -> 44.9 us (1.018)
  blocking collectives: 10.9 us -> 9.61 us
  starting transfers between devices: 25 us -> 26.1 us
  waiting for transfers between devices: 4.02 us -> 4.99 us
    all_to_all x1, blocking collectives: 10.9 us -> 9.61 us  [shards(): returned = lax.all_to_all(best, 'shard', 0, 0, tiled=True)]
    ppermute x15, starting transfers between devices: 25 us -> 26.1 us  [swap(): lax.ppermute(block, 'shard', [(d, d ^ k) for d in range(owners)])]
    ppermute x15, waiting for transfers between devices: 4.02 us -> 4.99 us  [swap(): lax.ppermute(block, 'shard', [(d, d ^ k) for d in range(owners)])]
where the time goes in v15:
time: 44.9 us; the launch traced here: 44.7 us
  starting transfers between devices  26.1 us (58%)
  blocking collectives  9.61 us (21%)
  waiting for transfers between devices  4.99 us (11%)
  Pallas kernels  2.54 us (6%)
  local copies, waits for them, and re-layouts  0.71 us (2%)
  other arithmetic  0.7 us (2%)
    ppermute x15, starting transfers between devices, swap(): lax.ppermute(block, 'shard', [(d, d ^ k) for d in range(owners)])  26.1 us
    all_to_all x1, blocking collectives, shards(): returned = lax.all_to_all(best, 'shard', 0, 0, tiled=True)  9.61 us
    ppermute x15, waiting for transfers between devices, swap(): lax.ppermute(block, 'shard', [(d, d ^ k) for d in range(owners)])  4.99 us
    pallas_call x4, Pallas kernels, call(): pl.pallas_call(body, out_shape=shapes, compiler_params=pltpu.CompilerPara...  2.54 us
  transfers between devices with their start and end apart: 15, of which 4 were waited for; matrix products, arithmetic and copies ran while one was open for 0% of the time, Pallas kernels for 0%

profile of v15, /device:TPU:0, one launch (start us, length us, event | category | flops | bytes accessed | tf_op | source)
XLA Modules:
  0.0 44.7 jit_solution(3220444544344522793)
XLA Ops:
  0.0 0.7 %multiply_add_fusion = s32[256]{0:T(256)S(1)} fusion(s32[256]{0:T(256)} %param.5, s32[256]{0:T(256)} %param.4), kind=kLoop, calls=%fused_computation | loop fusion | flops 512 | bytes 3072 | tf_op jit(solution)/shard_map/add | solution.py:203
  0.7 0.0 copy-start
  0.7 0.3 shard_map.37
  1.0 0.7 %copy-done = bf16[256,1024]{1,0:T(8,128)(2,1)S(1)} copy-done((bf16[256,1024]{1,0:T(8,128)(2,1)S(1)}, bf16[256,1024]{1,0:T(8,128)(2,1)}, u32[]{:S(2)}) %copy-start) | copy-done | bytes 524312
  1.7 0.6 %shard_map.38 = (bf16[264,128]{1,0:T(8,128)(2,1)S(1)}, bf16[264,128]{1,0:T(8,128)(2,1)S(1)}, bf16[264,128]{1,0:T(8,128)(2,1)S(1)}, bf16[264,128]{1,0:T(8,128)(2,...) custom-call(bf16[256,1024]{1,0:T(8,128)(2,1)S(1)} %copy-done, ...), custom_call_target="tpu_custom_call" | custom-call | tf_op jit(solution)/shard_map/pallas_call | solution.py:173
  2.3 4.1 %collective-permute-start = (bf16[264,128]{1,0:T(8,128)(2,1)S(1)}, bf16[264,128]{1,0:T(8,128)(2,1)S(1)}, u32[]{:S(2)}, u32[]{:S(2)}) collective-permute-start(bf16[264,128]{1,0:T(8,128)(2,1)S(1)} %get-tuple-element.25), channel_id=1, source_target_pairs={{0,8},{1,9},{2,10},{3,11},{4,12},{5,13},{6,14},{7,15},{8,0},{9,1},... | collective-permute-start | bytes 202760 | tf_op jit(solution)/shard_map/ppermute | solution.py:184
  6.4 1.3 %collective-permute-start.1 = (bf16[264,128]{1,0:T(8,128)(2,1)S(1)}, bf16[264,128]{1,0:T(8,128)(2,1)S(1)}, u32[]{:S(2)}, u32[]{:S(2)}) collective-permute-start(bf16[264,128]{1,0:T(8,128)(2,1)S(1)} %get-tuple-element.26), channel_id=1, source_target_pairs={{0,12},{1,13},{2,14},{3,15},{4,8},{5,9},{6,10},{7,11},{8,4},{9,5},... | collective-permute-start | bytes 202760 | tf_op jit(solution)/shard_map/ppermute | solution.py:184
  7.8 1.5 %collective-permute-start.2 = (bf16[264,128]{1,0:T(8,128)(2,1)S(1)}, bf16[264,128]{1,0:T(8,128)(2,1)S(1)}, u32[]{:S(2)}, u32[]{:S(2)}) collective-permute-start(bf16[264,128]{1,0:T(8,128)(2,1)S(1)} %get-tuple-element.27), channel_id=1, source_target_pairs={{0,2},{1,3},{2,0},{3,1},{4,6},{5,7},{6,4},{7,5},{8,10},{9,11},{10,... | collective-permute-start | bytes 202760 | tf_op jit(solution)/shard_map/ppermute | solution.py:184
  9.3 0.3 collective-permute-start.3
  9.6 1.6 %collective-permute-start.4 = (bf16[264,128]{1,0:T(8,128)(2,1)S(1)}, bf16[264,128]{1,0:T(8,128)(2,1)S(1)}, u32[]{:S(2)}, u32[]{:S(2)}) collective-permute-start(bf16[264,128]{1,0:T(8,128)(2,1)S(1)} %get-tuple-element.29), channel_id=1, source_target_pairs={{0,3},{1,2},{2,1},{3,0},{4,7},{5,6},{6,5},{7,4},{8,11},{9,10},{10,... | collective-permute-start | bytes 202760 | tf_op jit(solution)/shard_map/ppermute | solution.py:184
  11.2 0.0 collective-permute-done.refs_0_
  11.2 3.1 %collective-permute-start.5 = (bf16[264,128]{1,0:T(8,128)(2,1)S(1)}, bf16[264,128]{1,0:T(8,128)(2,1)S(1)}, u32[]{:S(2)}, u32[]{:S(2)}) collective-permute-start(bf16[264,128]{1,0:T(8,128)(2,1)S(1)} %get-tuple-element.30), channel_id=1, source_target_pairs={{0,13},{1,12},{2,15},{3,14},{4,9},{5,8},{6,11},{7,10},{8,5},{9,4},... | collective-permute-start | bytes 202760 | tf_op jit(solution)/shard_map/ppermute | solution.py:184
  14.3 0.0 collective-permute-done.1.refs_1_
  14.4 1.1 %collective-permute-start.6 = (bf16[264,128]{1,0:T(8,128)(2,1)S(1)}, bf16[264,128]{1,0:T(8,128)(2,1)S(1)}, u32[]{:S(2)}, u32[]{:S(2)}) collective-permute-start(bf16[264,128]{1,0:T(8,128)(2,1)S(1)} %get-tuple-element.31), channel_id=1, source_target_pairs={{0,4},{1,5},{2,6},{3,7},{4,0},{5,1},{6,2},{7,3},{8,12},{9,13},{10,... | collective-permute-start | bytes 202760 | tf_op jit(solution)/shard_map/ppermute | solution.py:184
  15.5 0.0 collective-permute-done.2.refs_2_
  15.5 2.9 %collective-permute-start.7 = (bf16[264,128]{1,0:T(8,128)(2,1)S(1)}, bf16[264,128]{1,0:T(8,128)(2,1)S(1)}, u32[]{:S(2)}, u32[]{:S(2)}) collective-permute-start(bf16[264,128]{1,0:T(8,128)(2,1)S(1)} %get-tuple-element.32), channel_id=1, source_target_pairs={{0,10},{1,11},{2,8},{3,9},{4,14},{5,15},{6,12},{7,13},{8,2},{9,3},... | collective-permute-start | bytes 202760 | tf_op jit(solution)/shard_map/ppermute | solution.py:184
  18.4 0.0 collective-permute-done.3.refs_3_
  18.4 0.4 collective-permute-start.8
  18.8 0.0 collective-permute-done.4.refs_4_
  18.8 2.9 %collective-permute-start.9 = (bf16[264,128]{1,0:T(8,128)(2,1)S(1)}, bf16[264,128]{1,0:T(8,128)(2,1)S(1)}, u32[]{:S(2)}, u32[]{:S(2)}) collective-permute-start(bf16[264,128]{1,0:T(8,128)(2,1)S(1)} %get-tuple-element.34), channel_id=1, source_target_pairs={{0,14},{1,15},{2,12},{3,13},{4,10},{5,11},{6,8},{7,9},{8,6},{9,7},... | collective-permute-start | bytes 202760 | tf_op jit(solution)/shard_map/ppermute | solution.py:184
  21.7 0.0 collective-permute-done.5.refs_5_
  21.7 1.7 %collective-permute-start.10 = (bf16[264,128]{1,0:T(8,128)(2,1)S(1)}, bf16[264,128]{1,0:T(8,128)(2,1)S(1)}, u32[]{:S(2)}, u32[]{:S(2)}) collective-permute-start(bf16[264,128]{1,0:T(8,128)(2,1)S(1)} %get-tuple-element.35), channel_id=1, source_target_pairs={{0,6},{1,7},{2,4},{3,5},{4,2},{5,3},{6,0},{7,1},{8,14},{9,15},{10,... | collective-permute-start | bytes 202760 | tf_op jit(solution)/shard_map/ppermute | solution.py:184
  23.4 0.0 collective-permute-done.6.refs_6_
  23.4 1.4 %collective-permute-start.11 = (bf16[264,128]{1,0:T(8,128)(2,1)S(1)}, bf16[264,128]{1,0:T(8,128)(2,1)S(1)}, u32[]{:S(2)}, u32[]{:S(2)}) collective-permute-start(bf16[264,128]{1,0:T(8,128)(2,1)S(1)} %get-tuple-element.36), channel_id=1, source_target_pairs={{0,11},{1,10},{2,9},{3,8},{4,15},{5,14},{6,13},{7,12},{8,3},{9,2},... | collective-permute-start | bytes 202760 | tf_op jit(solution)/shard_map/ppermute | solution.py:184
  24.8 0.0 collective-permute-done.7.refs_7_
  24.8 0.7 %collective-permute-start.12 = (bf16[264,128]{1,0:T(8,128)(2,1)S(1)}, bf16[264,128]{1,0:T(8,128)(2,1)S(1)}, u32[]{:S(2)}, u32[]{:S(2)}) collective-permute-start(bf16[264,128]{1,0:T(8,128)(2,1)S(1)} %get-tuple-element.37), channel_id=1, source_target_pairs={{0,7},{1,6},{2,5},{3,4},{4,3},{5,2},{6,1},{7,0},{8,15},{9,14},{10,... | collective-permute-start | bytes 202760 | tf_op jit(solution)/shard_map/ppermute | solution.py:184
  25.5 0.0 collective-permute-done.8.refs_8_
  25.5 2.5 %collective-permute-start.13 = (bf16[264,128]{1,0:T(8,128)(2,1)S(1)}, bf16[264,128]{1,0:T(8,128)(2,1)S(1)}, u32[]{:S(2)}, u32[]{:S(2)}) collective-permute-start(bf16[264,128]{1,0:T(8,128)(2,1)S(1)} %get-tuple-element.38), channel_id=1, source_target_pairs={{0,15},{1,14},{2,13},{3,12},{4,11},{5,10},{6,9},{7,8},{8,7},{9,6},... | collective-permute-start | bytes 202760 | tf_op jit(solution)/shard_map/ppermute | solution.py:184
  28.0 0.0 collective-permute-done.9.refs_9_
  28.0 0.5 %collective-permute-start.14 = (bf16[264,128]{1,0:T(8,128)(2,1)S(1)}, bf16[264,128]{1,0:T(8,128)(2,1)S(1)}, u32[]{:S(2)}, u32[]{:S(2)}) collective-permute-start(bf16[264,128]{1,0:T(8,128)(2,1)S(1)} %get-tuple-element.39), channel_id=1, source_target_pairs={{0,1},{1,0},{2,3},{3,2},{4,5},{5,4},{6,7},{7,6},{8,9},{9,8},{10,11... | collective-permute-start | bytes 202760 | tf_op jit(solution)/shard_map/ppermute | solution.py:184
  28.5 0.4 collective-permute-done.10.refs_10_
  28.9 1.8 %collective-permute-done.11.refs_11_ = bf16[264,128]{1,0:T(8,128)(2,1)S(1)} collective-permute-done((bf16[264,128]{1,0:T(8,128)(2,1)S(1)}, bf16[264,128]{1,0:T(8,128)(2,1)S(1)}, u32[]{:S(2)}, u32[]{:S(2)}) %collective-permute-start.11) | collective-permute-done | bytes 67616 | tf_op jit(solution)/shard_map/ppermute | solution.py:184
  30.7 0.1 collective-permute-done.12.refs_12_
  30.8 2.7 %collective-permute-done.13.refs_13_ = bf16[264,128]{1,0:T(8,128)(2,1)S(1)} collective-permute-done((bf16[264,128]{1,0:T(8,128)(2,1)S(1)}, bf16[264,128]{1,0:T(8,128)(2,1)S(1)}, u32[]{:S(2)}, u32[]{:S(2)}) %collective-permute-start.13) | collective-permute-done | bytes 67616 | tf_op jit(solution)/shard_map/ppermute | solution.py:184
  33.4 0.0 collective-permute-done.14.refs_14_
  33.4 0.9 %shard_map.39 = f32[16,1,128]{2,1,0:T(1,128)S(1)} custom-call(bf16[264,128]{1,0:T(8,128)(2,1)S(1)} %collective-permute-done.refs_0_, bf16[264,128]{1,0:T(8,128)(2,1)S(1)} %collective-permute-done.1.refs_1_, bf16[264,128]{1,0:T(8,128)(2,1)S(1)} %collective-permute-done.2.refs_2_, bf16[264,128]{1,0:T(8,128)(2,1)S(1)} %collective-permute-done.3.refs_3_, ...), custom_call_target="tpu_custom_call" | custom-call | tf_op jit(solution)/shard_map/pallas_call | solution.py:173
  34.3 9.6 %all_to_all.5.refs_0_ = f32[16,1,128]{2,1,0:T(1,128)S(1)} all-to-all(f32[16,1,128]{2,1,0:T(1,128)S(1)} %shard_map.39), channel_id=1, replica_groups=mesh['groups'=2,'shard'=16] {'shard'}, dimensions={0} | all-to-all | bytes 16384 | tf_op jit(solution)/shard_map/all_to_all | solution.py:227
  43.9 0.7 %shard_map.40 = f32[1,256]{1,0:T(1,128)} custom-call(f32[16,1,128]{2,1,0:T(1,128)S(1)} %all_to_all.5.refs_0_, s32[1,256]{1,0:T(1,128)S(1)} %get-tuple-element.23.refs_1_), custom_call_target="tpu_custom_call" | custom-call | tf_op jit(solution)/shard_map/pallas_call | solution.py:173
Async XLA Ops:
  0.7 1.0 %copy-start = (bf16[256,1024]{1,0:T(8,128)(2,1)S(1)}, bf16[256,1024]{1,0:T(8,128)(2,1)}, u32[]{:S(2)}) copy-start(bf16[256,1024]{1,0:T(8,128)(2,1)} %refs_0_.1) | copy-start | bytes 1572868
  2.3 8.9 %collective-permute-start = (bf16[264,128]{1,0:T(8,128)(2,1)S(1)}, bf16[264,128]{1,0:T(8,128)(2,1)S(1)}, u32[]{:S(2)}, u32[]{:S(2)}) collective-permute-start(bf16[264,128]{1,0:T(8,128)(2,1)S(1)} %get-tuple-element.25), channel_id=1, source_target_pairs={{0,8},{1,9},{2,10},{3,11},{4,12},{5,13},{6,14},{7,15},{8,0},{9,1},... | collective-permute-start | bytes 202760 | tf_op jit(solution)/shard_map/ppermute | solution.py:184
  6.4 7.9 %collective-permute-start.1 = (bf16[264,128]{1,0:T(8,128)(2,1)S(1)}, bf16[264,128]{1,0:T(8,128)(2,1)S(1)}, u32[]{:S(2)}, u32[]{:S(2)}) collective-permute-start(bf16[264,128]{1,0:T(8,128)(2,1)S(1)} %get-tuple-element.26), channel_id=1, source_target_pairs={{0,12},{1,13},{2,14},{3,15},{4,8},{5,9},{6,10},{7,11},{8,4},{9,5},... | collective-permute-start | bytes 202760 | tf_op jit(solution)/shard_map/ppermute | solution.py:184
  7.8 7.7 %collective-permute-start.2 = (bf16[264,128]{1,0:T(8,128)(2,1)S(1)}, bf16[264,128]{1,0:T(8,128)(2,1)S(1)}, u32[]{:S(2)}, u32[]{:S(2)}) collective-permute-start(bf16[264,128]{1,0:T(8,128)(2,1)S(1)} %get-tuple-element.27), channel_id=1, source_target_pairs={{0,2},{1,3},{2,0},{3,1},{4,6},{5,7},{6,4},{7,5},{8,10},{9,11},{10,... | collective-permute-start | bytes 202760 | tf_op jit(solution)/shard_map/ppermute | solution.py:184
  9.3 9.1 %collective-permute-start.3 = (bf16[264,128]{1,0:T(8,128)(2,1)S(1)}, bf16[264,128]{1,0:T(8,128)(2,1)S(1)}, u32[]{:S(2)}, u32[]{:S(2)}) collective-permute-start(bf16[264,128]{1,0:T(8,128)(2,1)S(1)} %get-tuple-element.28), channel_id=1, source_target_pairs={{0,9},{1,8},{2,11},{3,10},{4,13},{5,12},{6,15},{7,14},{8,1},{9,0},... | collective-permute-start | bytes 202760 | tf_op jit(solution)/shard_map/ppermute | solution.py:184
  9.6 9.2 %collective-permute-start.4 = (bf16[264,128]{1,0:T(8,128)(2,1)S(1)}, bf16[264,128]{1,0:T(8,128)(2,1)S(1)}, u32[]{:S(2)}, u32[]{:S(2)}) collective-permute-start(bf16[264,128]{1,0:T(8,128)(2,1)S(1)} %get-tuple-element.29), channel_id=1, source_target_pairs={{0,3},{1,2},{2,1},{3,0},{4,7},{5,6},{6,5},{7,4},{8,11},{9,10},{10,... | collective-permute-start | bytes 202760 | tf_op jit(solution)/shard_map/ppermute | solution.py:184
  11.2 10.4 %collective-permute-start.5 = (bf16[264,128]{1,0:T(8,128)(2,1)S(1)}, bf16[264,128]{1,0:T(8,128)(2,1)S(1)}, u32[]{:S(2)}, u32[]{:S(2)}) collective-permute-start(bf16[264,128]{1,0:T(8,128)(2,1)S(1)} %get-tuple-element.30), channel_id=1, source_target_pairs={{0,13},{1,12},{2,15},{3,14},{4,9},{5,8},{6,11},{7,10},{8,5},{9,4},... | collective-permute-start | bytes 202760 | tf_op jit(solution)/shard_map/ppermute | solution.py:184
  14.4 9.0 %collective-permute-start.6 = (bf16[264,128]{1,0:T(8,128)(2,1)S(1)}, bf16[264,128]{1,0:T(8,128)(2,1)S(1)}, u32[]{:S(2)}, u32[]{:S(2)}) collective-permute-start(bf16[264,128]{1,0:T(8,128)(2,1)S(1)} %get-tuple-element.31), channel_id=1, source_target_pairs={{0,4},{1,5},{2,6},{3,7},{4,0},{5,1},{6,2},{7,3},{8,12},{9,13},{10,... | collective-permute-start | bytes 202760 | tf_op jit(solution)/shard_map/ppermute | solution.py:184
  15.5 9.3 %collective-permute-start.7 = (bf16[264,128]{1,0:T(8,128)(2,1)S(1)}, bf16[264,128]{1,0:T(8,128)(2,1)S(1)}, u32[]{:S(2)}, u32[]{:S(2)}) collective-permute-start(bf16[264,128]{1,0:T(8,128)(2,1)S(1)} %get-tuple-element.32), channel_id=1, source_target_pairs={{0,10},{1,11},{2,8},{3,9},{4,14},{5,15},{6,12},{7,13},{8,2},{9,3},... | collective-permute-start | bytes 202760 | tf_op jit(solution)/shard_map/ppermute | solution.py:184
  18.4 7.1 %collective-permute-start.8 = (bf16[264,128]{1,0:T(8,128)(2,1)S(1)}, bf16[264,128]{1,0:T(8,128)(2,1)S(1)}, u32[]{:S(2)}, u32[]{:S(2)}) collective-permute-start(bf16[264,128]{1,0:T(8,128)(2,1)S(1)} %get-tuple-element.33), channel_id=1, source_target_pairs={{0,5},{1,4},{2,7},{3,6},{4,1},{5,0},{6,3},{7,2},{8,13},{9,12},{10,... | collective-permute-start | bytes 202760 | tf_op jit(solution)/shard_map/ppermute | solution.py:184
  18.8 9.2 %collective-permute-start.9 = (bf16[264,128]{1,0:T(8,128)(2,1)S(1)}, bf16[264,128]{1,0:T(8,128)(2,1)S(1)}, u32[]{:S(2)}, u32[]{:S(2)}) collective-permute-start(bf16[264,128]{1,0:T(8,128)(2,1)S(1)} %get-tuple-element.34), channel_id=1, source_target_pairs={{0,14},{1,15},{2,12},{3,13},{4,10},{5,11},{6,8},{7,9},{8,6},{9,7},... | collective-permute-start | bytes 202760 | tf_op jit(solution)/shard_map/ppermute | solution.py:184
  21.7 7.2 %collective-permute-start.10 = (bf16[264,128]{1,0:T(8,128)(2,1)S(1)}, bf16[264,128]{1,0:T(8,128)(2,1)S(1)}, u32[]{:S(2)}, u32[]{:S(2)}) collective-permute-start(bf16[264,128]{1,0:T(8,128)(2,1)S(1)} %get-tuple-element.35), channel_id=1, source_target_pairs={{0,6},{1,7},{2,4},{3,5},{4,2},{5,3},{6,0},{7,1},{8,14},{9,15},{10,... | collective-permute-start | bytes 202760 | tf_op jit(solution)/shard_map/ppermute | solution.py:184
  23.4 7.3 %collective-permute-start.11 = (bf16[264,128]{1,0:T(8,128)(2,1)S(1)}, bf16[264,128]{1,0:T(8,128)(2,1)S(1)}, u32[]{:S(2)}, u32[]{:S(2)}) collective-permute-start(bf16[264,128]{1,0:T(8,128)(2,1)S(1)} %get-tuple-element.36), channel_id=1, source_target_pairs={{0,11},{1,10},{2,9},{3,8},{4,15},{5,14},{6,13},{7,12},{8,3},{9,2},... | collective-permute-start | bytes 202760 | tf_op jit(solution)/shard_map/ppermute | solution.py:184
  24.8 6.0 %collective-permute-start.12 = (bf16[264,128]{1,0:T(8,128)(2,1)S(1)}, bf16[264,128]{1,0:T(8,128)(2,1)S(1)}, u32[]{:S(2)}, u32[]{:S(2)}) collective-permute-start(bf16[264,128]{1,0:T(8,128)(2,1)S(1)} %get-tuple-element.37), channel_id=1, source_target_pairs={{0,7},{1,6},{2,5},{3,4},{4,3},{5,2},{6,1},{7,0},{8,15},{9,14},{10,... | collective-permute-start | bytes 202760 | tf_op jit(solution)/shard_map/ppermute | solution.py:184
  25.5 8.0 %collective-permute-start.13 = (bf16[264,128]{1,0:T(8,128)(2,1)S(1)}, bf16[264,128]{1,0:T(8,128)(2,1)S(1)}, u32[]{:S(2)}, u32[]{:S(2)}) collective-permute-start(bf16[264,128]{1,0:T(8,128)(2,1)S(1)} %get-tuple-element.38), channel_id=1, source_target_pairs={{0,15},{1,14},{2,13},{3,12},{4,11},{5,10},{6,9},{7,8},{8,7},{9,6},... | collective-permute-start | bytes 202760 | tf_op jit(solution)/shard_map/ppermute | solution.py:184
  28.0 5.5 %collective-permute-start.14 = (bf16[264,128]{1,0:T(8,128)(2,1)S(1)}, bf16[264,128]{1,0:T(8,128)(2,1)S(1)}, u32[]{:S(2)}, u32[]{:S(2)}) collective-permute-start(bf16[264,128]{1,0:T(8,128)(2,1)S(1)} %get-tuple-element.39), channel_id=1, source_target_pairs={{0,1},{1,0},{2,3},{3,2},{4,5},{5,4},{6,7},{7,6},{8,9},{9,8},{10,11... | collective-permute-start | bytes 202760 | tf_op jit(solution)/shard_map/ppermute | solution.py:184
